TPU v7x, 128 devices: a whole 4x4x4 slice. The times are simulated.
128 devices in a mesh: dp: 16 (over x, y), expert: 8 (over z, core).
Axes of the slice: x: 4, y: 4, z: 4, core: 2. Of those that a mesh axis runs over, the one named last changes fastest.
Arguments:
- tokens: bfloat16 [16384, 1536], P(('dp', 'expert')), may hold values from -6 to 6
- norm_attn: float32 [1536], replicated, may hold values from 0.5 to 1.5
- query_weight: bfloat16 [1536, 1536], P('dp'), may hold values from -0.15625 to 0.15625
- key_weight: bfloat16 [1536, 512], P('dp'), may hold values from -0.15625 to 0.15625
- value_weight: bfloat16 [1536, 512], P('dp'), may hold values from -0.15625 to 0.15625
- out_weight: bfloat16 [1536, 1536], P('dp'), may hold values from -0.625 to 0.625
- norm_moe: float32 [1536], replicated, may hold values from 0.5 to 1.5
- router_weight: bfloat16 [1536, 24], P('dp'), may hold values from -0.078125 to 0.078125
- gate_weight: bfloat16 [24, 1536, 512], P('expert'), may hold values from -0.15625 to 0.15625
- up_weight: bfloat16 [24, 1536, 512], P('expert'), may hold values from -0.15625 to 0.15625
- down_weight: bfloat16 [24, 512, 1536], P('expert'), may hold values from -2 to 2
- routes: int32 [16384, 8], P(('dp', 'expert')), may hold values from 0 to 23, all different within a row; in each aligned block of 128 rows (0 to 127, 128 to 255, ...) at most 56 rows name the same one
- seq_lengths: int32 [16, 3], P('dp'), may hold values from 1 to 1022, as said below
- out_grad: bfloat16 [16384, 1536], P(('dp', 'expert')), may hold values from -6 to 6
Outputs:
- layer_out: bfloat16 [16384, 1536], P(('dp', 'expert'))
- input_grad: bfloat16 [16384, 1536], P(('dp', 'expert'))
- norm_attn_grad: float32 [1536], replicated
- query_grad: float32 [1536, 1536], P('dp')
- key_grad: float32 [1536, 512], P('dp')
- value_grad: float32 [1536, 512], P('dp')
- out_weight_grad: float32 [1536, 1536], P('dp')
- norm_moe_grad: float32 [1536], replicated
- router_grad: float32 [1536, 24], P('dp')
- gate_grad: float32 [24, 1536, 512], P('expert')
- up_grad: float32 [24, 1536, 512], P('expert')
- down_grad: float32 [24, 512, 1536], P('expert')
Inputs may be any that keep to these rules, and one draw needn't show every extreme that they name: `routes`: in each aligned block of 128 rows (the rows of one device) the 8 experts of a row differ, and no expert is named by more than 56 rows. `seq_lengths`: each row sums to 1024; in each row one sequence, at a place drawn from the seed, starts among the group's first 128 tokens and ends among its last 128; in some row it has 1022 tokens.
All inputs are finite; a program needn't handle non-finite values.
Results may differ from a plain program's by a relative error of at most 0.025.
Values may be sent and summed in bfloat16 or wider, within the bound.
No kernel may reach another device: no remote copies, remote signals or barrier semaphores. Data moves between devices by JAX's collectives and lax.ppermute only.
A program may use at most 192 MiB of HBM per device.

v0:
```python
import math

import jax
import jax.numpy as jnp
from jax import lax
from jax.sharding import PartitionSpec as P

QH = 24
KVH = 8
HD = 64
TOP = 8
EXP_DEV = 3


EPS = 1e-06
THETA = 10000.0
HIGHEST_PREC = lax.Precision.HIGHEST


def rotate(values, cos_table, sin_table):
    half = values.shape[-1] // 2
    first_half = values[..., :half]
    second_half = values[..., half:]
    return jnp.concatenate(
        [
            first_half * cos_table - second_half * sin_table,
            second_half * cos_table + first_half * sin_table,
        ],
        axis=-1,
    )


def sequence_table(seq_row, count):
    ends = jnp.cumsum(seq_row)
    starts = ends - seq_row
    where_all = jnp.arange(count, dtype=jnp.int32)
    seg_ids = jnp.sum((where_all[:, None] >= ends[None, :]).astype(jnp.int32), axis=1)
    seq_index = jnp.arange(seq_row.shape[0], dtype=jnp.int32)
    first_of = jnp.sum(
        jnp.where(seg_ids[:, None] == seq_index[None, :], starts[None, :], 0), axis=1
    )
    return (seg_ids, where_all - first_of)


def angle_tables(positions, head_size):
    steps_f = jnp.arange(head_size // 2, dtype=jnp.float32)
    freq = jnp.exp(steps_f * (-2.0 * math.log(THETA) / head_size))
    angles = positions.astype(jnp.float32)[:, None] * freq[None, :]
    return (jnp.cos(angles)[:, None, :], jnp.sin(angles)[:, None, :])


def body(
    tokens,
    norm_attn,
    query_weight,
    key_weight,
    value_weight,
    out_weight,
    norm_moe,
    router_weight,
    gate_weight,
    up_weight,
    down_weight,
    routes,
    seq_lengths,
    out_grad,
):
    f32 = jnp.float32
    bf16 = jnp.bfloat16
    tok_rows = tokens.shape[0]
    width = tokens.shape[1]
    owner_count = lax.axis_size("expert")
    own_rank = lax.axis_index("expert")
    experts = EXP_DEV * owner_count
    slot_cap = min(tok_rows, tok_rows * TOP * 4 // (experts * 3))
    group_rows = tok_rows * owner_count
    head_ratio = QH // KVH
    score_scale = 1.0 / math.sqrt(HD)
    full_q, full_k, full_v, full_o, full_r = (
        lax.all_gather(query_weight, "dp", axis=0, tiled=True),
        lax.all_gather(key_weight, "dp", axis=0, tiled=True),
        lax.all_gather(value_weight, "dp", axis=0, tiled=True),
        lax.all_gather(out_weight, "dp", axis=0, tiled=True),
        lax.all_gather(router_weight, "dp", axis=0, tiled=True),
    )
    seg_all, place_all = sequence_table(seq_lengths[0], group_rows)
    own_start = own_rank * tok_rows
    own_index = own_start + jnp.arange(tok_rows, dtype=jnp.int32)
    seg_own = lax.dynamic_slice_in_dim(seg_all, own_start, tok_rows)
    place_own = lax.dynamic_slice_in_dim(place_all, own_start, tok_rows)
    allowed = (seg_own[:, None] == seg_all[None, :]) & (
        jnp.arange(group_rows, dtype=jnp.int32)[None, :] <= own_index[:, None]
    )
    cos_own, sin_own = angle_tables(place_own, HD)
    x_val = tokens.astype(f32)
    scale_one = lax.rsqrt(jnp.mean(x_val * x_val, axis=-1, keepdims=True) + EPS)
    unit_one = x_val * scale_one
    normed_one = (unit_one * norm_attn).astype(bf16)
    query_raw = jnp.dot(normed_one, full_q, preferred_element_type=f32)
    key_raw = jnp.dot(normed_one, full_k, preferred_element_type=f32)
    value_b = jnp.dot(normed_one, full_v, preferred_element_type=f32).astype(bf16)
    query_b = rotate(query_raw.reshape(tok_rows, QH, HD), cos_own, sin_own).astype(bf16)
    key_b = (
        rotate(key_raw.reshape(tok_rows, KVH, HD), cos_own, sin_own)
        .astype(bf16)
        .reshape(tok_rows, KVH * HD)
    )
    key_all, value_all = (
        lax.all_gather(key_b, "expert", axis=0, tiled=True),
        lax.all_gather(value_b, "expert", axis=0, tiled=True),
    )
    q_heads = jnp.moveaxis(query_b.reshape(tok_rows, KVH, head_ratio, HD), 1, 0)

    def attend(head_block):
        q_h, k_h, v_h = head_block
        scores = jnp.einsum("qrd,kd->rqk", q_h, k_h, preferred_element_type=f32) * score_scale
        scores = jnp.where(allowed[None], scores, -1e30)
        row_top = jnp.max(scores, axis=-1, keepdims=True)
        exp_terms = jnp.exp(scores - row_top)
        exp_total = jnp.sum(exp_terms, axis=-1, keepdims=True)
        prob_b = (exp_terms / exp_total).astype(bf16)
        mixed_h = jnp.einsum("rqk,kd->qrd", prob_b, v_h, preferred_element_type=f32)
        return (mixed_h, (row_top + jnp.log(exp_total))[..., 0])

    k_heads = jnp.moveaxis(key_all.reshape(group_rows, KVH, HD), 1, 0)
    v_heads = jnp.moveaxis(value_all.reshape(group_rows, KVH, HD), 1, 0)
    mixed, log_totals = lax.map(attend, (q_heads, k_heads, v_heads))
    attn_b = jnp.moveaxis(mixed, 0, 1).reshape(tok_rows, QH * HD).astype(bf16)
    hidden = x_val + jnp.dot(attn_b, full_o, preferred_element_type=f32)
    scale_two = lax.rsqrt(jnp.mean(hidden * hidden, axis=-1, keepdims=True) + EPS)
    unit_two = hidden * scale_two
    normed_two = (unit_two * norm_moe).astype(bf16)
    logits = jnp.dot(normed_two, full_r, preferred_element_type=f32)
    logit_top = jnp.max(logits, axis=-1, keepdims=True)
    logit_exp = jnp.exp(logits - logit_top)
    router_prob = logit_exp / jnp.sum(logit_exp, axis=-1, keepdims=True)
    picks = routes[:, :, None] == jnp.arange(experts, dtype=jnp.int32)[None, None, :]
    gate_vals = jnp.sum(jnp.where(picks, router_prob[:, None, :], 0.0), axis=-1)
    flat_expert = routes.reshape(-1)
    one_hot = (flat_expert[:, None] == jnp.arange(experts, dtype=jnp.int32)[None, :]).astype(
        jnp.int32
    )
    slot_ranks = jnp.sum(jnp.cumsum(one_hot, axis=0) * one_hot, axis=1) - 1
    slot_place = flat_expert * slot_cap + slot_ranks
    slot_count = tok_rows * TOP
    source_slot = (
        jnp.full((experts * slot_cap,), slot_count, jnp.int32)
        .at[slot_place]
        .set(jnp.arange(slot_count, dtype=jnp.int32))
    )
    source_token = source_slot // TOP
    padded_rows = jnp.concatenate([normed_two, jnp.zeros((1, width), bf16)], axis=0)
    send_rows = padded_rows[source_token].reshape(owner_count, EXP_DEV, slot_cap, width)
    arrived = lax.all_to_all(send_rows, "expert", split_axis=0, concat_axis=0, tiled=True)
    gate_in = jnp.einsum("secd,edf->secf", arrived, gate_weight, preferred_element_type=f32)
    up_in = jnp.einsum("secd,edf->secf", arrived, up_weight, preferred_element_type=f32)
    sig_gate = jax.nn.sigmoid(gate_in)
    silu_val = gate_in * sig_gate
    inner_act = (silu_val * up_in).astype(bf16)
    expert_out = jnp.einsum(
        "secf,efd->secd", inner_act, down_weight, preferred_element_type=f32
    ).astype(bf16)
    returned = lax.all_to_all(
        expert_out, "expert", split_axis=0, concat_axis=0, tiled=True
    ).reshape(experts * slot_cap, width)
    per_slot = returned[slot_place].reshape(tok_rows, TOP, width)
    mixture = jnp.sum(gate_vals[:, :, None] * per_slot, axis=1)
    layer_out = (hidden + mixture).astype(bf16)
    grad_y = out_grad.astype(f32)
    gate_vals_grad = jnp.sum(grad_y[:, None, :] * per_slot, axis=-1)
    slot_grads = (
        (gate_vals[:, :, None] * grad_y[:, None, :]).astype(bf16).reshape(slot_count, width)
    )
    padded_grads = jnp.concatenate([slot_grads, jnp.zeros((1, width), bf16)], axis=0)
    send_grads = padded_grads[source_slot].reshape(owner_count, EXP_DEV, slot_cap, width)
    grads_in = lax.all_to_all(send_grads, "expert", split_axis=0, concat_axis=0, tiled=True)
    inner_grad = jnp.einsum("secd,efd->secf", grads_in, down_weight, preferred_element_type=f32)
    down_part = jnp.einsum("secf,secd->efd", inner_act, grads_in, preferred_element_type=f32)
    gate_in_grad = (inner_grad * up_in * sig_gate * (1.0 + gate_in * (1.0 - sig_gate))).astype(bf16)
    up_in_grad = (inner_grad * silu_val).astype(bf16)
    gate_part = jnp.einsum("secd,secf->edf", arrived, gate_in_grad, preferred_element_type=f32)
    up_part = jnp.einsum("secd,secf->edf", arrived, up_in_grad, preferred_element_type=f32)
    row_grads = (
        jnp.einsum("secf,edf->secd", gate_in_grad, gate_weight, preferred_element_type=f32)
        + jnp.einsum("secf,edf->secd", up_in_grad, up_weight, preferred_element_type=f32)
    ).astype(bf16)
    row_back = lax.all_to_all(row_grads, "expert", split_axis=0, concat_axis=0, tiled=True).reshape(
        experts * slot_cap, width
    )
    normed_two_grad = jnp.sum(
        row_back[slot_place].reshape(tok_rows, TOP, width).astype(f32), axis=1
    )
    prob_grad_r = jnp.sum(jnp.where(picks, gate_vals_grad[:, :, None], 0.0), axis=1)
    logit_grad = router_prob * (
        prob_grad_r - jnp.sum(prob_grad_r * router_prob, axis=-1, keepdims=True)
    )
    router_part = jnp.dot(normed_two.T.astype(f32), logit_grad, precision=HIGHEST_PREC)
    normed_two_grad = normed_two_grad + jnp.dot(
        logit_grad, full_r.astype(f32).T, precision=HIGHEST_PREC
    )
    unit_two_grad = normed_two_grad * norm_moe
    moe_gain_part = jnp.sum(normed_two_grad * unit_two, axis=0)
    hidden_grad = grad_y + scale_two * (
        unit_two_grad - unit_two * jnp.mean(unit_two_grad * unit_two, axis=-1, keepdims=True)
    )
    branch_grad = hidden_grad.astype(bf16)
    out_part = jnp.dot(attn_b.T, branch_grad, preferred_element_type=f32)
    mix_grad = jnp.dot(branch_grad, full_o.T, preferred_element_type=f32).astype(bf16)
    grad_heads = jnp.moveaxis(mix_grad.reshape(tok_rows, KVH, head_ratio, HD), 1, 0)

    def attend_back(head_block):
        q_h, k_h, v_h, log_h, g_h = head_block
        scores = jnp.einsum("qrd,kd->rqk", q_h, k_h, preferred_element_type=f32) * score_scale
        scores = jnp.where(allowed[None], scores, -1e30)
        prob_full = jnp.exp(scores - log_h[..., None])
        prob_b = prob_full.astype(bf16)
        value_h_grad = jnp.einsum("rqk,qrd->kd", prob_b, g_h, preferred_element_type=f32)
        prob_grad = jnp.einsum("qrd,kd->rqk", g_h, v_h, preferred_element_type=f32)
        score_grad = (
            prob_full * (prob_grad - jnp.sum(prob_grad * prob_full, axis=-1, keepdims=True))
        ).astype(bf16)
        query_h_grad = (
            jnp.einsum("rqk,kd->qrd", score_grad, k_h, preferred_element_type=f32) * score_scale
        )
        key_h_grad = (
            jnp.einsum("rqk,qrd->kd", score_grad, q_h, preferred_element_type=f32) * score_scale
        )
        return (query_h_grad, key_h_grad, value_h_grad)

    query_grads, key_grads, value_grads = lax.map(
        attend_back, (q_heads, k_heads, v_heads, log_totals, grad_heads)
    )
    key_mine, value_mine = (
        lax.psum_scatter(
            key_grads.astype(jnp.bfloat16), "expert", scatter_dimension=1, tiled=True
        ).astype(jnp.float32),
        lax.psum_scatter(
            value_grads.astype(jnp.bfloat16), "expert", scatter_dimension=1, tiled=True
        ).astype(jnp.float32),
    )
    query_raw_grad = (
        rotate(jnp.moveaxis(query_grads, 0, 1).reshape(tok_rows, QH, HD), cos_own, -sin_own)
        .astype(bf16)
        .reshape(tok_rows, QH * HD)
    )
    key_raw_grad = (
        rotate(jnp.moveaxis(key_mine, 0, 1), cos_own, -sin_own)
        .astype(bf16)
        .reshape(tok_rows, KVH * HD)
    )
    value_raw_grad = jnp.moveaxis(value_mine, 0, 1).reshape(tok_rows, KVH * HD).astype(bf16)
    query_part = jnp.dot(normed_one.T, query_raw_grad, preferred_element_type=f32)
    key_part = jnp.dot(normed_one.T, key_raw_grad, preferred_element_type=f32)
    value_part = jnp.dot(normed_one.T, value_raw_grad, preferred_element_type=f32)
    normed_one_grad = (
        jnp.dot(query_raw_grad, full_q.T, preferred_element_type=f32)
        + jnp.dot(key_raw_grad, full_k.T, preferred_element_type=f32)
        + jnp.dot(value_raw_grad, full_v.T, preferred_element_type=f32)
    )
    unit_one_grad = normed_one_grad * norm_attn
    attn_gain_part = jnp.sum(normed_one_grad * unit_one, axis=0)
    input_grad = hidden_grad + scale_one * (
        unit_one_grad - unit_one * jnp.mean(unit_one_grad * unit_one, axis=-1, keepdims=True)
    )
    query_shard, key_shard, value_shard, out_shard, router_shard = (
        lax.psum_scatter(
            query_part.astype(jnp.bfloat16), "dp", scatter_dimension=0, tiled=True
        ).astype(jnp.float32),
        lax.psum_scatter(
            key_part.astype(jnp.bfloat16), "dp", scatter_dimension=0, tiled=True
        ).astype(jnp.float32),
        lax.psum_scatter(
            value_part.astype(jnp.bfloat16), "dp", scatter_dimension=0, tiled=True
        ).astype(jnp.float32),
        lax.psum_scatter(
            out_part.astype(jnp.bfloat16), "dp", scatter_dimension=0, tiled=True
        ).astype(jnp.float32),
        lax.psum_scatter(
            router_part.astype(jnp.bfloat16), "dp", scatter_dimension=0, tiled=True
        ).astype(jnp.float32),
    )
    down_total, gate_total, up_total, gain_attn_dp, gain_moe_dp = (
        lax.psum(down_part.astype(jnp.bfloat16), "dp").astype(jnp.float32),
        lax.psum(gate_part.astype(jnp.bfloat16), "dp").astype(jnp.float32),
        lax.psum(up_part.astype(jnp.bfloat16), "dp").astype(jnp.float32),
        lax.psum(attn_gain_part.astype(jnp.bfloat16), "dp").astype(jnp.float32),
        lax.psum(moe_gain_part.astype(jnp.bfloat16), "dp").astype(jnp.float32),
    )
    query_total, key_total, value_total, out_total, router_total, gain_attn, gain_moe = (
        lax.psum(query_shard.astype(jnp.bfloat16), "expert").astype(jnp.float32),
        lax.psum(key_shard.astype(jnp.bfloat16), "expert").astype(jnp.float32),
        lax.psum(value_shard.astype(jnp.bfloat16), "expert").astype(jnp.float32),
        lax.psum(out_shard.astype(jnp.bfloat16), "expert").astype(jnp.float32),
        lax.psum(router_shard.astype(jnp.bfloat16), "expert").astype(jnp.float32),
        lax.psum(gain_attn_dp.astype(jnp.bfloat16), "expert").astype(jnp.float32),
        lax.psum(gain_moe_dp.astype(jnp.bfloat16), "expert").astype(jnp.float32),
    )
    return (
        layer_out,
        input_grad.astype(bf16),
        gain_attn,
        query_total,
        key_total,
        value_total,
        out_total,
        gain_moe,
        router_total,
        gate_total,
        up_total,
        down_total,
    )


def solution(mesh):
    placed = (
        P(("dp", "expert"), None),
        P(),
        P("dp", None),
        P("dp", None),
        P("dp", None),
        P("dp", None),
        P(),
        P("dp", None),
        P("expert", None, None),
        P("expert", None, None),
        P("expert", None, None),
        P(("dp", "expert"), None),
        P("dp", None),
        P(("dp", "expert"), None),
    )
    return jax.shard_map(
        body,
        mesh=mesh,
        in_specs=placed,
        out_specs=(
            P(("dp", "expert"), None),
            P(("dp", "expert"), None),
            P(),
            P("dp", None),
            P("dp", None),
            P("dp", None),
            P("dp", None),
            P(),
            P("dp", None),
            P("expert", None, None),
            P("expert", None, None),
            P("expert", None, None),
        ),
        check_vma=False,
    )
```

profile of v0, /device:TPU:1, one launch (start us, length us, event | category | flops | bytes accessed | tf_op | source)
XLA Modules:
  0.0 1342.0 jit_solution(3703439757215106419)
XLA Ops:
  9.9 46.4 %all-gather.8.cloned.1.call-done = bf16[1536,512]{1,0:T(8,128)(2,1)} async-done(((bf16[96,512]{1,0:T(8,128)(2,1)}), bf16[1536,512]{1,0:T(8,128)(2,1)}) %all-gather.8.cloned.1.call-update) | async-done | bytes 1572880 | tf_op jit(solution)/shard_map/all_gather | solution.py:82
  60.8 40.9 %all-gather.12.cloned.1.call-done = bf16[1536,512]{1,0:T(8,128)(2,1)} async-done(((bf16[96,512]{1,0:T(8,128)(2,1)}), bf16[1536,512]{1,0:T(8,128)(2,1)}) %all-gather.12.cloned.1.call-update) | async-done | bytes 1572880 | tf_op jit(solution)/shard_map/all_gather | solution.py:81
  117.6 10.9 all-gather.10.cloned.1.call-done
  129.9 53.9 %all-gather.16.cloned.1.call-done = bf16[1536,1536]{1,0:T(8,128)(2,1)} async-done(((bf16[96,1536]{1,0:T(8,128)(2,1)}), bf16[1536,1536]{1,0:T(8,128)(2,1)}) %all-gather.16.cloned.1.call-update) | async-done | bytes 4718608 | tf_op jit(solution)/shard_map/all_gather | solution.py:80
  188.3 21.3 %all-gather.14.cloned.1.call-done = bf16[1024,512]{0,1:T(8,128)(2,1)} async-done(((bf16[128,512]{0,1:T(8,128)(2,1)}), bf16[1024,512]{0,1:T(8,128)(2,1)}) %all-gather.14.cloned.1.call-update) | async-done | bytes 1048592 | tf_op jit(solution)/shard_map/all_gather | solution.py:109
  209.7 22.1 %while.30 = (s32[]{:T(128)}, bf16[8,128,3,64]{1,3,2,0:T(8,128)(2,1)S(1)}, f32[8,3,128]{2,1,0:T(4,128)}, bf16[8,1024,64]{1,2,0:T(8,128)(2,1)S(1)}, bf16[8,1024,64...) while((s32[]{:T(128)}, ...), condition=%wide.region_7.8_spmd.clone.clone, body=%wide.region_4.7_spmd.clone.sunk.clone | while | flops 104201856 | bytes 5411433 | solution.py:127
  231.8 34.2 %all-gather.18.cloned.1.call-done = bf16[1536,1536]{1,0:T(8,128)(2,1)} async-done(((bf16[96,1536]{1,0:T(8,128)(2,1)}), bf16[1536,1536]{1,0:T(8,128)(2,1)}) %all-gather.18.cloned.1.call-update) | async-done | bytes 4718608 | tf_op jit(solution)/shard_map/all_gather | solution.py:83
  281.8 19.2 %all-gather = bf16[16,96,24]{1,2,0:T(8,128)(2,1)S(1)} all-gather(bf16[1,96,24]{1,2,0:T(8,128)(2,1)S(1)} %bitcast.368), channel_id=1, replica_groups=mesh['dp'=16,'expert'=8] {'dp'}, dimensions={0}, use_global_device_ids=true | all-gather | bytes 78336 | tf_op jit(solution)/shard_map/all_gather | solution.py:84
  309.4 20.5 %all-to-all-done = bf16[8,3,56,1536]{3,2,1,0:T(8,128)(2,1)} async-done(((bf16[8,3,56,1536]{3,2,1,0:T(8,128)(2,1)}), bf16[8,3,56,1536]{3,2,1,0:T(8,128)(2,1)}, u32[]{:S(2)}, u32[]{:S(2)}) %all-to-all-start) | async-done | bytes 4128800 | tf_op jit(solution)/shard_map/all_to_all | solution.py:154
  349.5 34.6 %all-to-all-done.2 = bf16[8,3,56,1536]{3,2,1,0:T(8,128)(2,1)} async-done(((bf16[8,3,56,1536]{3,2,1,0:T(8,128)(2,1)}), bf16[8,3,56,1536]{3,2,1,0:T(8,128)(2,1)}, u32[]{:S(2)}, u32[]{:S(2)}) %all-to-all-start.2) | async-done | bytes 4128800 | tf_op jit(solution)/shard_map/all_to_all | solution.py:176
  417.9 41.3 %all-to-all-done.3 = bf16[8,3,56,1536]{3,2,1,0:T(8,128)(2,1)} async-done(((bf16[8,3,56,1536]{3,2,1,0:T(8,128)(2,1)}), bf16[8,3,56,1536]{3,2,1,0:T(8,128)(2,1)}, u32[]{:S(2)}, u32[]{:S(2)}) %all-to-all-start.3) | async-done | bytes 4128800 | tf_op jit(solution)/shard_map/all_to_all | solution.py:187
  477.0 35.7 %all-to-all-done.1 = bf16[8,3,56,1536]{3,2,1,0:T(8,128)(2,1)} async-done(((bf16[8,3,56,1536]{3,2,1,0:T(8,128)(2,1)}), bf16[8,3,56,1536]{3,2,1,0:T(8,128)(2,1)}, u32[]{:S(2)}, u32[]{:S(2)}) %all-to-all-start.1) | async-done | bytes 4128800 | tf_op jit(solution)/shard_map/all_to_all | solution.py:163
  512.7 10.0 gather_fusion.1
  537.1 58.3 %while.31 = (s32[]{:T(128)}, f32[8,128,3,64]{1,3,2,0:T(8,128)S(1)}, bf16[8,1024,64]{1,2,0:T(8,128)(2,1)S(1)}, bf16[8,1024,64]{1,2,0:T(8,128)(2,1)}, bf16[8,1024,...) while((s32[]{:T(128)}, f32[8,128,3,64]{1,3,2,0:T(8,128)S(1)}, ...), condition=%wide.region_24.25_spmd.clone.clone, body=%wide.region_22.24_spmd.clone.sunk.clone | while | flops 255680128 | bytes 13289089 | solution.py:230
  609.0 20.2 %reduce-scatter.22.cloned.1.call-done = bf16[128,512]{1,0:T(8,128)(2,1)} async-done(((bf16[1024,512]{1,0:T(8,128)(2,1)}), bf16[128,512]{1,0:T(8,128)(2,1)}) %reduce-scatter.22.cloned.1.call-update) | async-done | bytes 131088
  632.5 29.7 %reduce-scatter.24.cloned.1.call-done = bf16[128,512]{1,0:T(8,128)(2,1)} async-done(((bf16[1024,512]{1,0:T(8,128)(2,1)}), bf16[128,512]{1,0:T(8,128)(2,1)}) %reduce-scatter.24.cloned.1.call-update) | async-done | bytes 131088
  691.3 47.7 %reduce-scatter.16.cloned.1.call-done = bf16[96,512]{1,0:T(8,128)(2,1)} async-done(((bf16[1536,512]{1,0:T(8,128)(2,1)}), bf16[96,512]{1,0:T(8,128)(2,1)}) %reduce-scatter.16.cloned.1.call-update) | async-done | bytes 98320 | tf_op jit(solution)/shard_map/reduce_scatter | solution.py:269
  739.1 75.9 %reduce-scatter.18.cloned.1.call-done = bf16[96,512]{1,0:T(8,128)(2,1)} async-done(((bf16[1536,512]{1,0:T(8,128)(2,1)}), bf16[96,512]{1,0:T(8,128)(2,1)}) %reduce-scatter.18.cloned.1.call-update) | async-done | bytes 98320 | tf_op jit(solution)/shard_map/reduce_scatter | solution.py:272
  815.0 81.6 %reduce-scatter.14.cloned.1.call-done = bf16[96,1536]{1,0:T(8,128)(2,1)} async-done(((bf16[1536,1536]{1,0:T(8,128)(2,1)}), bf16[96,1536]{1,0:T(8,128)(2,1)}) %reduce-scatter.14.cloned.1.call-update) | async-done | bytes 294928 | tf_op jit(solution)/shard_map/reduce_scatter | solution.py:266
  896.6 81.5 %reduce-scatter.20.cloned.1.call-done = bf16[96,1536]{1,0:T(8,128)(2,1)} async-done(((bf16[1536,1536]{1,0:T(8,128)(2,1)}), bf16[96,1536]{1,0:T(8,128)(2,1)}) %reduce-scatter.20.cloned.1.call-update) | async-done | bytes 294928 | tf_op jit(solution)/shard_map/reduce_scatter | solution.py:275
  989.9 63.4 %reduce-scatter.26.cloned.1.call-done = bf16[96,24]{1,0:T(8,128)(2,1)} async-done(((bf16[1536,24]{1,0:T(8,128)(2,1)}), bf16[96,24]{1,0:T(8,128)(2,1)}) %reduce-scatter.26.cloned.1.call-update) | async-done | bytes 4624
  1056.9 31.4 %all-reduce.2 = (bf16[1536]{0:T(1024)(128)(2,1)S(1)}, bf16[1536]{0:T(1024)(128)(2,1)S(1)}) all-reduce(bf16[1536]{0:T(1024)(128)(2,1)S(1)} %get-tuple-element.165, bf16[1536]{0:T(1024)(128)(2,1)S(1)} %get-tuple-element.163), channel_id=1, replica_groups=mesh['dp'=16,'expert'=8] {'dp'}, use_global_device_ids=true, to_apply=%region_29.30 | all-reduce | flops 3072 | bytes 12288 | tf_op jit(solution)/shard_map/psum | solution.py:286
  1088.3 29.6 %all-reduce.4 = (bf16[1536]{0:T(1024)(128)(2,1)S(1)}, bf16[1536]{0:T(1024)(128)(2,1)S(1)}, bf16[96,24]{0,1:T(8,128)(2,1)S(1)}) all-reduce(bf16[1536]{0:T(1024)(128)(2,1)S(1)} %get-tuple-element.209, bf16[1536]{0:T(1024)(128)(2,1)S(1)} %get-tuple-element.210, ...), channel_id=1, replica_groups=mesh['dp'=16,'expert'=8] {'expert'}, use_global_device_ids=true, to_apply=%region_30.31 | all-reduce | flops 5376 | bytes 21504 | tf_op jit(solution)/shard_map/psum | solution.py:295
  1127.6 189.6 %all-reduce.9.cloned.1.call-done = (bf16[3,1536,512]{2,1,0:T(8,128)(2,1)}, bf16[3,1536,512]{2,1,0:T(8,128)(2,1)}, bf16[3,512,1536]{2,1,0:T(8,128)(2,1)}) async-done(((bf16[3,1536,512]{2,1,0:T(8,128)(2,1)}, bf16[3,1536,512]{2,1,0:T(8,128)(2,1)}, bf16[3,512,1536]{2,1,0:T(8,128)(2,1)}), (bf16[3,1536,512]{2,1,0:T(8,128)(2,1)}, bf16[3,1536,512]{2,1,0:T(8,128)(2,1)}, ...) | async-done | bytes 14155792 | tf_op jit(solution)/shard_map/psum | solution.py:284
  (382 shorter events, 306.5 us)
Async XLA Ops:
  7.2 94.6 %copy-start = (bf16[128,1536]{1,0:T(8,128)(2,1)S(1)}, bf16[128,1536]{1,0:T(8,128)(2,1)}, u32[]{:S(2)}) copy-start(bf16[128,1536]{1,0:T(8,128)(2,1)} %param.18) | copy-start | bytes 1179652
  7.2 49.1 %all-gather.8.cloned.1.call-start = ((), (), s32[]{:S(2)}) async-start(), calls=%async_computation.11 | async-start | bytes 1671168 | tf_op jit(solution)/shard_map/all_gather | solution.py:82
  7.9 93.8 %all-gather.12.cloned.1.call-start = ((), (), s32[]{:S(2)}) async-start(), calls=%async_computation.13 | async-start | bytes 1671168 | tf_op jit(solution)/shard_map/all_gather | solution.py:81
  8.7 119.7 %all-gather.10.cloned.1.call-start = ((), (), s32[]{:S(2)}) async-start(), calls=%async_computation.12 | async-start | bytes 1179648 | tf_op jit(solution)/shard_map/all_gather | solution.py:110
  9.9 173.9 %copy-start.45 = (f32[128]{0:T(128)}, f32[128]{0:T(128)S(1)}, u32[]{:S(2)}) copy-start(f32[128]{0:T(128)S(1)} %add_rsqrt_fusion.1) | copy-start | bytes 1540
  9.9 95.5 %copy-start.40 = (s32[128,8]{0,1:T(8,128)S(1)}, s32[128,8]{0,1:T(8,128)}, u32[]{:S(2)}) copy-start(s32[128,8]{0,1:T(8,128)} %param.29) | copy-start | bytes 12292
  59.0 124.8 %all-gather.16.cloned.1.call-start = ((), (), s32[]{:S(2)}) async-start(), calls=%async_computation.15 | async-start | bytes 5013504 | tf_op jit(solution)/shard_map/all_gather | solution.py:80
  59.6 150.1 %all-gather.14.cloned.1.call-start = ((), (), s32[]{:S(2)}) async-start(), calls=%async_computation.14 | async-start | bytes 1179648 | tf_op jit(solution)/shard_map/all_gather | solution.py:109
  60.8 127.3 %copy-start.31 = (f32[128,32]{0,1:T(8,128)}, f32[128,32]{0,1:T(8,128)S(1)}, u32[]{:S(2)}) copy-start(f32[128,32]{0,1:T(8,128)S(1)} %get-tuple-element.242) | copy-start | bytes 49156
  104.7 161.4 %all-gather.18.cloned.1.call-start = ((), (), s32[]{:S(2)}) async-start(), calls=%async_computation.16 | async-start | bytes 5013504 | tf_op jit(solution)/shard_map/all_gather | solution.py:83
  276.5 53.5 %all-to-all-start = ((bf16[8,3,56,1536]{3,2,1,0:T(8,128)(2,1)}), bf16[8,3,56,1536]{3,2,1,0:T(8,128)(2,1)}, u32[]{:S(2)}, u32[]{:S(2)}) async-start(bf16[8,3,56,1536]{3,2,1,0:T(8,128)(2,1)} %bitcast.336), calls=%async_computation | async-start | bytes 8257536 | tf_op jit(solution)/shard_map/all_to_all | solution.py:154
  329.9 54.1 %all-to-all-start.2 = ((bf16[8,3,56,1536]{3,2,1,0:T(8,128)(2,1)}), bf16[8,3,56,1536]{3,2,1,0:T(8,128)(2,1)}, u32[]{:S(2)}, u32[]{:S(2)}) async-start(bf16[8,3,56,1536]{3,2,1,0:T(8,128)(2,1)} %bitcast.337), calls=%async_computation.2 | async-start | bytes 8257536 | tf_op jit(solution)/shard_map/all_to_all | solution.py:176
  405.7 53.5 %all-to-all-start.3 = ((bf16[8,3,56,1536]{3,2,1,0:T(8,128)(2,1)}), bf16[8,3,56,1536]{3,2,1,0:T(8,128)(2,1)}, u32[]{:S(2)}, u32[]{:S(2)}) async-start(bf16[8,3,56,1536]{3,2,1,0:T(8,128)(2,1)} %copy.130), calls=%async_computation.3 | async-start | bytes 8257536 | tf_op jit(solution)/shard_map/all_to_all | solution.py:187
  459.2 53.5 %all-to-all-start.1 = ((bf16[8,3,56,1536]{3,2,1,0:T(8,128)(2,1)}), bf16[8,3,56,1536]{3,2,1,0:T(8,128)(2,1)}, u32[]{:S(2)}, u32[]{:S(2)}) async-start(bf16[8,3,56,1536]{3,2,1,0:T(8,128)(2,1)} %copy.127), calls=%async_computation.1 | async-start | bytes 8257536 | tf_op jit(solution)/shard_map/all_to_all | solution.py:163
  464.5 164.7 %reduce-scatter.22.cloned.1.call-start = ((), (), s32[]{:S(2)}) async-start(), calls=%async_computation.21 | async-start | bytes 1179648
  602.0 60.3 %reduce-scatter.24.cloned.1.call-start = ((), (), s32[]{:S(2)}) async-start(), calls=%async_computation.22 | async-start | bytes 1179648
  608.9 130.2 %reduce-scatter.16.cloned.1.call-start = ((), (), s32[]{:S(2)}) async-start(), calls=%async_computation.18 | async-start | bytes 1671168 | tf_op jit(solution)/shard_map/reduce_scatter | solution.py:269
  632.5 182.5 %reduce-scatter.18.cloned.1.call-start = ((), (), s32[]{:S(2)}) async-start(), calls=%async_computation.19 | async-start | bytes 1671168 | tf_op jit(solution)/shard_map/reduce_scatter | solution.py:272
  665.5 231.1 %reduce-scatter.14.cloned.1.call-start = ((), (), s32[]{:S(2)}) async-start(), calls=%async_computation.17 | async-start | bytes 5013504 | tf_op jit(solution)/shard_map/reduce_scatter | solution.py:266
  669.4 308.6 %reduce-scatter.20.cloned.1.call-start = ((), (), s32[]{:S(2)}) async-start(), calls=%async_computation.20 | async-start | bytes 5013504 | tf_op jit(solution)/shard_map/reduce_scatter | solution.py:275
  674.0 379.3 %reduce-scatter.26.cloned.1.call-start = ((), (), s32[]{:S(2)}) async-start(), calls=%async_computation.23 | async-start | bytes 417792
  683.7 294.6 %copy-start.55 = (bf16[8,3,56,512]{3,2,0,1:T(8,128)(2,1)S(1)}, bf16[8,3,56,512]{3,2,0,1:T(8,128)(2,1)}, u32[]{:S(2)}) copy-start(bf16[8,3,56,512]{3,2,0,1:T(8,128)(2,1)} %copy-done.54) | copy-start | bytes 4128772
  683.7 437.1 %all-reduce.11.cloned.1.call-start = ((), (), s32[]{:S(2)}) async-start(), calls=%async_computation.25 | async-start | bytes 1572864 | tf_op jit(solution)/shard_map/psum | solution.py:290
  978.1 339.2 %all-reduce.9.cloned.1.call-start = ((), (), s32[]{:S(2)}) async-start(), calls=%async_computation.24 | async-start | bytes 28311552 | tf_op jit(solution)/shard_map/psum | solution.py:284
  (55 other events, 936.2 us)
Sparse Core Ops, SparseCore 0:
  10.2 46.0 all-gather.7
  58.5 43.1 all-gather.11
  104.1 24.3 all-gather.9
  130.5 53.3 all-gather.15
  185.9 23.6 all-gather.13
  211.7 54.2 all-gather.17
  602.1 27.0 reduce-scatter.21
  631.6 30.6 reduce-scatter.23
  665.5 73.5 reduce-scatter.15
  742.1 72.8 reduce-scatter.17
  818.9 77.5 reduce-scatter.13
  900.3 77.6 reduce-scatter.19
  981.8 71.4 reduce-scatter.25
  1055.9 61.1 all-reduce.10
  1121.7 195.4 all-reduce.8
where the time goes:
time: 1350 us; the launch traced here: 1340 us
  waiting for transfers between devices  932 us (69%)
  matrix products  160 us (12%)
  blocking collectives  80.2 us (6%)
  local copies, waits for them, and re-layouts  71.5 us (5%)
  other arithmetic  59.8 us (4%)
  starting transfers between devices  23 us (2%)
  between operations  15.5 us (1%)
    psum x1, waiting for transfers between devices, body(): lax.psum(gate_part.astype(jnp.bfloat16), 'dp').astype(jnp.float32)  190 us
    unnamed x18, waiting for transfers between devices  116 us
    reduce_scatter x1, waiting for transfers between devices, body(): lax.psum_scatter(query_part.astype(jnp.bfloat16), 'dp', scatter_dimension...  81.6 us
    reduce_scatter x1, waiting for transfers between devices, body(): lax.psum_scatter(out_part.astype(jnp.bfloat16), 'dp', scatter_dimension=0...  81.5 us
    reduce_scatter x1, waiting for transfers between devices, body(): lax.psum_scatter(value_part.astype(jnp.bfloat16), 'dp', scatter_dimension...  75.9 us
    all_gather x1, waiting for transfers between devices, body(): lax.all_gather(query_weight, 'dp', axis=0, tiled=True)  53.9 us
    reduce_scatter x1, waiting for transfers between devices, body(): lax.psum_scatter(key_part.astype(jnp.bfloat16), 'dp', scatter_dimension=0...  47.7 us
    all_gather x1, waiting for transfers between devices, body(): lax.all_gather(value_weight, 'dp', axis=0, tiled=True)  46.4 us
  transfers between devices with their start and end apart: 19, of which 18 were waited for; matrix products, arithmetic and copies ran while one was open for 11% of the time, Pallas kernels for 0%

commit v1 on v0

v1 whole, which is shorter than its diff:
```python
import functools
import math

import jax
import jax.numpy as jnp
from jax import lax
from jax.experimental import pallas as pl
from jax.experimental.pallas import tpu as pltpu
from jax.sharding import PartitionSpec as P

QH = 24
KVH = 8
HD = 64
TOP = 8
EXP_DEV = 3
CAP = 56
D = 1536
FFE = 512
ROWS = 128
OWN = 8
GROUP = 1024
DP = 16
EXPERTS = 24
HEADS = 3
QW = HEADS * HD
PAIR = 2 * CAP
PAIRS = OWN // 2
SLOTS = OWN * CAP
BLK = 256
WW = 384
XW = D + 128
EPS = 1e-06
THETA = 10000.0
VMEM = 60 * 1024 * 1024
f32 = jnp.float32
bf16 = jnp.bfloat16

NN = (((1,), (0,)), ((), ()))
NT = (((1,), (1,)), ((), ()))
TN = (((0,), (0,)), ((), ()))


def mm(a, b, dims=NN):
    return lax.dot_general(a, b, dims, preferred_element_type=f32)


def iota(shape, dim):
    return lax.broadcasted_iota(jnp.int32, shape, dim)


def swap_halves(v):
    lane = iota(v.shape, 1) % HD
    width = v.shape[1]
    ahead = pltpu.roll(v, width - HD // 2, 1)
    behind = pltpu.roll(v, HD // 2, 1)
    return jnp.where(lane < HD // 2, ahead, behind)


def block_mask(start_ref, at, keys):
    place = at + iota((BLK, keys), 0)
    key = iota((BLK, keys), 1)
    first = start_ref[pl.ds(at, BLK), :]
    return (key <= place) & (key >= first)


def attend_kernel(x_ref, w_ref, gain_ref, cos_ref, sin_ref, start_ref, normed_ref, qkv_ref, mix_ref, log_ref):
    for at in range(0, GROUP, BLK):
        rows = pl.ds(at, BLK)
        x = x_ref[rows, :].astype(f32)
        scale = lax.rsqrt(jnp.mean(x * x, axis=-1, keepdims=True) + EPS)
        normed = (x * scale * gain_ref[...]).astype(bf16)
        normed_ref[rows, :] = normed
        raw = mm(normed, w_ref[...])
        turned = raw[:, :BLK]
        turned = turned * cos_ref[rows, :] + swap_halves(turned) * sin_ref[rows, :]
        qkv_ref[rows, 0:BLK] = turned.astype(bf16)
        qkv_ref[rows, BLK:WW] = raw[:, BLK:WW].astype(bf16)
    for at in range(0, GROUP, BLK):
        rows = pl.ds(at, BLK)
        keys = at + BLK
        seen = block_mask(start_ref, at, keys)
        k_h = qkv_ref[0:keys, QW : QW + HD]
        v_h = qkv_ref[0:keys, BLK : BLK + HD]
        for r in range(HEADS):
            q_h = qkv_ref[rows, r * HD : (r + 1) * HD] * jnp.asarray(HD**-0.5, bf16)
            scores = jnp.where(seen, mm(q_h, k_h, NT), -1e30)
            top = jnp.max(scores, axis=-1, keepdims=True)
            terms = jnp.exp(scores - top)
            total = jnp.sum(terms, axis=-1, keepdims=True)
            prob = (terms / total).astype(bf16)
            mix_ref[rows, r * HD : (r + 1) * HD] = mm(prob, v_h).astype(bf16)
            log_ref[rows, r : r + 1] = top + jnp.log(total)


def out_kernel(mix_ref, wo_ref, x_ref, gain_ref, hidden_ref, normed_ref):
    hidden = x_ref[...].astype(f32)
    for j in range(OWN):
        hidden = hidden + mm(mix_ref[j], wo_ref[j * QW : (j + 1) * QW, :])
    hidden_ref[...] = hidden
    scale = lax.rsqrt(jnp.mean(hidden * hidden, axis=-1, keepdims=True) + EPS)
    normed_ref[...] = (hidden * scale * gain_ref[...]).astype(bf16)


def router_probs(normed, w_ref):
    logits = mm(normed, w_ref[:, BLK:WW])
    lane = iota(logits.shape, 1)
    real = (lane >= HD) & (lane < HD + EXPERTS)
    logits = jnp.where(real, logits, -1e30)
    terms = jnp.exp(logits - jnp.max(logits, axis=-1, keepdims=True))
    terms = jnp.where(real, terms, 0.0)
    return terms / jnp.sum(terms, axis=-1, keepdims=True)


def pick_rows(slot_row, b):
    row = slot_row[:, b * BLK : (b + 1) * BLK]
    return iota((PAIR, BLK), 0) == row


def expert_kernel(
    own_ref, n_ref, dy_ref, routes_ref, w_ref, wg_ref, wu_ref, wd_ref,
    gg_ref, gu_ref, gd_ref, hg_ref, hu_ref, gated_ref, p_ref, slot_ref,
    prob_ref, x_ref, d_ref, gate_ref,
):
    e = pl.program_id(0)
    own = own_ref[0] * EXP_DEV + e

    @pl.when(e == 0)
    def _():
        for at in range(0, GROUP, BLK):
            probs = router_probs(n_ref[at : at + BLK, :], w_ref)
            prob_ref[:, at : at + BLK] = jnp.transpose(probs)

    chosen = jnp.max((routes_ref[...] == own).astype(f32), axis=0, keepdims=True)
    gate_row = jnp.sum(jnp.where(iota((128, GROUP), 0) == HD + own, prob_ref[...], 0.0), axis=0, keepdims=True)
    before = (iota((ROWS, ROWS), 0) < iota((ROWS, ROWS), 1)).astype(f32).astype(bf16)
    ranks = []
    for s in range(OWN):
        part = jnp.broadcast_to(chosen[:, s * ROWS : (s + 1) * ROWS], (8, ROWS)).astype(bf16)
        ranks.append(mm(part, before)[0:1] + float(CAP * (s % 2)))
    rank = jnp.concatenate(ranks, axis=1)
    slot_row = jnp.where(chosen > 0.0, rank, -1.0).astype(jnp.int32)
    slot_ref[0] = jnp.broadcast_to(slot_row, (8, GROUP))
    for b in range(PAIRS):
        pick = pick_rows(slot_row, b)
        pick_b = pick.astype(f32).astype(bf16)
        tokens = pl.ds(b * BLK, BLK)
        slots = pl.ds(b * PAIR, PAIR)
        x_ref[slots, :] = mm(pick_b, n_ref[tokens, :]).astype(bf16)
        d_ref[slots, :] = mm(pick_b, dy_ref[tokens, 0:D]).astype(bf16)
        gate_ref[slots, :] = jnp.sum(jnp.where(pick, gate_row[:, b * BLK : (b + 1) * BLK], 0.0), axis=1, keepdims=True)
    x = x_ref[...]
    gate_in = mm(x, wg_ref[0])
    up_in = mm(x, wu_ref[0])
    sig = jax.nn.sigmoid(gate_in)
    silu = gate_in * sig
    inner = (silu * up_in).astype(bf16)
    out = mm(inner, wd_ref[0]).astype(bf16).astype(f32)
    gates = gate_ref[...]
    gated_ref[0] = (gates * out).astype(bf16)
    dy = d_ref[...].astype(f32)
    p = jnp.sum(dy * out, axis=-1, keepdims=True)
    high = p.astype(bf16).astype(f32)
    lane = iota((SLOTS, 128), 1)
    p_ref[0] = jnp.where(lane == HD + own, high, jnp.where(lane == HD + 32 + own, p - high, 0.0)).astype(bf16)
    slot_grad = (gates * dy).astype(bf16)
    inner_grad = mm(slot_grad, wd_ref[0], NT)
    gd_ref[0] = mm(inner, slot_grad, TN).astype(bf16)
    hg = (inner_grad * up_in * sig * (1.0 + gate_in * (1.0 - sig))).astype(bf16)
    hu = (inner_grad * silu).astype(bf16)
    hg_ref[0] = hg
    hu_ref[0] = hu
    gg_ref[0] = mm(x, hg, TN).astype(bf16)
    gu_ref[0] = mm(x, hu, TN).astype(bf16)


def return_kernel(hg_ref, hu_ref, gated_ref, p_ref, slot_ref, wg_ref, wu_ref, dx_ref, mix_ref, rows_ref):
    e = pl.program_id(0)
    rows_ref[e] = (mm(hg_ref[0], wg_ref[0], NT) + mm(hu_ref[0], wu_ref[0], NT)).astype(bf16)

    @pl.when(e == EXP_DEV - 1)
    def _():
        for b in range(PAIRS):
            tokens = pl.ds(b * BLK, BLK)
            slots = pl.ds(b * PAIR, PAIR)
            pick = jnp.concatenate(
                [pick_rows(slot_ref[k, 0:1, :], b).astype(f32).astype(bf16) for k in range(EXP_DEV)], axis=0
            )
            grads = jnp.concatenate([rows_ref[k, slots, :] for k in range(EXP_DEV)], axis=0)
            dx_ref[tokens, 0:D] = mm(pick, grads, TN).astype(bf16)
            probs = jnp.concatenate([p_ref[k, slots, :] for k in range(EXP_DEV)], axis=0)
            dx_ref[tokens, D:XW] = mm(pick, probs, TN).astype(bf16)
            outs = jnp.concatenate([gated_ref[k, slots, :] for k in range(EXP_DEV)], axis=0)
            mix_ref[tokens, :] = mm(pick, outs, TN).astype(bf16)


def hidden_kernel(part_ref, dy_ref, hidden_ref, normed_ref, gain_ref, w_ref, wo_ref, grad_ref, gain_grad_ref, send_ref):
    hidden = hidden_ref[...]
    scale = lax.rsqrt(jnp.mean(hidden * hidden, axis=-1, keepdims=True) + EPS)
    unit = hidden * scale
    total = part_ref[0].astype(f32)
    for s in range(1, OWN):
        total = total + part_ref[s].astype(f32)
    tail = total[:, D:XW]
    probs = router_probs(normed_ref[...], w_ref)
    p = tail + pltpu.roll(tail, 128 - 32, 1)
    logit_grad = probs * (p - jnp.sum(p * probs, axis=-1, keepdims=True))
    high = logit_grad.astype(bf16)
    low = (logit_grad - high.astype(f32)).astype(bf16)
    router = w_ref[:, BLK:WW]
    normed_grad = total[:, 0:D] + mm(high, router, NT) + mm(low, router, NT)
    gain_grad_ref[...] = jnp.sum(normed_grad * unit, axis=0, keepdims=True)
    unit_grad = normed_grad * gain_ref[...]
    grad = dy_ref[...].astype(f32) + scale * (unit_grad - unit * jnp.mean(unit_grad * unit, axis=-1, keepdims=True))
    grad_ref[...] = grad
    branch = grad.astype(bf16)
    for j in range(OWN):
        cols = slice(j * QW, (j + 1) * QW)
        send_ref[j, :, 0:QW] = mm(branch, wo_ref[cols, :], NT).astype(bf16)
        send_ref[j, :, QW : 2 * QW] = grad[:, cols].astype(bf16)
        send_ref[j, :, 2 * QW : 2 * QW + 128] = high


def attend_back_kernel(qkv_ref, log_ref, g_ref, cos_ref, sin_ref, start_ref, dqkv_ref, turn_ref, dk_ref, dv_ref):
    dk_ref[...] = jnp.zeros_like(dk_ref)
    dv_ref[...] = jnp.zeros_like(dv_ref)
    for at in range(0, GROUP, BLK):
        rows = pl.ds(at, BLK)
        keys = at + BLK
        seen = block_mask(start_ref, at, keys)
        k_h = qkv_ref[0:keys, QW : QW + HD]
        v_h = qkv_ref[0:keys, BLK : BLK + HD]
        for r in range(HEADS):
            q_h = qkv_ref[rows, r * HD : (r + 1) * HD] * jnp.asarray(HD**-0.5, bf16)
            g_h = g_ref[rows, r * HD : (r + 1) * HD]
            scores = jnp.where(seen, mm(q_h, k_h, NT), -1e30)
            prob = jnp.exp(scores - log_ref[rows, r : r + 1])
            dv_ref[0:keys, :] += mm(prob.astype(bf16), g_h, TN)
            prob_grad = mm(g_h, v_h, NT)
            delta = jnp.sum(prob_grad * prob, axis=-1, keepdims=True)
            score_grad = (prob * (prob_grad - delta)).astype(bf16)
            turn_ref[rows, r * HD : (r + 1) * HD] = mm(score_grad, k_h) * (HD**-0.5)
            dk_ref[0:keys, :] += mm(score_grad, q_h, TN)
    turn_ref[:, QW : QW + HD] = dk_ref[...]
    for at in range(0, GROUP, BLK):
        rows = pl.ds(at, BLK)
        turned = turn_ref[rows, :]
        turned = turned * cos_ref[rows, :] - swap_halves(turned) * sin_ref[rows, :]
        dqkv_ref[rows, 0:BLK] = turned.astype(bf16)
        dqkv_ref[rows, BLK : BLK + HD] = dv_ref[rows, :].astype(bf16)
        dqkv_ref[rows, BLK + HD : WW] = jnp.zeros((BLK, WW - BLK - HD), bf16)


def weight_kernel(normed_ref, dqkv_ref, mix_ref, got_ref, n_ref, moe_gain_ref, x_ref, w_ref, back_ref, pay_ref, gain_ref):
    gain_ref[...] = jnp.zeros_like(gain_ref)
    for at in range(0, GROUP, BLK):
        rows = pl.ds(at, BLK)
        back = mm(dqkv_ref[rows, :], w_ref[...], NT)
        back_ref[rows, :] = back.astype(bf16)
        x = x_ref[rows, :].astype(f32)
        unit = x * lax.rsqrt(jnp.mean(x * x, axis=-1, keepdims=True) + EPS)
        gain_ref[0:1, :] += jnp.sum(back * unit, axis=0, keepdims=True)
    pay_ref[:, 0:BLK] = mm(normed_ref[...], dqkv_ref[:, 0:BLK], TN).astype(bf16)
    hid = got_ref[:, 128:WW]
    hid = jnp.where(iota((GROUP, BLK), 1) < HD, jnp.zeros_like(hid), hid)
    value = jnp.concatenate([dqkv_ref[:, BLK:WW], jnp.zeros((GROUP, 128), bf16)], axis=1)
    pay_ref[:, BLK : 2 * BLK] = (mm(normed_ref[...], value, TN) + mm(mix_ref[...], hid, TN)).astype(bf16)
    router = mm(n_ref[...], got_ref[:, 2 * QW : 2 * QW + 128], TN)
    attn_gain = jnp.transpose(jnp.broadcast_to(gain_ref[0:1, :], (128, D)))
    moe_gain = jnp.transpose(jnp.broadcast_to(moe_gain_ref[...], (128, D)))
    lane = iota((D, 128), 1)
    tail = jnp.where(lane == 0, attn_gain, jnp.where(lane == 1, moe_gain, jnp.where(lane >= HD, router, 0.0)))
    pay_ref[:, 2 * BLK : 2 * BLK + 128] = tail.astype(bf16)


def input_kernel(part_ref, x_ref, gain_ref, hidden_grad_ref, out_ref):
    x = x_ref[...].astype(f32)
    scale = lax.rsqrt(jnp.mean(x * x, axis=-1, keepdims=True) + EPS)
    unit = x * scale
    total = part_ref[0].astype(f32)
    for s in range(1, OWN):
        total = total + part_ref[s].astype(f32)
    unit_grad = total * gain_ref[...]
    out_ref[...] = (
        hidden_grad_ref[...] + scale * (unit_grad - unit * jnp.mean(unit_grad * unit, axis=-1, keepdims=True))
    ).astype(bf16)


def sds(shape, dtype):
    return jax.ShapeDtypeStruct(shape, dtype)


def call(kernel, outs, scratch=(), cost=None, **grid):
    return pl.pallas_call(
        kernel,
        out_shape=outs,
        scratch_shapes=list(scratch),
        compiler_params=pltpu.CompilerParams(vmem_limit_bytes=VMEM),
        cost_estimate=cost,
        **grid,
    )


def cost(gmac, mbytes):
    return pl.CostEstimate(flops=int(2e9 * gmac), bytes_accessed=int(1e6 * mbytes), transcendentals=0)


def body(
    tokens, norm_attn, query_weight, key_weight, value_weight, out_weight, norm_moe, router_weight,
    gate_weight, up_weight, down_weight, routes, seq_lengths, out_grad,
):
    own = lax.axis_index("expert")
    gain_one = norm_attn.reshape(1, D)
    gain_two = norm_moe.reshape(1, D)

    shard = jnp.concatenate(
        [
            lax.dynamic_slice_in_dim(query_weight, own * QW, QW, 1),
            lax.dynamic_slice_in_dim(key_weight, own * HD, HD, 1),
            lax.dynamic_slice_in_dim(value_weight, own * HD, HD, 1),
            router_weight,
            jnp.zeros((D // DP, WW - BLK - HD - EXPERTS), bf16),
        ],
        axis=1,
    )
    weights = lax.all_to_all(
        jnp.broadcast_to(shard[None], (DP, D // DP, WW)), "dp", 0, 0, tiled=True
    ).reshape(D, WW)
    x_all = lax.all_gather(tokens, "expert", axis=0, tiled=True)
    out_full = lax.all_gather(out_weight, "dp", axis=0, tiled=True)
    dy_own = jnp.concatenate([out_grad, routes.astype(bf16), jnp.zeros((ROWS, XW - D - TOP), bf16)], axis=1)
    dy_all = lax.all_gather(dy_own, "expert", axis=0, tiled=True)
    routes_t = dy_all[:, D : D + TOP].T.astype(jnp.int32)

    end_one = seq_lengths[0, 0]
    end_two = end_one + seq_lengths[0, 1]
    place = jnp.arange(GROUP, dtype=jnp.int32)
    start = jnp.where(place >= end_two, end_two, jnp.where(place >= end_one, end_one, 0)).astype(jnp.int32)
    steps = jnp.arange(HD // 2, dtype=f32)
    freq = jnp.exp(steps * (-2.0 * math.log(THETA) / HD))
    angles = (place - start).astype(f32)[:, None] * freq[None, :]
    cos_half, sin_half = jnp.cos(angles), jnp.sin(angles)
    cos_t = jnp.tile(cos_half, (1, 8))
    sin_t = jnp.tile(jnp.concatenate([-sin_half, sin_half], axis=1), (1, 4))
    start = start.reshape(GROUP, 1)

    normed_one, qkv, mix, logs = call(
        attend_kernel,
        [sds((GROUP, D), bf16), sds((GROUP, WW), bf16), sds((GROUP, QW), bf16), sds((GROUP, 8), f32)],
        cost=cost(2, 10),
    )(x_all, weights, gain_one, cos_t, sin_t, start)

    mix_own = lax.all_to_all(mix, "expert", 0, 0, tiled=True).reshape(OWN, ROWS, QW)
    hidden, normed_two = call(out_kernel, [sds((ROWS, D), f32), sds((ROWS, D), bf16)], cost=cost(0.5, 6))(
        mix_own, out_full, tokens, gain_two
    )
    n_all = lax.all_gather(normed_two, "expert", axis=0, tiled=True)

    whole = lambda *shape: pl.BlockSpec(shape, lambda e: (0,) * len(shape), pipeline_mode=pl.Buffered(1))
    each = lambda *shape: pl.BlockSpec((1,) + shape, lambda e: (e, 0, 0))
    gg, gu, gd, hg, hu, gated, p_slots, slot_rows = call(
        expert_kernel,
        [
            sds((EXP_DEV, D, FFE), bf16), sds((EXP_DEV, D, FFE), bf16), sds((EXP_DEV, FFE, D), bf16),
            sds((EXP_DEV, SLOTS, FFE), bf16), sds((EXP_DEV, SLOTS, FFE), bf16), sds((EXP_DEV, SLOTS, D), bf16),
            sds((EXP_DEV, SLOTS, 128), bf16), sds((EXP_DEV, 8, GROUP), jnp.int32),
        ],
        scratch=[
            pltpu.VMEM((128, GROUP), f32), pltpu.VMEM((SLOTS, D), bf16), pltpu.VMEM((SLOTS, D), bf16),
            pltpu.VMEM((SLOTS, 1), f32),
        ],
        cost=cost(9, 45),
        grid=(EXP_DEV,),
        in_specs=[
            pl.BlockSpec(memory_space=pltpu.SMEM), whole(GROUP, D), whole(GROUP, XW), whole(TOP, GROUP), whole(D, WW),
            each(D, FFE), each(D, FFE), each(FFE, D),
        ],
        out_specs=[
            each(D, FFE), each(D, FFE), each(FFE, D), each(SLOTS, FFE), each(SLOTS, FFE), each(SLOTS, D),
            each(SLOTS, 128), each(8, GROUP),
        ],
    )(own.reshape(1).astype(jnp.int32), n_all, dy_all, routes_t, weights, gate_weight, up_weight, down_weight)

    down_total, gate_total, up_total = lax.psum((gd, gg, gu), "dp")

    dx_part, mix_part = call(
        return_kernel,
        [sds((GROUP, XW), bf16), sds((GROUP, D), bf16)],
        scratch=[pltpu.VMEM((EXP_DEV, SLOTS, D), bf16)],
        cost=cost(4, 20),
        grid=(EXP_DEV,),
        in_specs=[
            each(SLOTS, FFE), each(SLOTS, FFE), whole(EXP_DEV, SLOTS, D), whole(EXP_DEV, SLOTS, 128),
            whole(EXP_DEV, 8, GROUP), each(D, FFE), each(D, FFE),
        ],
        out_specs=[whole(GROUP, XW), whole(GROUP, D)],
    )(hg, hu, gated, p_slots, slot_rows, gate_weight, up_weight)

    dx_parts = lax.all_to_all(dx_part, "expert", 0, 0, tiled=True).reshape(OWN, ROWS, XW)
    hidden_grad, moe_gain, send = call(
        hidden_kernel,
        [sds((ROWS, D), f32), sds((1, D), f32), sds((OWN, ROWS, 512), bf16)],
        cost=cost(0.6, 10),
    )(dx_parts, out_grad, hidden, normed_two, gain_two, weights, out_full)
    got = lax.all_to_all(send.reshape(GROUP, 512), "expert", 0, 0, tiled=True)
    dqkv = call(
        attend_back_kernel,
        sds((GROUP, WW), bf16),
        scratch=[pltpu.VMEM((GROUP, BLK), f32), pltpu.VMEM((GROUP, HD), f32), pltpu.VMEM((GROUP, HD), f32)],
        cost=cost(4, 8),
    )(qkv, logs, got, cos_t, sin_t, start)
    mix_all = lax.all_to_all(
        jnp.broadcast_to(jnp.moveaxis(mix_own, 0, 1).reshape(1, ROWS, D), (OWN, ROWS, D)).reshape(GROUP, D),
        "expert", 0, 0, tiled=True,
    )
    back_part, pay = call(
        weight_kernel,
        [sds((GROUP, D), bf16), sds((D, 640), bf16)],
        scratch=[pltpu.VMEM((8, D), f32)],
        cost=cost(2, 20),
    )(normed_one, dqkv, mix_all, got, n_all, moe_gain, x_all, weights)

    pay_parts = lax.all_to_all(pay, "dp", 0, 0, tiled=True).reshape(DP, D // DP, 640)
    back_parts = lax.all_to_all(back_part, "expert", 0, 0, tiled=True).reshape(OWN, ROWS, D)
    pay_own = jnp.sum(pay_parts.astype(f32), axis=0)
    pay_all = lax.all_to_all(
        jnp.broadcast_to(pay_own.astype(bf16)[None], (OWN, D // DP, 640)), "expert", 0, 0, tiled=True
    )
    join = lambda lo, hi: jnp.moveaxis(pay_all[:, :, lo:hi], 0, 1).reshape(D // DP, OWN * (hi - lo)).astype(f32)
    query_total, key_total, value_total, out_total = join(0, QW), join(QW, BLK), join(BLK, BLK + HD), join(BLK + HD, 512)
    router_total = pay_own[:, 512 + HD : 512 + HD + EXPERTS]
    gains = jnp.sum(pay_all[:, :, 512:514].astype(f32), axis=0).T.reshape(1, 2, D // DP)
    gains = jnp.pad(gains, ((0, 0), (0, 6), (0, 32)))
    gains = lax.all_to_all(jnp.broadcast_to(gains, (DP, 8, 128)), "dp", 0, 0, tiled=True)
    gain_attn = gains[:, 0, : D // DP].reshape(D)
    gain_moe = gains[:, 1, : D // DP].reshape(D)

    input_grad = call(input_kernel, sds((ROWS, D), bf16), cost=cost(0, 6))(back_parts, tokens, gain_one, hidden_grad)
    mix_parts = lax.all_to_all(mix_part, "expert", 0, 0, tiled=True).reshape(OWN, ROWS, D)
    layer_out = (hidden + jnp.sum(mix_parts.astype(f32), axis=0)).astype(bf16)
    return (
        layer_out, input_grad, gain_attn, query_total, key_total, value_total, out_total, gain_moe, router_total,
        gate_total.astype(f32), up_total.astype(f32), down_total.astype(f32),
    )


def solution(mesh):
    both, dp, expert = P(("dp", "expert"), None), P("dp", None), P("expert", None, None)
    return jax.shard_map(
        body,
        mesh=mesh,
        in_specs=(both, P(), dp, dp, dp, dp, P(), dp, expert, expert, expert, both, dp, both),
        out_specs=(both, both, P(), dp, dp, dp, dp, P(), dp, expert, expert, expert),
        check_vma=False,
    )
```

time: 1350 us -> 560 us (0.41)
  waiting for transfers between devices: 932 us -> 235 us
  matrix products: 160 us -> 0 us
  Pallas kernels: 0 us -> 99.4 us
  other arithmetic: 59.8 us -> 31.6 us
  starting transfers between devices: 23 us -> 48.1 us
  local copies, waits for them, and re-layouts: 71.5 us -> 55.4 us
  blocking collectives: 80.2 us -> 64.6 us
    reduce_scatter x4 -> x0, waiting for transfers between devices: 287 us -> none  [the longest x1 81.6 us: body(): lax.psum_scatter(query_part.astype(jnp.bfloat16), 'dp', scatter_dimension...]
    psum x2 -> x1, waiting for transfers between devices: 190 us -> 0.01 us  [body(): down_total, gate_total, up_total = lax.psum((gd, gg, gu), 'dp')]
    dot_general x80 -> x0, matrix products: 160 us -> none  [the longest x8 12.5 us: attend_back(): jnp.einsum('qrd,kd->rqk', q_h, k_h, preferred_element_type=f32)]
    all_gather x6 -> x4, waiting for transfers between devices: 208 us -> 71.7 us  [the longest x1 30.8 us: body(): dy_all = lax.all_gather(dy_own, 'expert', axis=0, tiled=True)]
    unnamed x18 -> x5, waiting for transfers between devices: 116 us -> 1.97 us
    pallas_call x0 -> x8, Pallas kernels: none -> 99.4 us  [the longest x1 29.1 us: body(): call(expert_kernel, [sds((EXP_DEV, D, FFE), bf16), sds((EXP_DEV, D, FFE),...]
    all_to_all x0 -> x2, blocking collectives: none -> 64.6 us  [the longest x1 46.2 us: body(): lax.all_to_all(pay, 'dp', 0, 0, tiled=True).reshape(DP, D // DP, 640)]
    psum x2 -> x0, blocking collectives: 61.1 us -> none  [the longest x1 31.4 us: body(): lax.psum(attn_gain_part.astype(jnp.bfloat16), 'dp').astype(jnp.float32)]
  transfers between devices with their start and end apart: 19 -> 13, of which waited for: 18 -> 11; matrix products, arithmetic and copies ran while one was open for 11% -> 12% of each run, Pallas kernels for 0% -> 10%
where the time goes in v1:
time: 560 us; the launch traced here: 550 us
  waiting for transfers between devices  235 us (42%)
  Pallas kernels  99.4 us (18%)
  blocking collectives  64.6 us (12%)
  local copies, waits for them, and re-layouts  55.4 us (10%)
  starting transfers between devices  48.1 us (9%)
  other arithmetic  31.6 us (6%)
  between operations  15.5 us (3%)
    all_to_all x1, blocking collectives, body(): lax.all_to_all(pay, 'dp', 0, 0, tiled=True).reshape(DP, D // DP, 640)  46.2 us
    all_to_all x1, waiting for transfers between devices, body(): lax.all_to_all(dx_part, 'expert', 0, 0, tiled=True).reshape(OWN, ROWS, XW)  39.8 us
    all_to_all x1, waiting for transfers between devices, body(): lax.all_to_all(mix_part, 'expert', 0, 0, tiled=True).reshape(OWN, ROWS, D)  36.7 us
    all_gather x1, waiting for transfers between devices, body(): dy_all = lax.all_gather(dy_own, 'expert', axis=0, tiled=True)  30.8 us
    all_to_all x1, waiting for transfers between devices, body(): lax.all_to_all(back_part, 'expert', 0, 0, tiled=True).reshape(OWN, ROWS, D)  30 us
    pallas_call x1, Pallas kernels, body(): call(expert_kernel, [sds((EXP_DEV, D, FFE), bf16), sds((EXP_DEV, D, FFE),...  29.1 us
    all_gather x1, waiting for transfers between devices, body(): out_full = lax.all_gather(out_weight, 'dp', axis=0, tiled=True)  25 us
    all_to_all x1, waiting for transfers between devices, body(): lax.all_to_all(jnp.broadcast_to(jnp.moveaxis(mix_own, 0, 1).reshape(1, RO...  24.6 us
  transfers between devices with their start and end apart: 13, of which 11 were waited for; matrix products, arithmetic and copies ran while one was open for 12% of the time, Pallas kernels for 10%

profile of v1, /device:TPU:1, one launch (start us, length us, event | category | flops | bytes accessed | tf_op | source)
XLA Modules:
  0.0 549.6 jit_solution(12848768406510581633)
XLA Ops:
  14.8 7.6 %all-to-all-start = ((bf16[16,96,384]{2,1,0:T(8,128)(2,1)}), bf16[16,96,384]{2,1,0:T(8,128)(2,1)S(1)}, u32[]{:S(2)}, u32[]{:S(2)}) async-start(bf16[16,96,384]{2,1,0:T(8,128)(2,1)} %broadcast_in_dim.45), calls=%async_computation | async-start | bytes 2359296 | tf_op jit(solution)/shard_map/all_to_all | solution.py:325
  30.5 8.7 %all-to-all-done = bf16[16,96,384]{2,1,0:T(8,128)(2,1)S(1)} async-done(((bf16[16,96,384]{2,1,0:T(8,128)(2,1)}), bf16[16,96,384]{2,1,0:T(8,128)(2,1)S(1)}, u32[]{:S(2)}, u32[]{:S(2)}) %all-to-all-start) | async-done | bytes 1179680 | tf_op jit(solution)/shard_map/all_to_all | solution.py:325
  41.4 11.9 %shard_map.229 = (bf16[1024,1536]{1,0:T(8,128)(2,1)}, bf16[1024,384]{1,0:T(8,128)(2,1)}, bf16[1024,192]{1,0:T(8,128)(2,1)}, f32[1024,8]{1,0:T(8,128)}) custom-call(bf16[1024,1536]{1,0:T(8,128)(2,1)} %all-gather.5.cloned.1.call-done.x_ref, bf16[1536,384]{1,0:T(8,128)(2,1)} %bitcast.34, f32[1,1536]{1,0:T(1,128)} %reshape.150.gain_ref, ...), custom_call_target="tpu_custom_call" | custom-call | flops 4000000000 | bytes 10000000 | tf_op jit(solution)/shard_map/pallas_call | solution.py:346
  55.2 7.6 %all-to-all-start.1 = ((bf16[8,128,192]{1,2,0:T(8,128)(2,1)}), bf16[8,128,192]{1,2,0:T(8,128)(2,1)S(1)}, u32[]{:S(2)}, u32[]{:S(2)}) async-start(bf16[8,128,192]{1,2,0:T(8,128)(2,1)} %copy.82), calls=%async_computation.1 | async-start | bytes 786432 | tf_op jit(solution)/shard_map/all_to_all | solution.py:352
  63.5 7.5 %all-to-all-done.1 = bf16[8,128,192]{1,2,0:T(8,128)(2,1)S(1)} async-done(((bf16[8,128,192]{1,2,0:T(8,128)(2,1)}), bf16[8,128,192]{1,2,0:T(8,128)(2,1)S(1)}, u32[]{:S(2)}, u32[]{:S(2)}) %all-to-all-start.1) | async-done | bytes 393248 | tf_op jit(solution)/shard_map/all_to_all | solution.py:352
  71.9 25.0 %all-gather.7.cloned.1.call-done.wo_ref = bf16[1536,1536]{1,0:T(8,128)(2,1)} async-done(((bf16[96,1536]{1,0:T(8,128)(2,1)}), bf16[1536,1536]{1,0:T(8,128)(2,1)}) %all-gather.7.cloned.1.call-update) | async-done | bytes 4718608 | tf_op jit(solution)/shard_map/all_gather | solution.py:329
  101.5 30.8 %all-gather.11.cloned.1.call-done = bf16[1024,1664]{0,1:T(8,128)(2,1)} async-done(((bf16[128,1664]{0,1:T(8,128)(2,1)}), bf16[1024,1664]{0,1:T(8,128)(2,1)}) %all-gather.11.cloned.1.call-update) | async-done | bytes 3407888 | tf_op jit(solution)/shard_map/all_gather | solution.py:331
  132.3 15.8 %copy.85.dy_ref = bf16[1024,1664]{1,0:T(8,128)(2,1)} copy(bf16[1024,1664]{0,1:T(8,128)(2,1)} %all-gather.11.cloned.1.call-done) | data formatting | bytes 6815744 | tf_op jit(solution)/shard_map/all_gather | solution.py:331
  149.5 13.8 %all-gather.9.cloned.1.call-done.n_ref = bf16[1024,1536]{1,0:T(8,128)(2,1)} async-done(((bf16[128,1536]{1,0:T(8,128)(2,1)}), bf16[1024,1536]{1,0:T(8,128)(2,1)}) %all-gather.9.cloned.1.call-update) | async-done | bytes 3145744 | tf_op jit(solution)/shard_map/all_gather | solution.py:356
  163.3 29.1 %shard_map.231 = (bf16[3,1536,512]{2,1,0:T(8,128)(2,1)}, bf16[3,1536,512]{2,1,0:T(8,128)(2,1)}, bf16[3,512,1536]{2,1,0:T(8,128)(2,1)}, bf16[3,448,512]{2,1,0:T(8...) custom-call(s32[1]{0:T(128)} %bitcast.6.own_ref, ...), custom_call_target="tpu_custom_call" | custom-call | flops 17999998976 | bytes 45000000 | tf_op jit(solution)/shard_map/pallas_call | solution.py:360
  192.4 15.6 %shard_map.232 = (bf16[1024,1664]{1,0:T(8,128)(2,1)}, bf16[1024,1536]{1,0:T(8,128)(2,1)}) custom-call(bf16[3,448,512]{2,1,0:T(8,128)(2,1)} %get-tuple-element.36.hg_ref, bf16[3,448,512]{2,1,0:T(8,128)(2,1)} %get-tuple-element.37.hu_ref, bf16[3,448,1536]{2,1,0:T(8,128)(2,1)} %get-tuple-element.38.gated_ref, bf16[3,448,128]{2,1,0:T(8,128)(2,1)} %get-tuple-element.39.p_ref, ...), custom_call_target="tpu_custom_call" | custom-call | flops 8000000000 | bytes 20000000 | tf_op jit(solution)/shard_map/pallas_call | solution.py:385
  212.4 39.8 %all-to-all-done.3.part_ref = bf16[8,128,1664]{2,1,0:T(8,128)(2,1)S(1)} async-done(((bf16[8,128,1664]{2,1,0:T(8,128)(2,1)}), bf16[8,128,1664]{2,1,0:T(8,128)(2,1)S(1)}, u32[]{:S(2)}, u32[]{:S(2)}) %all-to-all-start.3) | async-done | bytes 3407904 | tf_op jit(solution)/shard_map/all_to_all | solution.py:398
  254.0 9.0 %shard_map.233 = (f32[128,1536]{1,0:T(8,128)}, f32[1,1536]{1,0:T(1,128)}, bf16[8,128,512]{2,1,0:T(8,128)(2,1)}) custom-call(bf16[8,128,1664]{2,1,0:T(8,128)(2,1)} %copy-done.2, bf16[128,1536]{1,0:T(8,128)(2,1)} %dy_ref.1, f32[128,1536]{1,0:T(8,128)} %get-tuple-element.34.hidden_ref, bf16[128,1536]{1,0:T(8,128)(2,1)} %get-tuple-element.35.normed_ref, ...), custom_call_target="tpu_custom_call" | custom-call | flops 1200000000 | bytes 10000000 | tf_op jit(solution)/shard_map/pallas_call | solution.py:399
  268.4 13.9 %all-to-all-done.4 = bf16[8,128,512]{2,1,0:T(8,128)(2,1)S(1)} async-done(((bf16[8,128,512]{2,1,0:T(8,128)(2,1)}), bf16[8,128,512]{2,1,0:T(8,128)(2,1)S(1)}, u32[]{:S(2)}, u32[]{:S(2)}) %all-to-all-start.4) | async-done | bytes 1048608 | tf_op jit(solution)/shard_map/all_to_all | solution.py:404
  289.3 12.6 %shard_map.234.dqkv_ref = bf16[1024,384]{1,0:T(8,128)(2,1)} custom-call(bf16[1024,384]{1,0:T(8,128)(2,1)} %get-tuple-element.43.qkv_ref, f32[1024,8]{1,0:T(8,128)} %get-tuple-element.44.log_ref, bf16[1024,512]{1,0:T(8,128)(2,1)} %bitcast.40, f32[1024,256]{1,0:T(8,128)} %copy.80.cos_ref, f32[1024,256]{1,0:T(8,128)} %copy.81.sin_ref, ...), custom_call_target="tpu_custom_call" | custom-call | flops 8000000000 | bytes 8000000 | tf_op jit(solution)/shard_map/pallas_call | solution.py:405
  301.9 24.6 %all-to-all-done.5 = bf16[8,128,1536]{2,1,0:T(8,128)(2,1)S(1)} async-done(((bf16[8,128,1536]{2,1,0:T(8,128)(2,1)}), bf16[8,128,1536]{2,1,0:T(8,128)(2,1)S(1)}, u32[]{:S(2)}, u32[]{:S(2)}) %all-to-all-start.5) | async-done | bytes 3145760 | tf_op jit(solution)/shard_map/all_to_all | solution.py:411
  328.2 12.8 %shard_map.235 = (bf16[1024,1536]{1,0:T(8,128)(2,1)}, bf16[1536,640]{1,0:T(8,128)(2,1)}) custom-call(bf16[1024,1536]{1,0:T(8,128)(2,1)} %get-tuple-element.42.normed_ref, bf16[1024,384]{1,0:T(8,128)(2,1)} %shard_map.234.dqkv_ref, bf16[1024,1536]{1,0:T(8,128)(2,1)} %bitcast.33, bf16[1024,512]{1,0:T(8,128)(2,1)} %bitcast.41, ...), custom_call_target="tpu_custom_call" | custom-call | flops 4000000000 | bytes 20000000 | tf_op jit(solution)/shard_map/pallas_call | solution.py:415
  341.1 46.2 %all_to_all.76 = bf16[16,96,640]{2,1,0:T(8,128)(2,1)S(1)} all-to-all(bf16[16,96,640]{2,1,0:T(8,128)(2,1)} %bitcast.48), channel_id=1, replica_groups=mesh['dp'=16,'expert'=8] {'dp'}, dimensions={0} | all-to-all | bytes 3932160 | tf_op jit(solution)/shard_map/all_to_all | solution.py:422
  387.3 10.6 %all-to-all-start.2 = ((bf16[8,128,1536]{2,1,0:T(8,128)(2,1)}), bf16[8,128,1536]{2,1,0:T(8,128)(2,1)}, u32[]{:S(2)}, u32[]{:S(2)}) async-start(bf16[8,128,1536]{2,1,0:T(8,128)(2,1)} %bitcast.46), calls=%async_computation.2 | async-start | bytes 6291456 | tf_op jit(solution)/shard_map/all_to_all | solution.py:438
  398.9 36.7 %all-to-all-done.2 = bf16[8,128,1536]{2,1,0:T(8,128)(2,1)} async-done(((bf16[8,128,1536]{2,1,0:T(8,128)(2,1)}), bf16[8,128,1536]{2,1,0:T(8,128)(2,1)}, u32[]{:S(2)}, u32[]{:S(2)}) %all-to-all-start.2) | async-done | bytes 3145760 | tf_op jit(solution)/shard_map/all_to_all | solution.py:438
  435.7 18.4 %all_to_all.77 = bf16[8,96,640]{2,1,0:T(8,128)(2,1)} all-to-all(bf16[8,96,640]{2,1,0:T(8,128)(2,1)S(1)} %broadcast_in_dim.51), channel_id=1, replica_groups=mesh['dp'=16,'expert'=8] {'expert'}, dimensions={0} | all-to-all | bytes 1966080 | tf_op jit(solution)/shard_map/all_to_all | solution.py:425
  466.2 30.0 %all-to-all-done.6.part_ref = bf16[8,128,1536]{2,1,0:T(8,128)(2,1)S(1)} async-done(((bf16[8,128,1536]{2,1,0:T(8,128)(2,1)}), bf16[8,128,1536]{2,1,0:T(8,128)(2,1)S(1)}, u32[]{:S(2)}, u32[]{:S(2)}) %all-to-all-start.6) | async-done | bytes 3145760 | tf_op jit(solution)/shard_map/all_to_all | solution.py:423
  525.2 7.6 %convert_element_type.102 = f32[3,1536,512]{2,1,0:T(8,128)} convert(bf16[3,1536,512]{2,1,0:T(8,128)(2,1)} %get-tuple-element.104) | non-fusion elementwise | flops 2359296 | bytes 14155776 | tf_op jit(solution)/shard_map/convert_element_type | solution.py:442
  532.7 5.1 convert_element_type.103
  (108 shorter events, 93.3 us)
Async XLA Ops:
  7.2 5.4 copy-start
  7.2 15.2 %copy-start.11 = (f32[1536]{0:T(1024)S(1)}, f32[1536]{0:T(1024)}, u32[]{:S(2)}) copy-start(f32[1536]{0:T(1024)} %param.15) | copy-start | bytes 18436
  7.2 15.8 %copy-start.13 = (s32[1,3]{1,0:T(1,128)S(1)}, s32[1,3]{1,0:T(1,128)}, u32[]{:S(2)}) copy-start(s32[1,3]{1,0:T(1,128)} %param.26) | copy-start | bytes 40
  7.2 34.2 %all-gather.5.cloned.1.call-start = ((), (), s32[]{:S(2)}) async-start(), calls=%async_computation.10 | async-start | bytes 3538944 | tf_op jit(solution)/shard_map/all_gather | solution.py:328
  7.9 89.0 %all-gather.7.cloned.1.call-start = ((), (), s32[]{:S(2)}) async-start(), calls=%async_computation.11 | async-start | bytes 5013504 | tf_op jit(solution)/shard_map/all_gather | solution.py:329
  8.7 123.6 %all-gather.11.cloned.1.call-start = ((), (), s32[]{:S(2)}) async-start(), calls=%async_computation.13 | async-start | bytes 3833856 | tf_op jit(solution)/shard_map/all_gather | solution.py:331
  14.8 24.4 %all-to-all-start = ((bf16[16,96,384]{2,1,0:T(8,128)(2,1)}), bf16[16,96,384]{2,1,0:T(8,128)(2,1)S(1)}, u32[]{:S(2)}, u32[]{:S(2)}) async-start(bf16[16,96,384]{2,1,0:T(8,128)(2,1)} %broadcast_in_dim.45), calls=%async_computation | async-start | bytes 2359296 | tf_op jit(solution)/shard_map/all_to_all | solution.py:325
  41.4 21.5 %copy-start.12 = (f32[1536]{0:T(1024)S(1)}, f32[1536]{0:T(1024)}, u32[]{:S(2)}) copy-start(f32[1536]{0:T(1024)} %param.20) | copy-start | bytes 18436
  55.2 15.7 %all-to-all-start.1 = ((bf16[8,128,192]{1,2,0:T(8,128)(2,1)}), bf16[8,128,192]{1,2,0:T(8,128)(2,1)S(1)}, u32[]{:S(2)}, u32[]{:S(2)}) async-start(bf16[8,128,192]{1,2,0:T(8,128)(2,1)} %copy.82), calls=%async_computation.1 | async-start | bytes 786432 | tf_op jit(solution)/shard_map/all_to_all | solution.py:352
  62.9 100.4 %all-gather.9.cloned.1.call-start = ((), (), s32[]{:S(2)}) async-start(), calls=%async_computation.12 | async-start | bytes 3538944 | tf_op jit(solution)/shard_map/all_gather | solution.py:356
  70.9 30.6 %copy-start.8 = (bf16[8,128,192]{1,2,0:T(8,128)(2,1)}, bf16[8,128,192]{1,2,0:T(8,128)(2,1)S(1)}, u32[]{:S(2)}) copy-start(bf16[8,128,192]{1,2,0:T(8,128)(2,1)S(1)} %all-to-all-done.1) | copy-start | bytes 1179652
  208.1 44.2 %all-to-all-start.3 = ((bf16[8,128,1664]{2,1,0:T(8,128)(2,1)}), bf16[8,128,1664]{2,1,0:T(8,128)(2,1)S(1)}, u32[]{:S(2)}, u32[]{:S(2)}) async-start(bf16[8,128,1664]{2,1,0:T(8,128)(2,1)} %bitcast.45), calls=%async_computation.3 | async-start | bytes 6815744 | tf_op jit(solution)/shard_map/all_to_all | solution.py:398
  211.9 313.3 %all-reduce.4.cloned.1.call-start = ((), (), s32[]{:S(2)}) async-start(), calls=%async_computation.14 | async-start | bytes 28311552 | tf_op jit(solution)/shard_map/psum | solution.py:383
  263.0 19.4 %all-to-all-start.4 = ((bf16[8,128,512]{2,1,0:T(8,128)(2,1)}), bf16[8,128,512]{2,1,0:T(8,128)(2,1)S(1)}, u32[]{:S(2)}, u32[]{:S(2)}) async-start(bf16[8,128,512]{2,1,0:T(8,128)(2,1)} %get-tuple-element.46), calls=%async_computation.4 | async-start | bytes 2097152 | tf_op jit(solution)/shard_map/all_to_all | solution.py:404
  284.5 42.0 %all-to-all-start.5 = ((bf16[8,128,1536]{2,1,0:T(8,128)(2,1)}), bf16[8,128,1536]{2,1,0:T(8,128)(2,1)S(1)}, u32[]{:S(2)}, u32[]{:S(2)}) async-start(bf16[8,128,1536]{2,1,0:T(8,128)(2,1)} %broadcast_in_dim.50), calls=%async_computation.5 | async-start | bytes 6291456 | tf_op jit(solution)/shard_map/all_to_all | solution.py:411
  387.3 48.3 %all-to-all-start.2 = ((bf16[8,128,1536]{2,1,0:T(8,128)(2,1)}), bf16[8,128,1536]{2,1,0:T(8,128)(2,1)}, u32[]{:S(2)}, u32[]{:S(2)}) async-start(bf16[8,128,1536]{2,1,0:T(8,128)(2,1)} %bitcast.46), calls=%async_computation.2 | async-start | bytes 6291456 | tf_op jit(solution)/shard_map/all_to_all | solution.py:438
  454.1 42.1 %all-to-all-start.6 = ((bf16[8,128,1536]{2,1,0:T(8,128)(2,1)}), bf16[8,128,1536]{2,1,0:T(8,128)(2,1)S(1)}, u32[]{:S(2)}, u32[]{:S(2)}) async-start(bf16[8,128,1536]{2,1,0:T(8,128)(2,1)} %bitcast.47), calls=%async_computation.6 | async-start | bytes 6291456 | tf_op jit(solution)/shard_map/all_to_all | solution.py:423
  458.6 4.9 slice-start
  496.2 20.7 %copy-start.3 = (bf16[8,128,1536]{2,1,0:T(8,128)(2,1)}, bf16[8,128,1536]{2,1,0:T(8,128)(2,1)S(1)}, u32[]{:S(2)}) copy-start(bf16[8,128,1536]{2,1,0:T(8,128)(2,1)S(1)} %all-to-all-done.6.part_ref) | copy-start | bytes 9437188
  496.8 26.0 %all-to-all-start.9 = ((f32[16,8,128]{2,1,0:T(8,128)}), f32[16,8,128]{2,1,0:T(8,128)}, u32[]{:S(2)}, u32[]{:S(2)}) async-start(f32[16,8,128]{2,1,0:T(8,128)} %broadcast_in_dim.53), calls=%async_computation.9 | async-start | bytes 131072 | tf_op jit(solution)/shard_map/all_to_all | solution.py:433
  525.2 7.6 %copy-start.6 = (bf16[3,1536,512]{2,1,0:T(8,128)(2,1)S(1)}, bf16[3,1536,512]{2,1,0:T(8,128)(2,1)}, u32[]{:S(2)}) copy-start(bf16[3,1536,512]{2,1,0:T(8,128)(2,1)} %get-tuple-element.105) | copy-start | bytes 14155780
  525.2 12.7 %slice-start.1 = ((s8[4718592]{0:T(1024)(128)(4,1)}), s8[4194304]{0:T(1024)(128)(4,1)S(1)}, s32[]{:S(2)}) async-start(s8[4718592]{0:T(1024)(128)(4,1)} %bitcast.38), calls=%async_computation.16 | async-start | bytes 8388608
  532.7 5.1 slice-start.2
  537.8 5.1 copy-start.1
  (6 other events, 10.8 us)
Sparse Core Ops, SparseCore 0:
  9.7 31.5 all-gather.4
  43.6 53.3 all-gather.6
  99.2 33.0 all-gather.10
  134.5 28.7 all-gather.8
  217.1 213.4 all-reduce.3

commit v2 on v1

v2 whole, which is shorter than its diff:
```python
import functools
import math

import jax
import jax.numpy as jnp
from jax import lax
from jax.experimental import pallas as pl
from jax.experimental.pallas import tpu as pltpu
from jax.sharding import PartitionSpec as P

QH = 24
KVH = 8
HD = 64
TOP = 8
EXP_DEV = 3
CAP = 56
D = 1536
FFE = 512
ROWS = 128
OWN = 8
GROUP = 1024
DP = 16
EXPERTS = 24
HEADS = 3
QW = HEADS * HD
PAIR = 2 * CAP
PAIRS = OWN // 2
SLOTS = OWN * CAP
BLK = 256
WW = 384
XW = D + 128
PW = 2 * D + 128
HALF = D // 2
EPS = 1e-06
THETA = 10000.0
VMEM = 60 * 1024 * 1024
f32 = jnp.float32
bf16 = jnp.bfloat16

NN = (((1,), (0,)), ((), ()))
NT = (((1,), (1,)), ((), ()))
TN = (((0,), (0,)), ((), ()))


def mm(a, b, dims=NN):
    return lax.dot_general(a, b, dims, preferred_element_type=f32)


def iota(shape, dim):
    return lax.broadcasted_iota(jnp.int32, shape, dim)


def swap_halves(v):
    lane = iota(v.shape, 1) % HD
    width = v.shape[1]
    ahead = pltpu.roll(v, width - HD // 2, 1)
    behind = pltpu.roll(v, HD // 2, 1)
    return jnp.where(lane < HD // 2, ahead, behind)


def block_mask(start_ref, at, keys):
    place = at + iota((BLK, keys), 0)
    key = iota((BLK, keys), 1)
    first = start_ref[pl.ds(at, BLK), :]
    return (key <= place) & (key >= first)


def prep_kernel(
    own_ref, wq_ref, wk_ref, wv_ref, wr_ref, wo_ref, x_ref, dy_ref, routes_ref, shard_ref, half_ref, rows_ref, own_cols
):
    own = own_ref[0]
    rows_ref[:, 0:D] = x_ref[...]
    rows_ref[:, D : 2 * D] = dy_ref[...]
    rows_ref[:, 2 * D : PW] = jnp.zeros((ROWS, PW - 2 * D), bf16)
    rows_ref[:, 2 * D : 2 * D + TOP] = routes_ref[...].astype(f32).astype(bf16)
    own_cols[...] = jnp.zeros_like(own_cols)
    for j in range(OWN):

        @pl.when(own == j)
        def _(j=j):
            own_cols[:, 0:QW] = wq_ref[:, j * QW : (j + 1) * QW]
            own_cols[:, QW:BLK] = wk_ref[:, j * HD : (j + 1) * HD]
            own_cols[:, BLK : BLK + HD] = wv_ref[:, j * HD : (j + 1) * HD]

    own_cols[:, BLK + HD : BLK + HD + EXPERTS] = wr_ref[...]
    shard_ref[...] = jnp.broadcast_to(own_cols[...][None], shard_ref.shape)
    half_ref[...] = jnp.where(own % 2 == 0, wo_ref[:, 0:HALF], wo_ref[:, HALF:D])


def gate_kernel(in_ref, after_ref, out_ref):
    pass


def owner_of(own, dz, dc):
    return ((own // 2 + dz) % 4) * 2 + (own + dc) % 2


def pieces_of(refs):
    near, up, down, far_a, far_b = range(5)
    for dc in range(2):
        mine = refs[dc * 5 : dc * 5 + 5]
        yield 0, dc, lambda mine=mine: mine[near][...]
        yield 1, dc, lambda mine=mine: mine[down][...]
        yield 3, dc, lambda mine=mine: mine[up][...]
        yield 2, dc, lambda mine=mine: jnp.concatenate([mine[far_a][...], mine[far_b][...]], axis=0)


def attend_kernel(own_ref, *refs):
    x_refs, refs = refs[:10], refs[10:]
    w_ref, gain_ref, cos_ref, sin_ref, start_ref, normed_ref, qkv_ref, mix_ref, log_ref = refs
    own = own_ref[0]
    for dz, dc, load in pieces_of(x_refs):
        rows = pl.ds(pl.multiple_of(owner_of(own, dz, dc) * ROWS, ROWS), ROWS)
        x = load().astype(f32)
        scale = lax.rsqrt(jnp.mean(x * x, axis=-1, keepdims=True) + EPS)
        normed = (x * scale * gain_ref[...]).astype(bf16)
        normed_ref[rows, :] = normed
        raw = mm(normed, w_ref[...])
        turned = raw[:, :BLK]
        turned = turned * cos_ref[rows, :] + swap_halves(turned) * sin_ref[rows, :]
        qkv_ref[rows, 0:BLK] = turned.astype(bf16)
        qkv_ref[rows, BLK:WW] = raw[:, BLK:WW].astype(bf16)
    for at in range(0, GROUP, BLK):
        rows = pl.ds(at, BLK)
        keys = at + BLK
        seen = block_mask(start_ref, at, keys)
        k_h = qkv_ref[0:keys, QW : QW + HD]
        v_h = qkv_ref[0:keys, BLK : BLK + HD]
        outs = []
        for r in range(HEADS):
            q_h = qkv_ref[rows, r * HD : (r + 1) * HD] * jnp.asarray(HD**-0.5, bf16)
            scores = jnp.where(seen, mm(q_h, k_h, NT), -1e30)
            top = jnp.max(scores, axis=-1, keepdims=True)
            terms = jnp.exp(scores - top)
            total = jnp.sum(terms, axis=-1, keepdims=True)
            prob = (terms / total).astype(bf16)
            outs.append(mm(prob, v_h))
            log_ref[rows, r : r + 1] = top + jnp.log(total)
        block = jnp.concatenate(outs + [jnp.zeros_like(outs[0])], axis=1).astype(bf16)
        mix_ref[at // ROWS] = block[0:ROWS]
        mix_ref[at // ROWS + 1] = block[ROWS:BLK]


def out_kernel(own_ref, mix_ref, mine_ref, other_ref, x_ref, gain_ref, hidden_ref, normed_ref, flat_ref):
    core = own_ref[0] % 2
    for j in range(OWN):
        flat_ref[:, j * QW : (j + 1) * QW] = mix_ref[j, :, 0:QW]
    flat = flat_ref[...]
    for at, wo_ref in ((core, mine_ref), (1 - core, other_ref)):
        cols = pl.ds(pl.multiple_of(at * HALF, 128), HALF)
        hidden_ref[:, cols] = x_ref[:, cols].astype(f32) + mm(flat, wo_ref[...])
    hidden = hidden_ref[...]
    scale = lax.rsqrt(jnp.mean(hidden * hidden, axis=-1, keepdims=True) + EPS)
    normed_ref[...] = (hidden * scale * gain_ref[...]).astype(bf16)


def router_probs(normed, w_ref):
    logits = mm(normed, w_ref[:, BLK:WW])
    lane = iota(logits.shape, 1)
    real = (lane >= HD) & (lane < HD + EXPERTS)
    logits = jnp.where(real, logits, -1e30)
    terms = jnp.exp(logits - jnp.max(logits, axis=-1, keepdims=True))
    terms = jnp.where(real, terms, 0.0)
    return terms / jnp.sum(terms, axis=-1, keepdims=True)


def pick_rows(slot_row, b):
    row = slot_row[:, b * BLK : (b + 1) * BLK]
    return iota((PAIR, BLK), 0) == row


def expert_kernel(own_ref, *refs):
    dy_refs, route_refs, refs = refs[:10], refs[10:20], refs[20:]
    n_ref, w_ref, wg_ref, wu_ref, wd_ref, gg_ref, gu_ref, gd_ref, hg_ref, hu_ref = refs[:10]
    gated_ref, p_ref, slot_ref, prob_ref, x_ref, d_ref, gate_ref, dy_ref, routes_ref = refs[10:]
    e = pl.program_id(0)
    own = own_ref[0] * EXP_DEV + e

    @pl.when(e == 0)
    def _():
        for at in range(0, GROUP, BLK):
            probs = router_probs(n_ref[at : at + BLK, :], w_ref)
            prob_ref[:, at : at + BLK] = jnp.transpose(probs)
        for dz, dc, load in pieces_of(dy_refs):
            rows = pl.ds(pl.multiple_of(owner_of(own_ref[0], dz, dc) * ROWS, ROWS), ROWS)
            dy_ref[rows, :] = load()
        for dz, dc, load in pieces_of(route_refs):
            rows = pl.ds(pl.multiple_of(owner_of(own_ref[0], dz, dc) * ROWS, ROWS), ROWS)
            routes_ref[:, rows] = jnp.transpose(load().astype(f32))[0:TOP]

    chosen = jnp.max((routes_ref[...] == own.astype(f32)).astype(f32), axis=0, keepdims=True)
    gate_row = jnp.sum(jnp.where(iota((128, GROUP), 0) == HD + own, prob_ref[...], 0.0), axis=0, keepdims=True)
    before = (iota((ROWS, ROWS), 0) < iota((ROWS, ROWS), 1)).astype(f32).astype(bf16)
    ranks = []
    for s in range(OWN):
        part = jnp.broadcast_to(chosen[:, s * ROWS : (s + 1) * ROWS], (8, ROWS)).astype(bf16)
        ranks.append(mm(part, before)[0:1] + float(CAP * (s % 2)))
    rank = jnp.concatenate(ranks, axis=1)
    slot_row = jnp.where(chosen > 0.0, rank, -1.0).astype(jnp.int32)
    slot_ref[0] = jnp.broadcast_to(slot_row, (8, GROUP))
    for b in range(PAIRS):
        pick = pick_rows(slot_row, b)
        pick_b = pick.astype(f32).astype(bf16)
        tokens = pl.ds(b * BLK, BLK)
        slots = pl.ds(b * PAIR, PAIR)
        x_ref[slots, :] = mm(pick_b, n_ref[tokens, :]).astype(bf16)
        d_ref[slots, :] = mm(pick_b, dy_ref[tokens, :]).astype(bf16)
        gate_ref[slots, :] = jnp.sum(jnp.where(pick, gate_row[:, b * BLK : (b + 1) * BLK], 0.0), axis=1, keepdims=True)
    x = x_ref[...]
    gate_in = mm(x, wg_ref[0])
    up_in = mm(x, wu_ref[0])
    sig = jax.nn.sigmoid(gate_in)
    silu = gate_in * sig
    inner = (silu * up_in).astype(bf16)
    out = mm(inner, wd_ref[0]).astype(bf16).astype(f32)
    gates = gate_ref[...]
    gated_ref[0] = (gates * out).astype(bf16)
    dy = d_ref[...].astype(f32)
    p = jnp.sum(dy * out, axis=-1, keepdims=True)
    high = p.astype(bf16).astype(f32)
    lane = iota((SLOTS, 128), 1)
    p_ref[0] = jnp.where(lane == HD + own, high, jnp.where(lane == HD + 32 + own, p - high, 0.0)).astype(bf16)
    slot_grad = (gates * dy).astype(bf16)
    inner_grad = mm(slot_grad, wd_ref[0], NT)
    gd_ref[0] = mm(inner, slot_grad, TN).astype(bf16)
    hg = (inner_grad * up_in * sig * (1.0 + gate_in * (1.0 - sig))).astype(bf16)
    hu = (inner_grad * silu).astype(bf16)
    hg_ref[0] = hg
    hu_ref[0] = hu
    gg_ref[0] = mm(x, hg, TN).astype(bf16)
    gu_ref[0] = mm(x, hu, TN).astype(bf16)


def split_core(core, both):
    first, second = both[0:ROWS], both[ROWS:BLK]
    return jnp.where(core == 0, first, second), jnp.where(core == 0, second, first)


def scatter_pairs(own, slot_ref, parts):
    for dz in range(PAIRS):
        b = (own // 2 + dz) % PAIRS
        tokens = pl.ds(pl.multiple_of(b * BLK, BLK), BLK)
        slots = pl.ds(pl.multiple_of(b * PAIR, PAIR), PAIR)
        pick = jnp.concatenate(
            [(iota((PAIR, BLK), 0) == slot_ref[k, 0:1, tokens]).astype(f32).astype(bf16) for k in range(EXP_DEV)],
            axis=0,
        )
        for ref, width, at, keep_ref, send_ref in parts:
            values = jnp.concatenate([ref[k, slots, :] for k in range(EXP_DEV)], axis=0)
            keep, send = split_core(own % 2, mm(pick, values, TN))
            keep_ref[dz, :, at : at + width] = keep.astype(bf16)
            send_ref[dz, :, at : at + width] = send.astype(bf16)


def return_kernel(own_ref, hg_ref, hu_ref, p_ref, slot_ref, wg_ref, wu_ref, keep_ref, send_ref, rows_ref):
    e = pl.program_id(0)
    rows_ref[e] = (mm(hg_ref[0], wg_ref[0], NT) + mm(hu_ref[0], wu_ref[0], NT)).astype(bf16)

    @pl.when(e == EXP_DEV - 1)
    def _():
        scatter_pairs(
            own_ref[0], slot_ref, ((rows_ref, D, 0, keep_ref, send_ref), (p_ref, 128, D, keep_ref, send_ref))
        )


def mixture_kernel(own_ref, gated_ref, slot_ref, keep_ref, send_ref):
    scatter_pairs(own_ref[0], slot_ref, ((gated_ref, D, 0, keep_ref, send_ref),))


def hidden_kernel(
    own_ref, part_a, part_b, part_c, dy_ref, hidden_ref, normed_ref, gain_ref, w_ref, mine_ref, other_ref,
    grad_ref, gain_grad_ref, send_ref, cols_ref,
):
    core = own_ref[0] % 2
    hidden = hidden_ref[...]
    scale = lax.rsqrt(jnp.mean(hidden * hidden, axis=-1, keepdims=True) + EPS)
    unit = hidden * scale
    total = part_a[0].astype(f32) + part_b[...].astype(f32) + part_c[...].astype(f32)
    tail = total[:, D:XW]
    probs = router_probs(normed_ref[...], w_ref)
    p = tail + pltpu.roll(tail, 128 - 32, 1)
    logit_grad = probs * (p - jnp.sum(p * probs, axis=-1, keepdims=True))
    high = logit_grad.astype(bf16)
    low = (logit_grad - high.astype(f32)).astype(bf16)
    router = w_ref[:, BLK:WW]
    normed_grad = total[:, 0:D] + mm(high, router, NT) + mm(low, router, NT)
    gain_grad_ref[...] = jnp.sum(normed_grad * unit, axis=0, keepdims=True)
    unit_grad = normed_grad * gain_ref[...]
    grad = dy_ref[...].astype(f32) + scale * (unit_grad - unit * jnp.mean(unit_grad * unit, axis=-1, keepdims=True))
    grad_ref[...] = grad
    mix_grad = jnp.zeros((ROWS, D), f32)
    for at, wo_ref in ((core, mine_ref), (1 - core, other_ref)):
        cols = pl.ds(pl.multiple_of(at * HALF, 128), HALF)
        mix_grad = mix_grad + mm(grad_ref[:, cols].astype(bf16), wo_ref[...], NT)
    for j in range(OWN):
        cols = slice(j * QW, (j + 1) * QW)
        send_ref[j, :, 0:QW] = mix_grad[:, cols].astype(bf16)
        send_ref[j, :, QW:BLK] = jnp.zeros((ROWS, BLK - QW), bf16)
        cols_ref[j, :, 0:HD] = jnp.zeros((ROWS, HD), bf16)
        cols_ref[j, :, HD:BLK] = grad[:, cols].astype(bf16)
        cols_ref[j, :, BLK:WW] = high


def attend_back_kernel(qkv_ref, log_ref, g_ref, cos_ref, sin_ref, start_ref, dqkv_ref, turn_ref, dk_ref, dv_ref):
    dk_ref[...] = jnp.zeros_like(dk_ref)
    dv_ref[...] = jnp.zeros_like(dv_ref)
    for at in range(0, GROUP, BLK):
        rows = pl.ds(at, BLK)
        keys = at + BLK
        seen = block_mask(start_ref, at, keys)
        k_h = qkv_ref[0:keys, QW : QW + HD]
        v_h = qkv_ref[0:keys, BLK : BLK + HD]
        for r in range(HEADS):
            q_h = qkv_ref[rows, r * HD : (r + 1) * HD] * jnp.asarray(HD**-0.5, bf16)
            g_h = g_ref[rows, r * HD : (r + 1) * HD]
            scores = jnp.where(seen, mm(q_h, k_h, NT), -1e30)
            prob = jnp.exp(scores - log_ref[rows, r : r + 1])
            dv_ref[0:keys, :] += mm(prob.astype(bf16), g_h, TN)
            prob_grad = mm(g_h, v_h, NT)
            delta = jnp.sum(prob_grad * prob, axis=-1, keepdims=True)
            score_grad = (prob * (prob_grad - delta)).astype(bf16)
            turn_ref[rows, r * HD : (r + 1) * HD] = mm(score_grad, k_h) * (HD**-0.5)
            dk_ref[0:keys, :] += mm(score_grad, q_h, TN)
    turn_ref[:, QW : QW + HD] = dk_ref[...]
    for at in range(0, GROUP, BLK):
        rows = pl.ds(at, BLK)
        turned = turn_ref[rows, :]
        turned = turned * cos_ref[rows, :] - swap_halves(turned) * sin_ref[rows, :]
        dqkv_ref[rows, 0:BLK] = turned.astype(bf16)
        dqkv_ref[rows, BLK : BLK + HD] = dv_ref[rows, :].astype(bf16)
        dqkv_ref[rows, BLK + HD : WW] = jnp.zeros((BLK, WW - BLK - HD), bf16)


def weight_kernel(
    own_ref, normed_ref, dqkv_ref, mix_ref, got_ref, n_ref, moe_gain_ref, norm_ref, w_ref,
    keep_ref, send_ref, pay_ref, gain_ref,
):
    own = own_ref[0]
    gain_ref[...] = jnp.zeros_like(gain_ref)
    for dz in range(PAIRS):
        b = (own // 2 + dz) % PAIRS
        rows = pl.ds(pl.multiple_of(b * BLK, BLK), BLK)
        back = mm(dqkv_ref[rows, :], w_ref[...], NT)
        gain_ref[0:1, :] += jnp.sum(back * normed_ref[rows, :].astype(f32), axis=0, keepdims=True)
        keep, send = split_core(own % 2, back)
        keep_ref[dz] = keep.astype(bf16)
        send_ref[dz] = send.astype(bf16)
    pay_ref[:, 0:BLK] = mm(normed_ref[...], dqkv_ref[:, 0:BLK], TN).astype(bf16)
    value = jnp.concatenate([dqkv_ref[:, BLK:WW], jnp.zeros((GROUP, 128), bf16)], axis=1)
    pay_ref[:, BLK : 2 * BLK] = (mm(normed_ref[...], value, TN) + mm(mix_ref[...], got_ref[:, 0:BLK], TN)).astype(bf16)
    router = mm(n_ref[...], got_ref[:, BLK:WW], TN)
    attn_gain = jnp.transpose(jnp.broadcast_to(gain_ref[0:1, :] / norm_ref[...], (128, D)))
    moe_gain = jnp.transpose(jnp.broadcast_to(moe_gain_ref[...], (128, D)))
    lane = iota((D, 128), 1)
    tail = jnp.where(lane == 0, attn_gain, jnp.where(lane == 1, moe_gain, jnp.where(lane >= HD, router, 0.0)))
    pay_ref[:, 2 * BLK : 2 * BLK + 128] = tail.astype(bf16)


def input_kernel(part_a, part_b, part_c, x_ref, gain_ref, hidden_grad_ref, out_ref):
    x = x_ref[...].astype(f32)
    scale = lax.rsqrt(jnp.mean(x * x, axis=-1, keepdims=True) + EPS)
    unit = x * scale
    total = part_a[0].astype(f32) + part_b[...].astype(f32) + part_c[...].astype(f32)
    unit_grad = total * gain_ref[...]
    out_ref[...] = (
        hidden_grad_ref[...] + scale * (unit_grad - unit * jnp.mean(unit_grad * unit, axis=-1, keepdims=True))
    ).astype(bf16)


def layer_kernel(part_a, part_b, part_c, hidden_ref, out_ref):
    total = part_a[0].astype(f32) + part_b[...].astype(f32) + part_c[...].astype(f32)
    out_ref[...] = (hidden_ref[...] + total).astype(bf16)


def sum_kernel(part_ref, sum_ref, router_ref):
    total = part_ref[0].astype(f32)
    for s in range(1, DP):
        total = total + part_ref[s].astype(f32)
    sum_ref[...] = jnp.broadcast_to(total.astype(bf16)[None], sum_ref.shape)
    router_ref[...] = total[:, 2 * BLK + HD : 2 * BLK + HD + EXPERTS]


def join_kernel(part_ref, q_ref, k_ref, v_ref, o_ref, gain_ref):
    gains = jnp.zeros((D // DP, 128), f32)
    for j in range(OWN):
        part = part_ref[j].astype(f32)
        q_ref[:, j * QW : (j + 1) * QW] = part[:, 0:QW]
        k_ref[:, j * HD : (j + 1) * HD] = part[:, QW:BLK]
        v_ref[:, j * HD : (j + 1) * HD] = part[:, BLK : BLK + HD]
        o_ref[:, j * QW : (j + 1) * QW] = part[:, BLK + HD : 2 * BLK]
        gains = gains + part[:, 2 * BLK : 2 * BLK + 128]
    gains = jnp.concatenate([gains, jnp.zeros((128 - D // DP, 128), f32)], axis=0)
    gain_ref[...] = jnp.broadcast_to(jnp.transpose(gains)[0:8][None], gain_ref.shape)


def sds(shape, dtype):
    return jax.ShapeDtypeStruct(shape, dtype)


def call(kernel, outs, scratch=(), cost=None, **grid):
    return pl.pallas_call(
        kernel,
        out_shape=outs,
        scratch_shapes=list(scratch),
        compiler_params=pltpu.CompilerParams(vmem_limit_bytes=VMEM),
        cost_estimate=cost,
        **grid,
    )


def cost(micros):
    return pl.CostEstimate(flops=int(micros * 1.15e9), bytes_accessed=1024, transcendentals=0)


VM = pl.BlockSpec(memory_space=pltpu.VMEM)
SM = pl.BlockSpec(memory_space=pltpu.SMEM)
ANY = pl.BlockSpec(memory_space=pl.ANY)


def along_z(step):
    return [(i, ((i // 2 + step) % 4) * 2 + i % 2) for i in range(OWN)]


UP, DOWN, SWAP = along_z(1), along_z(-1), [(i, i ^ 1) for i in range(OWN)]


def move(value, pairs):
    return lax.ppermute(value, "expert", pairs)


def gate(value, after):
    return pl.pallas_call(
        gate_kernel,
        out_shape=sds(value.shape, value.dtype),
        in_specs=[ANY, ANY],
        out_specs=ANY,
        input_output_aliases={0: 0},
        compiler_params=pltpu.CompilerParams(vmem_limit_bytes=VMEM),
        cost_estimate=cost(0.5),
    )(value, after)


def gather_rows(value):
    half = value.shape[0] // 2
    up, down = move(value, UP), move(value, DOWN)
    far_a, far_b = move(up[:half], UP), move(down[half:], DOWN)
    mine = [value, up, down, far_a, far_b]
    return mine + [move(piece, SWAP) for piece in mine]


def add(left, right):
    return (left.astype(f32) + right.astype(f32)).astype(bf16)


def scatter_rows(keep, send):
    half = ROWS // 2
    both = add(keep, move(send, SWAP))
    up, down = move(both[2, :half], UP), move(both[2, half:], DOWN)
    first = jnp.concatenate([add(both[1, :half], up), both[1, half:]], axis=0)
    last = jnp.concatenate([both[3, :half], add(both[3, half:], down)], axis=0)
    return both, move(first, UP), move(last, DOWN)


def body(
    tokens, norm_attn, query_weight, key_weight, value_weight, out_weight, norm_moe, router_weight,
    gate_weight, up_weight, down_weight, routes, seq_lengths, out_grad,
):
    own = lax.axis_index("expert").astype(jnp.int32).reshape(1)
    gain_one = norm_attn.reshape(1, D)
    gain_two = norm_moe.reshape(1, D)
    shard_rows = D // DP

    shard, half, rows = call(
        prep_kernel,
        [sds((DP, shard_rows, WW), bf16), sds((shard_rows, HALF), bf16), sds((ROWS, PW), bf16)],
        scratch=[pltpu.VMEM((shard_rows, WW), bf16)],
        cost=cost(3),
        in_specs=[SM] + [VM] * 8,
    )(own, query_weight, key_weight, value_weight, router_weight, out_weight, tokens, out_grad, routes)
    pieces = gather_rows(rows)
    weights = lax.all_to_all(shard, "dp", 0, 0, tiled=True).reshape(D, WW)
    out_mine = lax.all_gather(half, "dp", axis=0, tiled=True)

    end_one = seq_lengths[0, 0]
    end_two = end_one + seq_lengths[0, 1]
    place = jnp.arange(GROUP, dtype=jnp.int32)
    start = jnp.where(place >= end_two, end_two, jnp.where(place >= end_one, end_one, 0)).astype(jnp.int32)
    steps = jnp.arange(HD // 2, dtype=f32)
    freq = jnp.exp(steps * (-2.0 * math.log(THETA) / HD))
    angles = (place - start).astype(f32)[:, None] * freq[None, :]
    cos_half, sin_half = jnp.cos(angles), jnp.sin(angles)
    cos_t = jnp.tile(cos_half, (1, 8))
    sin_t = jnp.tile(jnp.concatenate([-sin_half, sin_half], axis=1), (1, 4))
    start = start.reshape(GROUP, 1)

    part = lambda piece, width, at: pl.BlockSpec(
        (piece.shape[0], width), lambda e: (0, at), pipeline_mode=pl.Buffered(1)
    )
    normed_one, qkv, mix, logs = call(
        attend_kernel,
        [sds((GROUP, D), bf16), sds((GROUP, WW), bf16), sds((OWN, ROWS, BLK), bf16), sds((GROUP, 8), f32)],
        cost=cost(12),
        grid=(1,),
        in_specs=[SM] + [part(p, D, 0) for p in pieces] + [VM] * 5,
    )(own, *pieces, weights, gain_one, cos_t, sin_t, start)
    out_mine = gate(out_mine, mix)
    out_other = move(out_mine, SWAP)

    mix_own = lax.all_to_all(mix, "expert", 0, 0, tiled=True)
    hidden, normed_two, mix_flat = call(
        out_kernel,
        [sds((ROWS, D), f32), sds((ROWS, D), bf16), sds((ROWS, D), bf16)],
        cost=cost(4),
        in_specs=[SM] + [VM] * 5,
    )(own, mix_own, out_mine, out_other, tokens, gain_two)
    n_all = lax.all_gather(normed_two, "expert", axis=0, tiled=True)
    mix_flat = gate(mix_flat, n_all)
    mix_all = lax.all_gather(mix_flat, "expert", axis=0, tiled=True)

    whole = lambda *shape: pl.BlockSpec(shape, lambda e: (0,) * len(shape), pipeline_mode=pl.Buffered(1))
    each = lambda *shape: pl.BlockSpec((1,) + shape, lambda e: (e, 0, 0))
    gg, gu, gd, hg, hu, gated, p_slots, slot_rows = call(
        expert_kernel,
        [
            sds((EXP_DEV, D, FFE), bf16), sds((EXP_DEV, D, FFE), bf16), sds((EXP_DEV, FFE, D), bf16),
            sds((EXP_DEV, SLOTS, FFE), bf16), sds((EXP_DEV, SLOTS, FFE), bf16), sds((EXP_DEV, SLOTS, D), bf16),
            sds((EXP_DEV, SLOTS, 128), bf16), sds((EXP_DEV, 8, GROUP), jnp.int32),
        ],
        scratch=[
            pltpu.VMEM((128, GROUP), f32), pltpu.VMEM((SLOTS, D), bf16), pltpu.VMEM((SLOTS, D), bf16),
            pltpu.VMEM((SLOTS, 1), f32), pltpu.VMEM((GROUP, D), bf16), pltpu.VMEM((TOP, GROUP), f32),
        ],
        cost=cost(28),
        grid=(EXP_DEV,),
        in_specs=[SM] + [part(p, D, 1) for p in pieces] + [part(p, 128, 2 * D // 128) for p in pieces] + [
            whole(GROUP, D), whole(D, WW), each(D, FFE), each(D, FFE), each(FFE, D),
        ],
        out_specs=[
            each(D, FFE), each(D, FFE), each(FFE, D), each(SLOTS, FFE), each(SLOTS, FFE), each(SLOTS, D),
            each(SLOTS, 128), each(8, GROUP),
        ],
    )(own, *pieces, *pieces, n_all, weights, gate_weight, up_weight, down_weight)

    down_total, gate_total, up_total = lax.psum((gd, gg, gu), "dp")

    dx_keep, dx_send = call(
        return_kernel,
        [sds((PAIRS, ROWS, XW), bf16)] * 2,
        scratch=[pltpu.VMEM((EXP_DEV, SLOTS, D), bf16)],
        cost=cost(1),
        grid=(EXP_DEV,),
        in_specs=[
            SM, each(SLOTS, FFE), each(SLOTS, FFE), whole(EXP_DEV, SLOTS, 128), whole(EXP_DEV, 8, GROUP),
            each(D, FFE), each(D, FFE),
        ],
        out_specs=[whole(PAIRS, ROWS, XW)] * 2,
    )(own, hg, hu, p_slots, slot_rows, gate_weight, up_weight)
    mix_keep, mix_send = call(
        mixture_kernel, [sds((PAIRS, ROWS, D), bf16)] * 2, cost=cost(5), in_specs=[SM, VM, VM]
    )(own, gated, slot_rows)

    first = pl.BlockSpec((1, ROWS, XW), lambda i: (0, 0, 0))
    first_d = pl.BlockSpec((1, ROWS, D), lambda i: (0, 0, 0))
    dx_parts = scatter_rows(dx_keep, dx_send)
    hidden_grad, moe_gain, send, cols = call(
        hidden_kernel,
        [sds((ROWS, D), f32), sds((1, D), f32), sds((OWN, ROWS, BLK), bf16), sds((OWN, ROWS, WW), bf16)],
        cost=cost(1),
        grid=(1,),
        in_specs=[SM, first] + [VM] * 9,
    )(own, *dx_parts, out_grad, hidden, normed_two, gain_two, weights, out_mine, out_other)
    mix_grad = lax.all_to_all(send, "expert", 0, 0, tiled=True).reshape(GROUP, BLK)
    got = lax.all_to_all(cols, "expert", 0, 0, tiled=True).reshape(GROUP, WW)
    dqkv = call(
        attend_back_kernel,
        sds((GROUP, WW), bf16),
        scratch=[pltpu.VMEM((GROUP, BLK), f32), pltpu.VMEM((GROUP, HD), f32), pltpu.VMEM((GROUP, HD), f32)],
        cost=cost(12),
    )(qkv, logs, mix_grad, cos_t, sin_t, start)
    back_keep, back_send, pay = call(
        weight_kernel,
        [sds((PAIRS, ROWS, D), bf16)] * 2 + [sds((D, 640), bf16)],
        scratch=[pltpu.VMEM((8, D), f32)],
        cost=cost(1),
        in_specs=[SM] + [VM] * 8,
    )(own, normed_one, dqkv, mix_all, got, n_all, moe_gain, gain_one, weights)

    pay_parts = lax.all_to_all(pay.reshape(DP, shard_rows, 640), "dp", 0, 0, tiled=True)
    pay_own, router_total = call(
        sum_kernel, [sds((OWN, shard_rows, 640), bf16), sds((shard_rows, EXPERTS), f32)], cost=cost(1)
    )(pay_parts)
    pay_all = lax.all_to_all(pay_own, "expert", 0, 0, tiled=True)
    query_total, key_total, value_total, out_total, gains = call(
        join_kernel,
        [sds((shard_rows, w), f32) for w in (D, KVH * HD, KVH * HD, D)] + [sds((DP, 8, 128), f32)],
        cost=cost(1),
    )(pay_all)
    gains = lax.all_to_all(gains, "dp", 0, 0, tiled=True)
    gain_attn = gains[:, 0, :shard_rows].reshape(D)
    gain_moe = gains[:, 1, :shard_rows].reshape(D)

    mix_parts = scatter_rows(mix_keep, mix_send)
    layer_out = call(
        layer_kernel, sds((ROWS, D), bf16), cost=cost(1), grid=(1,), in_specs=[first_d, VM, VM, VM]
    )(*mix_parts, hidden)
    back_parts = scatter_rows(back_keep, back_send)
    input_grad = call(
        input_kernel, sds((ROWS, D), bf16), cost=cost(1), grid=(1,), in_specs=[first_d] + [VM] * 5
    )(*back_parts, tokens, gain_one, hidden_grad)
    return (
        layer_out, input_grad, gain_attn, query_total, key_total, value_total, out_total, gain_moe, router_total,
        gate_total.astype(f32), up_total.astype(f32), down_total.astype(f32),
    )


def solution(mesh):
    both, dp, expert = P(("dp", "expert"), None), P("dp", None), P("expert", None, None)
    return jax.shard_map(
        body,
        mesh=mesh,
        in_specs=(both, P(), dp, dp, dp, dp, P(), dp, expert, expert, expert, both, dp, both),
        out_specs=(both, both, P(), dp, dp, dp, dp, P(), dp, expert, expert, expert),
        check_vma=False,
    )
```

time: 560 us -> 394 us (0.70)
  waiting for transfers between devices: 235 us -> 136 us
  blocking collectives: 64.6 us -> 0 us
  local copies, waits for them, and re-layouts: 55.4 us -> 20.9 us
  starting transfers between devices: 48.1 us -> 75.4 us
  Pallas kernels: 99.4 us -> 110 us
    all_to_all x8 -> x7, waiting for transfers between devices: 161 us -> 42.5 us  [the longest x1 19.8 us: body(): lax.all_to_all(pay.reshape(DP, shard_rows, 640), 'dp', 0, 0, tiled=True)]
    all_to_all x2 -> x0, blocking collectives: 64.6 us -> none  [the longest x1 46.2 us: body(): lax.all_to_all(pay, 'dp', 0, 0, tiled=True).reshape(DP, D // DP, 640)]
    all_gather x3 -> x2, waiting for transfers between devices: 57.9 us -> 0.01 us  [the longest x1 0.01 us: body(): mix_all = lax.all_gather(mix_flat, 'expert', axis=0, tiled=True)]
    ppermute x0 -> x25, waiting for transfers between devices: none -> 34 us  [move(): return lax.ppermute(value, 'expert', pairs)]
    psum x1, waiting for transfers between devices: 0.01 us -> 31 us  [body(): down_total, gate_total, up_total = lax.psum((gd, gg, gu), 'dp')]
    ppermute x0 -> x25, starting transfers between devices: none -> 29.3 us  [move(): return lax.ppermute(value, 'expert', pairs)]
    all_gather x1 -> x0, local copies, waits for them, and re-layouts: 15.8 us -> none  [body(): dy_all = lax.all_gather(dy_own, 'expert', axis=0, tiled=True)]
    all_gather x1, waiting for transfers between devices: 13.8 us -> 28.1 us  [body(): n_all = lax.all_gather(normed_two, 'expert', axis=0, tiled=True)]
  transfers between devices with their start and end apart: 13 -> 36, of which waited for: 11 -> 14; matrix products, arithmetic and copies ran while one was open for 12% -> 6% of each run, Pallas kernels for 10% -> 26%
where the time goes in v2:
time: 394 us; the launch traced here: 389 us
  waiting for transfers between devices  136 us (35%)
  Pallas kernels  110 us (28%)
  starting transfers between devices  75.4 us (19%)
  other arithmetic  31.1 us (8%)
  local copies, waits for them, and re-layouts  20.9 us (5%)
  between operations  15.7 us (4%)
    ppermute x25, waiting for transfers between devices, move(): return lax.ppermute(value, 'expert', pairs)  34 us
    psum x1, waiting for transfers between devices, body(): down_total, gate_total, up_total = lax.psum((gd, gg, gu), 'dp')  31 us
    pallas_call x1, Pallas kernels, body(): call(expert_kernel, [sds((EXP_DEV, D, FFE), bf16), sds((EXP_DEV, D, FFE),...  29.5 us
    ppermute x25, starting transfers between devices, move(): return lax.ppermute(value, 'expert', pairs)  29.3 us
    all_gather x1, waiting for transfers between devices, body(): n_all = lax.all_gather(normed_two, 'expert', axis=0, tiled=True)  28.1 us
    all_to_all x1, waiting for transfers between devices, body(): lax.all_to_all(pay.reshape(DP, shard_rows, 640), 'dp', 0, 0, tiled=True)  19.8 us
    pallas_call x1, Pallas kernels, body(): call(attend_back_kernel, sds((GROUP, WW), bf16), scratch=[pltpu.VMEM((GRO...  12.5 us
    pallas_call x1, Pallas kernels, body(): call(attend_kernel, [sds((GROUP, D), bf16), sds((GROUP, WW), bf16), sds((...  12.2 us
  transfers between devices with their start and end apart: 36, of which 14 were waited for; matrix products, arithmetic and copies ran while one was open for 6% of the time, Pallas kernels for 26%

profile of v2, /device:TPU:1, one launch (start us, length us, event | category | flops | bytes accessed | tf_op | source)
XLA Modules:
  0.0 389.1 jit_solution(9200548861492238301)
XLA Ops:
  17.7 6.9 %all-to-all-start = ((bf16[16,96,384]{2,1,0:T(8,128)(2,1)}), bf16[16,96,384]{2,1,0:T(8,128)(2,1)S(1)}, u32[]{:S(2)}, u32[]{:S(2)}) async-start(bf16[16,96,384]{2,1,0:T(8,128)(2,1)} %get-tuple-element.49), calls=%async_computation | async-start | bytes 2359296 | tf_op jit(solution)/shard_map/all_to_all | solution.py:481
  24.6 11.2 %collective-permute-done.refs_1_.refs_11_ = bf16[128,3200]{1,0:T(8,128)(2,1)S(1)} collective-permute-done((bf16[128,3200]{1,0:T(8,128)(2,1)}, bf16[128,3200]{1,0:T(8,128)(2,1)S(1)}, u32[]{:S(2)}, u32[]{:S(2)}) %collective-permute-start) | collective-permute-done | bytes 819232 | tf_op jit(solution)/shard_map/ppermute | solution.py:428
  55.6 12.2 %shard_map.230 = (bf16[1024,1536]{1,0:T(8,128)(2,1)}, bf16[1024,384]{1,0:T(8,128)(2,1)}, bf16[8,128,256]{2,1,0:T(8,128)(2,1)}, f32[1024,8]{1,0:T(8,128)}) custom-call(s32[1]{0:T(128)} %bitcast.own_ref, bf16[128,3200]{1,0:T(8,128)(2,1)} %get-tuple-element.48.refs_0_.refs_10_, bf16[128,3200]{1,0:T(8,128)(2,1)} %copy-done.18, ...), custom_call_target="tpu_custom_call" | custom-call | flops 13799999488 | bytes 1024 | tf_op jit(solution)/shard_map/pallas_call | solution.py:499
  74.4 8.9 %all-to-all-done.1.mix_ref = bf16[8,128,256]{2,1,0:T(8,128)(2,1)S(1)} async-done(((bf16[8,128,256]{2,1,0:T(8,128)(2,1)}), bf16[8,128,256]{2,1,0:T(8,128)(2,1)S(1)}, u32[]{:S(2)}, u32[]{:S(2)}) %all-to-all-start.1) | async-done | bytes 524320 | tf_op jit(solution)/shard_map/all_to_all | solution.py:509
  85.5 4.7 %shard_map.232 = (f32[128,1536]{1,0:T(8,128)}, bf16[128,1536]{1,0:T(8,128)(2,1)}, bf16[128,1536]{1,0:T(8,128)(2,1)}) custom-call(s32[1]{0:T(128)} %bitcast.own_ref, bf16[8,128,256]{2,1,0:T(8,128)(2,1)} %copy-done.15, bf16[1536,768]{1,0:T(8,128)(2,1)} %shard_map.231.mine_ref, bf16[1536,768]{1,0:T(8,128)(2,1)} %copy-done.6, bf16[128,1536]{1,0:T(8,128)(2,1)} %x_ref.5, ...), custom_call_target="tpu_custom_call" | custom-call | flops 4600000000 | bytes 1024 | tf_op jit(solution)/shard_map/pallas_call | solution.py:510
  90.3 28.1 %all-gather.6.cloned.1.call-done.refs_20_.after_ref.n_ref = bf16[1024,1536]{1,0:T(8,128)(2,1)} async-done(((bf16[128,1536]{1,0:T(8,128)(2,1)}), bf16[1024,1536]{1,0:T(8,128)(2,1)}) %all-gather.6.cloned.1.call-update) | async-done | bytes 3145744 | tf_op jit(solution)/shard_map/all_gather | solution.py:516
  118.8 29.5 %shard_map.233 = (bf16[3,1536,512]{2,1,0:T(8,128)(2,1)}, bf16[3,1536,512]{2,1,0:T(8,128)(2,1)}, bf16[3,512,1536]{2,1,0:T(8,128)(2,1)}, bf16[3,448,512]{2,1,0:T(8...) custom-call(s32[1]{0:T(128)} %bitcast.own_ref, ...), custom_call_target="tpu_custom_call" | custom-call | flops 32199999488 | bytes 1024 | tf_op jit(solution)/shard_map/pallas_call | solution.py:522
  148.4 11.6 %shard_map.236 = (bf16[4,128,1664]{2,1,0:T(8,128)(2,1)}, bf16[4,128,1664]{2,1,0:T(8,128)(2,1)}) custom-call(s32[1]{0:T(128)} %bitcast.own_ref, bf16[3,448,512]{2,1,0:T(8,128)(2,1)} %get-tuple-element.61.hg_ref, bf16[3,448,512]{2,1,0:T(8,128)(2,1)} %get-tuple-element.62.hu_ref, bf16[3,448,128]{2,1,0:T(8,128)(2,1)} %get-tuple-element.63.p_ref, ...), custom_call_target="tpu_custom_call" | custom-call | flops 1150000000 | bytes 1024 | tf_op jit(solution)/shard_map/pallas_call | solution.py:546
  167.3 5.2 %collective-permute-done.18 = bf16[64,1664]{1,0:T(8,128)(2,1)S(1)} collective-permute-done((bf16[64,1664]{1,0:T(8,128)(2,1)S(1)}, bf16[64,1664]{1,0:T(8,128)(2,1)S(1)}, u32[]{:S(2)}, u32[]{:S(2)}) %collective-permute-start.18) | collective-permute-done | bytes 213024 | tf_op jit(solution)/shard_map/ppermute | solution.py:428
  177.8 8.5 %collective-permute-done.17.part_b = bf16[128,1664]{1,0:T(8,128)(2,1)S(1)} collective-permute-done((bf16[128,1664]{1,0:T(8,128)(2,1)S(1)}, bf16[128,1664]{1,0:T(8,128)(2,1)S(1)}, u32[]{:S(2)}, u32[]{:S(2)}) %collective-permute-start.17) | collective-permute-done | bytes 426016 | tf_op jit(solution)/shard_map/ppermute | solution.py:428
  187.2 8.0 %shard_map.237 = (f32[128,1536]{1,0:T(8,128)}, f32[1,1536]{1,0:T(1,128)}, bf16[8,128,256]{2,1,0:T(8,128)(2,1)}, bf16[8,128,384]{2,1,0:T(8,128)(2,1)}) custom-call(s32[1]{0:T(128)} %bitcast.own_ref, bf16[4,128,1664]{2,1,0:T(8,128)(2,1)} %copy-done, bf16[128,1664]{1,0:T(8,128)(2,1)} %copy-done.16, bf16[128,1664]{1,0:T(8,128)(2,1)} %copy-done.17, ...), custom_call_target="tpu_custom_call" | custom-call | flops 1150000000 | bytes 1024 | tf_op jit(solution)/shard_map/pallas_call | solution.py:565
  195.2 6.7 %all-to-all-start.2 = ((bf16[8,128,256]{2,1,0:T(8,128)(2,1)}), bf16[8,128,256]{2,1,0:T(8,128)(2,1)S(1)}, u32[]{:S(2)}, u32[]{:S(2)}) async-start(bf16[8,128,256]{2,1,0:T(8,128)(2,1)} %get-tuple-element.66), calls=%async_computation.2 | async-start | bytes 1048576 | tf_op jit(solution)/shard_map/all_to_all | solution.py:572
  201.8 5.7 %shard_map.234 = (bf16[4,128,1536]{2,1,0:T(8,128)(2,1)}, bf16[4,128,1536]{2,1,0:T(8,128)(2,1)}) custom-call(s32[1]{0:T(128)} %bitcast.own_ref, bf16[3,448,1536]{2,1,0:T(8,128)(2,1)} %get-tuple-element.53.gated_ref, s32[3,8,1024]{2,1,0:T(8,128)} %get-tuple-element.54.slot_ref), custom_call_target="tpu_custom_call" | custom-call | flops 5750000128 | bytes 1024 | tf_op jit(solution)/shard_map/pallas_call | solution.py:558
  215.8 12.5 %shard_map.238.dqkv_ref = bf16[1024,384]{1,0:T(8,128)(2,1)} custom-call(bf16[1024,384]{1,0:T(8,128)(2,1)} %get-tuple-element.59.qkv_ref, f32[1024,8]{1,0:T(8,128)} %get-tuple-element.60.log_ref, bf16[1024,256]{1,0:T(8,128)(2,1)} %bitcast.72, f32[1024,256]{1,0:T(8,128)} %copy.33.refs_12_.cos_ref, f32[1024,256]{1,0:T(8,128)} %copy.34.refs_13_.sin_ref, ...), custom_call_target="tpu_custom_call" | custom-call | flops 13799999488 | bytes 1024 | tf_op jit(solution)/shard_map/pallas_call | solution.py:574
  229.2 12.2 %shard_map.240 = (bf16[4,128,1536]{2,1,0:T(8,128)(2,1)}, bf16[4,128,1536]{2,1,0:T(8,128)(2,1)}, bf16[1536,640]{1,0:T(8,128)(2,1)}) custom-call(s32[1]{0:T(128)} %bitcast.own_ref, bf16[1024,1536]{1,0:T(8,128)(2,1)} %get-tuple-element.58.normed_ref, bf16[1024,384]{1,0:T(8,128)(2,1)} %shard_map.238.dqkv_ref, ...), custom_call_target="tpu_custom_call" | custom-call | flops 1150000000 | bytes 1024 | tf_op jit(solution)/shard_map/pallas_call | solution.py:580
  247.1 6.2 %all-to-all-start.4 = ((bf16[16,96,640]{2,1,0:T(8,128)(2,1)}), bf16[16,96,640]{2,1,0:T(8,128)(2,1)S(1)}, u32[]{:S(2)}, u32[]{:S(2)}) async-start(bf16[16,96,640]{2,1,0:T(8,128)(2,1)} %bitcast.26), calls=%async_computation.4 | async-start | bytes 3932160 | tf_op jit(solution)/shard_map/all_to_all | solution.py:588
  266.5 19.8 %all-to-all-done.4.part_ref = bf16[16,96,640]{2,1,0:T(8,128)(2,1)S(1)} async-done(((bf16[16,96,640]{2,1,0:T(8,128)(2,1)}), bf16[16,96,640]{2,1,0:T(8,128)(2,1)S(1)}, u32[]{:S(2)}, u32[]{:S(2)}) %all-to-all-start.4) | async-done | bytes 1966112 | tf_op jit(solution)/shard_map/all_to_all | solution.py:588
  290.4 9.7 %all-to-all-start.5 = ((bf16[8,96,640]{2,1,0:T(8,128)(2,1)}), bf16[8,96,640]{2,1,0:T(8,128)(2,1)S(1)}, u32[]{:S(2)}, u32[]{:S(2)}) async-start(bf16[8,96,640]{2,1,0:T(8,128)(2,1)} %get-tuple-element.74), calls=%async_computation.5 | async-start | bytes 1966080 | tf_op jit(solution)/shard_map/all_to_all | solution.py:592
  307.5 7.0 %all-to-all-done.5.part_ref = bf16[8,96,640]{2,1,0:T(8,128)(2,1)S(1)} async-done(((bf16[8,96,640]{2,1,0:T(8,128)(2,1)}), bf16[8,96,640]{2,1,0:T(8,128)(2,1)S(1)}, u32[]{:S(2)}, u32[]{:S(2)}) %all-to-all-start.5) | async-done | bytes 983072 | tf_op jit(solution)/shard_map/all_to_all | solution.py:592
  318.1 7.2 %all-to-all-start.6 = ((f32[16,8,128]{2,1,0:T(8,128)}), f32[16,8,128]{2,1,0:T(8,128)S(1)}, u32[]{:S(2)}, u32[]{:S(2)}) async-start(f32[16,8,128]{2,1,0:T(8,128)} %get-tuple-element.75), calls=%async_computation.6 | async-start | bytes 131072 | tf_op jit(solution)/shard_map/all_to_all | solution.py:598
  333.6 31.0 %all-reduce.3.cloned.1.call-done = (bf16[3,1536,512]{2,1,0:T(8,128)(2,1)}, bf16[3,1536,512]{2,1,0:T(8,128)(2,1)}, bf16[3,512,1536]{2,1,0:T(8,128)(2,1)}) async-done(((bf16[3,1536,512]{2,1,0:T(8,128)(2,1)}, bf16[3,1536,512]{2,1,0:T(8,128)(2,1)}, bf16[3,512,1536]{2,1,0:T(8,128)(2,1)}), (bf16[3,1536,512]{2,1,0:T(8,128)(2,1)}, bf16[3,1536,512]{2,1,0:T(8,128)(2,1)}, ...) | async-done | bytes 14155792 | tf_op jit(solution)/shard_map/psum | solution.py:544
  364.6 7.6 %convert_element_type.149 = f32[3,1536,512]{2,1,0:T(8,128)} convert(bf16[3,1536,512]{2,1,0:T(8,128)(2,1)} %get-tuple-element.110) | non-fusion elementwise | flops 2359296 | bytes 14155776 | tf_op jit(solution)/shard_map/convert_element_type | solution.py:612
  372.2 5.1 %convert_element_type.150 = f32[3,1536,512]{2,1,0:T(8,128)} convert(bf16[3,1536,512]{2,1,0:T(8,128)(2,1)S(1)} %copy-done.4) | non-fusion elementwise | flops 2359296 | bytes 14155776 | tf_op jit(solution)/shard_map/convert_element_type | solution.py:612
  377.3 5.1 %convert_element_type.151 = f32[3,512,1536]{2,1,0:T(8,128)} convert(bf16[3,512,1536]{2,1,0:T(8,128)(2,1)S(1)} %bitcast.68) | non-fusion elementwise | flops 2359296 | bytes 14155776 | tf_op jit(solution)/shard_map/convert_element_type | solution.py:612
  (160 shorter events, 102.9 us)
Async XLA Ops:
  7.2 60.7 %all-gather.4.cloned.1.call-start = ((), (), s32[]{:S(2)}) async-start(), calls=%async_computation.7 | async-start | bytes 2506752 | tf_op jit(solution)/shard_map/all_gather | solution.py:482
  13.0 22.9 %collective-permute-start = (bf16[128,3200]{1,0:T(8,128)(2,1)}, bf16[128,3200]{1,0:T(8,128)(2,1)S(1)}, u32[]{:S(2)}, u32[]{:S(2)}) collective-permute-start(bf16[128,3200]{1,0:T(8,128)(2,1)} %get-tuple-element.48.refs_0_.refs_10_), channel_id=1, source_target_pairs={{0,2},{1,3},{2,4},{3,5},{4,6},{5,7},{6,0},{7,1},{8,10},{9,11},{10,... | collective-permute-start | bytes 2457608 | tf_op jit(solution)/shard_map/ppermute | solution.py:428
  15.5 20.4 %collective-permute-start.1 = (bf16[128,3200]{1,0:T(8,128)(2,1)}, bf16[128,3200]{1,0:T(8,128)(2,1)}, u32[]{:S(2)}, u32[]{:S(2)}) collective-permute-start(bf16[128,3200]{1,0:T(8,128)(2,1)} %get-tuple-element.48.refs_0_.refs_10_), channel_id=1, source_target_pairs={{0,6},{1,7},{2,0},{3,1},{4,2},{5,3},{6,4},{7,5},{8,14},{9,15},{10,... | collective-permute-start | bytes 2457608 | tf_op jit(solution)/shard_map/ppermute | solution.py:428
  17.7 36.9 %all-to-all-start = ((bf16[16,96,384]{2,1,0:T(8,128)(2,1)}), bf16[16,96,384]{2,1,0:T(8,128)(2,1)S(1)}, u32[]{:S(2)}, u32[]{:S(2)}) async-start(bf16[16,96,384]{2,1,0:T(8,128)(2,1)} %get-tuple-element.49), calls=%async_computation | async-start | bytes 2359296 | tf_op jit(solution)/shard_map/all_to_all | solution.py:481
  39.7 14.9 %collective-permute-start.4 = (bf16[128,3200]{1,0:T(8,128)(2,1)}, bf16[128,3200]{1,0:T(8,128)(2,1)}, u32[]{:S(2)}, u32[]{:S(2)}) collective-permute-start(bf16[128,3200]{1,0:T(8,128)(2,1)} %get-tuple-element.48.refs_0_.refs_10_), channel_id=1, source_target_pairs={{0,1},{1,0},{2,3},{3,2},{4,5},{5,4},{6,7},{7,6},{8,9},{9,8},{10,11... | collective-permute-start | bytes 2457608 | tf_op jit(solution)/shard_map/ppermute | solution.py:428
  41.5 13.1 %collective-permute-start.6 = (bf16[128,3200]{1,0:T(8,128)(2,1)}, bf16[128,3200]{1,0:T(8,128)(2,1)}, u32[]{:S(2)}, u32[]{:S(2)}) collective-permute-start(bf16[128,3200]{1,0:T(8,128)(2,1)} %collective-permute-done.1.refs_2_.refs_12_), channel_id=1, source_target_pairs={{0,1},{1,0},{2,3},{3,2},{4,5},{5,4},{6,7},{7,6},{8,9},{9,8},{10,11... | collective-permute-start | bytes 2457608 | tf_op jit(solution)/shard_map/ppermute | solution.py:428
  67.9 15.4 %collective-permute-start.9 = (bf16[1536,768]{1,0:T(8,128)(2,1)}, bf16[1536,768]{1,0:T(8,128)(2,1)S(1)}, u32[]{:S(2)}, u32[]{:S(2)}) collective-permute-start(bf16[1536,768]{1,0:T(8,128)(2,1)} %shard_map.231.mine_ref), channel_id=1, source_target_pairs={{0,1},{1,0},{2,3},{3,2},{4,5},{5,4},{6,7},{7,6},{8,9},{9,8},{10,11... | collective-permute-start | bytes 7077896 | tf_op jit(solution)/shard_map/ppermute | solution.py:428
  69.3 13.9 %all-to-all-start.1 = ((bf16[8,128,256]{2,1,0:T(8,128)(2,1)}), bf16[8,128,256]{2,1,0:T(8,128)(2,1)S(1)}, u32[]{:S(2)}, u32[]{:S(2)}) async-start(bf16[8,128,256]{2,1,0:T(8,128)(2,1)} %get-tuple-element.50.after_ref), calls=%async_computation.1 | async-start | bytes 1048576 | tf_op jit(solution)/shard_map/all_to_all | solution.py:509
  73.8 44.6 %all-gather.6.cloned.1.call-start = ((), (), s32[]{:S(2)}) async-start(), calls=%async_computation.8 | async-start | bytes 3538944 | tf_op jit(solution)/shard_map/all_gather | solution.py:516
  90.2 138.1 %all-gather.8.cloned.1.call-start = ((), (), s32[]{:S(2)}) async-start(), calls=%async_computation.9 | async-start | bytes 3538944 | tf_op jit(solution)/shard_map/all_gather | solution.py:518
  118.4 246.2 %all-reduce.3.cloned.1.call-start = ((), (), s32[]{:S(2)}) async-start(), calls=%async_computation.10 | async-start | bytes 28311552 | tf_op jit(solution)/shard_map/psum | solution.py:544
  195.2 16.1 %all-to-all-start.2 = ((bf16[8,128,256]{2,1,0:T(8,128)(2,1)}), bf16[8,128,256]{2,1,0:T(8,128)(2,1)S(1)}, u32[]{:S(2)}, u32[]{:S(2)}) async-start(bf16[8,128,256]{2,1,0:T(8,128)(2,1)} %get-tuple-element.66), calls=%async_computation.2 | async-start | bytes 1048576 | tf_op jit(solution)/shard_map/all_to_all | solution.py:572
  207.6 34.3 %collective-permute-start.10 = (bf16[4,128,1536]{2,1,0:T(8,128)(2,1)}, bf16[4,128,1536]{2,1,0:T(8,128)(2,1)}, u32[]{:S(2)}, u32[]{:S(2)}) collective-permute-start(bf16[4,128,1536]{2,1,0:T(8,128)(2,1)} %get-tuple-element.56), channel_id=1, source_target_pairs={{0,1},{1,0},{2,3},{3,2},{4,5},{5,4},{6,7},{7,6},{8,9},{9,8},{10,11... | collective-permute-start | bytes 4718600 | tf_op jit(solution)/shard_map/ppermute | solution.py:428
  211.3 17.0 %all-to-all-start.3 = ((bf16[8,128,384]{2,1,0:T(8,128)(2,1)}), bf16[8,128,384]{2,1,0:T(8,128)(2,1)S(1)}, u32[]{:S(2)}, u32[]{:S(2)}) async-start(bf16[8,128,384]{2,1,0:T(8,128)(2,1)} %get-tuple-element.68), calls=%async_computation.3 | async-start | bytes 1572864 | tf_op jit(solution)/shard_map/all_to_all | solution.py:573
  241.4 16.1 %collective-permute-start.20 = (bf16[4,128,1536]{2,1,0:T(8,128)(2,1)}, bf16[4,128,1536]{2,1,0:T(8,128)(2,1)}, u32[]{:S(2)}, u32[]{:S(2)}) collective-permute-start(bf16[4,128,1536]{2,1,0:T(8,128)(2,1)} %get-tuple-element.71), channel_id=1, source_target_pairs={{0,1},{1,0},{2,3},{3,2},{4,5},{5,4},{6,7},{7,6},{8,9},{9,8},{10,11... | collective-permute-start | bytes 4718600 | tf_op jit(solution)/shard_map/ppermute | solution.py:428
  247.1 39.1 %all-to-all-start.4 = ((bf16[16,96,640]{2,1,0:T(8,128)(2,1)}), bf16[16,96,640]{2,1,0:T(8,128)(2,1)S(1)}, u32[]{:S(2)}, u32[]{:S(2)}) async-start(bf16[16,96,640]{2,1,0:T(8,128)(2,1)} %bitcast.26), calls=%async_computation.4 | async-start | bytes 3932160 | tf_op jit(solution)/shard_map/all_to_all | solution.py:588
  257.5 46.6 %collective-permute-start.12 = (bf16[128,1536]{1,0:T(8,128)(2,1)}, bf16[128,1536]{1,0:T(8,128)(2,1)}, u32[]{:S(2)}, u32[]{:S(2)}) collective-permute-start(bf16[128,1536]{1,0:T(8,128)(2,1)} %pad_maximum_fusion.2), channel_id=1, source_target_pairs={{0,2},{1,3},{2,4},{3,5},{4,6},{5,7},{6,0},{7,1},{8,10},{9,11},{10,... | collective-permute-start | bytes 1179656 | tf_op jit(solution)/shard_map/ppermute | solution.py:428
  260.4 39.7 %collective-permute-start.23 = (bf16[64,1536]{1,0:T(8,128)(2,1)}, bf16[64,1536]{1,0:T(8,128)(2,1)}, u32[]{:S(2)}, u32[]{:S(2)}) collective-permute-start(bf16[64,1536]{1,0:T(8,128)(2,1)} %get-tuple-element.120), channel_id=1, source_target_pairs={{0,6},{1,7},{2,0},{3,1},{4,2},{5,3},{6,4},{7,5},{8,14},{9,15},{10,... | collective-permute-start | bytes 589832 | tf_op jit(solution)/shard_map/ppermute | solution.py:428
  263.0 37.1 %collective-permute-start.21 = (bf16[64,1536]{1,0:T(8,128)(2,1)}, bf16[64,1536]{1,0:T(8,128)(2,1)}, u32[]{:S(2)}, u32[]{:S(2)}) collective-permute-start(bf16[64,1536]{1,0:T(8,128)(2,1)} %get-tuple-element.122), channel_id=1, source_target_pairs={{0,2},{1,3},{2,4},{3,5},{4,6},{5,7},{6,0},{7,1},{8,10},{9,11},{10,... | collective-permute-start | bytes 589832 | tf_op jit(solution)/shard_map/ppermute | solution.py:428
  263.8 40.4 %collective-permute-start.14 = (bf16[128,1536]{1,0:T(8,128)(2,1)}, bf16[128,1536]{1,0:T(8,128)(2,1)}, u32[]{:S(2)}, u32[]{:S(2)}) collective-permute-start(bf16[128,1536]{1,0:T(8,128)(2,1)} %pad_maximum_fusion.3), channel_id=1, source_target_pairs={{0,6},{1,7},{2,0},{3,1},{4,2},{5,3},{6,4},{7,5},{8,14},{9,15},{10,... | collective-permute-start | bytes 1179656 | tf_op jit(solution)/shard_map/ppermute | solution.py:428
  290.4 24.1 %all-to-all-start.5 = ((bf16[8,96,640]{2,1,0:T(8,128)(2,1)}), bf16[8,96,640]{2,1,0:T(8,128)(2,1)S(1)}, u32[]{:S(2)}, u32[]{:S(2)}) async-start(bf16[8,96,640]{2,1,0:T(8,128)(2,1)} %get-tuple-element.74), calls=%async_computation.5 | async-start | bytes 1966080 | tf_op jit(solution)/shard_map/all_to_all | solution.py:592
  301.3 24.0 %collective-permute-start.22 = (bf16[128,1536]{1,0:T(8,128)(2,1)S(1)}, bf16[128,1536]{1,0:T(8,128)(2,1)S(1)}, u32[]{:S(2)}, u32[]{:S(2)}) collective-permute-start(bf16[128,1536]{1,0:T(8,128)(2,1)S(1)} %pad_maximum_fusion.4), channel_id=1, source_target_pairs={{0,2},{1,3},{2,4},{3,5},{4,6},{5,7},{6,0},{7,1},{8,10},{9,11},{10,... | collective-permute-start | bytes 1179656 | tf_op jit(solution)/shard_map/ppermute | solution.py:428
  302.8 22.5 %collective-permute-start.24 = (bf16[128,1536]{1,0:T(8,128)(2,1)S(1)}, bf16[128,1536]{1,0:T(8,128)(2,1)S(1)}, u32[]{:S(2)}, u32[]{:S(2)}) collective-permute-start(bf16[128,1536]{1,0:T(8,128)(2,1)S(1)} %pad_maximum_fusion.5), channel_id=1, source_target_pairs={{0,6},{1,7},{2,0},{3,1},{4,2},{5,3},{6,4},{7,5},{8,14},{9,15},{10,... | collective-permute-start | bytes 1179656 | tf_op jit(solution)/shard_map/ppermute | solution.py:428
  318.1 14.1 %all-to-all-start.6 = ((f32[16,8,128]{2,1,0:T(8,128)}), f32[16,8,128]{2,1,0:T(8,128)S(1)}, u32[]{:S(2)}, u32[]{:S(2)}) async-start(f32[16,8,128]{2,1,0:T(8,128)} %get-tuple-element.75), calls=%async_computation.6 | async-start | bytes 131072 | tf_op jit(solution)/shard_map/all_to_all | solution.py:598
  (39 other events, 325.3 us)
Sparse Core Ops, SparseCore 0:
  13.1 54.4 all-gather.3
  90.3 27.9 all-gather.5
  120.6 27.8 all-gather.7
  153.1 211.4 all-reduce.2

commit v3 on v2

v3 whole, which is shorter than its diff:
```python
import functools
import math

import jax
import jax.numpy as jnp
from jax import lax
from jax.experimental import pallas as pl
from jax.experimental.pallas import tpu as pltpu
from jax.sharding import PartitionSpec as P

QH = 24
KVH = 8
HD = 64
TOP = 8
EXP_DEV = 3
CAP = 56
D = 1536
FFE = 512
ROWS = 128
OWN = 8
GROUP = 1024
DP = 16
EXPERTS = 24
HEADS = 3
QW = HEADS * HD
PAIR = 2 * CAP
PAIRS = OWN // 2
SLOTS = OWN * CAP
BLK = 256
WW = 384
XW = D + 128
CUT = FFE // 2
DOWN_ROWS = FFE // DP
GRAD_ROWS = 3 * (D // DP)
HALF = D // 2
EPS = 1e-06
THETA = 10000.0
VMEM = 60 * 1024 * 1024
f32 = jnp.float32
bf16 = jnp.bfloat16

NN = (((1,), (0,)), ((), ()))
NT = (((1,), (1,)), ((), ()))
TN = (((0,), (0,)), ((), ()))


def mm(a, b, dims=NN):
    return lax.dot_general(a, b, dims, preferred_element_type=f32)


def iota(shape, dim):
    return lax.broadcasted_iota(jnp.int32, shape, dim)


def swap_halves(v):
    lane = iota(v.shape, 1) % HD
    width = v.shape[1]
    ahead = pltpu.roll(v, width - HD // 2, 1)
    behind = pltpu.roll(v, HD // 2, 1)
    return jnp.where(lane < HD // 2, ahead, behind)


def block_mask(start_ref, at, keys):
    place = at + iota((BLK, keys), 0)
    key = iota((BLK, keys), 1)
    first = start_ref[pl.ds(at, BLK), :]
    return (key <= place) & (key >= first)


def turn(v):
    rows, cols = v.shape
    v = jnp.concatenate([v, jnp.zeros((128 - rows, cols), f32)], axis=0)
    if cols < 128:
        v = jnp.concatenate([v, jnp.zeros((128, 128 - cols), f32)], axis=1)
    return jnp.transpose(v)


def prep_kernel(
    own_ref, wq_ref, wk_ref, wv_ref, wr_ref, dy_ref, routes_ref, shard_ref, rows_ref, own_cols
):
    own = own_ref[0]
    rows_ref[:, 0:D] = dy_ref[...]
    rows_ref[:, D:XW] = turn(routes_ref[...].astype(f32)).astype(bf16)
    own_cols[...] = jnp.zeros_like(own_cols)
    for j in range(OWN):

        @pl.when(own == j)
        def _(j=j):
            own_cols[:, 0:QW] = wq_ref[:, j * QW : (j + 1) * QW]
            own_cols[:, QW:BLK] = wk_ref[:, j * HD : (j + 1) * HD]
            own_cols[:, BLK : BLK + HD] = wv_ref[:, j * HD : (j + 1) * HD]

    own_cols[:, BLK + HD : BLK + HD + EXPERTS] = turn(wr_ref[...].astype(f32))[0 : D // DP, 0:EXPERTS].astype(bf16)
    shard_ref[...] = jnp.broadcast_to(own_cols[...][None], shard_ref.shape)


def gate_kernel(in_ref, *refs):
    pass


def owner_of(own, dz, dc):
    return ((own // 2 + dz) % 4) * 2 + (own + dc) % 2


def pieces_of(refs):
    near, up, down, far_a, far_b = range(5)
    for dc in range(2):
        mine = refs[dc * 5 : dc * 5 + 5]
        yield 0, dc, lambda mine=mine: mine[near][...]
        yield 1, dc, lambda mine=mine: mine[down][...]
        yield 3, dc, lambda mine=mine: mine[up][...]
        yield 2, dc, lambda mine=mine: jnp.concatenate([mine[far_a][...], mine[far_b][...]], axis=0)


def whole_pieces_of(refs):
    for dc in range(2):
        for dz, at in ((0, 0), (3, 1), (1, 2), (2, 3)):
            yield dz, dc, lambda at=dc * 4 + at: refs[at][...]


def attend_kernel(own_ref, *refs):
    x_refs, refs = refs[:10], refs[10:]
    w_ref, gain_ref, cos_ref, sin_ref, start_ref, normed_ref, qkv_ref, mix_ref, log_ref = refs
    own = own_ref[0]
    for dz, dc, load in pieces_of(x_refs):
        rows = pl.ds(pl.multiple_of(owner_of(own, dz, dc) * ROWS, ROWS), ROWS)
        x = load().astype(f32)
        scale = lax.rsqrt(jnp.mean(x * x, axis=-1, keepdims=True) + EPS)
        normed_ref[rows, :] = (x * scale * gain_ref[...]).astype(bf16)
    for at in range(0, GROUP, 2 * BLK):
        rows = pl.ds(at, 2 * BLK)
        raw = mm(normed_ref[rows, :], w_ref[...])
        turned = raw[:, :BLK]
        turned = turned * cos_ref[rows, :] + swap_halves(turned) * sin_ref[rows, :]
        qkv_ref[rows, 0:BLK] = turned.astype(bf16)
        qkv_ref[rows, BLK:WW] = raw[:, BLK:WW].astype(bf16)
    for at in range(0, GROUP, BLK):
        rows = pl.ds(at, BLK)
        keys = at + BLK
        seen = block_mask(start_ref, at, keys)
        k_h = qkv_ref[0:keys, QW : QW + HD]
        v_h = qkv_ref[0:keys, BLK : BLK + HD]
        outs = []
        for r in range(HEADS):
            q_h = qkv_ref[rows, r * HD : (r + 1) * HD] * jnp.asarray(HD**-0.5, bf16)
            scores = jnp.where(seen, mm(q_h, k_h, NT), -1e30)
            top = jnp.max(scores, axis=-1, keepdims=True)
            terms = jnp.exp(scores - top)
            total = jnp.sum(terms, axis=-1, keepdims=True)
            prob = (terms / total).astype(bf16)
            outs.append(mm(prob, v_h))
            log_ref[rows, r : r + 1] = top + jnp.log(total)
        block = jnp.concatenate(outs + [jnp.zeros_like(outs[0])], axis=1).astype(bf16)
        mix_ref[at // ROWS] = block[0:ROWS]
        mix_ref[at // ROWS + 1] = block[ROWS:BLK]


def out_kernel(mix_ref, wo_ref, x_ref, gain_ref, hidden_ref, normed_ref, flat_ref):
    for j in range(OWN):
        flat_ref[:, j * QW : (j + 1) * QW] = mix_ref[j, :, 0:QW]
    hidden = x_ref[...].astype(f32) + mm(flat_ref[...], wo_ref[...])
    hidden_ref[...] = hidden
    scale = lax.rsqrt(jnp.mean(hidden * hidden, axis=-1, keepdims=True) + EPS)
    normed_ref[...] = (hidden * scale * gain_ref[...]).astype(bf16)


def router_probs(normed, w_ref):
    logits = mm(normed, w_ref[:, BLK:WW])
    lane = iota(logits.shape, 1)
    real = (lane >= HD) & (lane < HD + EXPERTS)
    logits = jnp.where(real, logits, -1e30)
    terms = jnp.exp(logits - jnp.max(logits, axis=-1, keepdims=True))
    terms = jnp.where(real, terms, 0.0)
    return terms / jnp.sum(terms, axis=-1, keepdims=True)


def pick_rows(slot_row, b):
    row = slot_row[:, b * BLK : (b + 1) * BLK]
    return iota((PAIR, BLK), 0) == row


def slots_kernel(own_ref, *refs):
    slot_ref, d_ref, routes_ref, dy_ref = refs[8:]
    for dz, dc, load in whole_pieces_of(refs[:8]):
        rows = pl.ds(pl.multiple_of(owner_of(own_ref[0], dz, dc) * ROWS, ROWS), ROWS)
        piece = load()
        dy_ref[rows, :] = piece[:, 0:D]
        routes_ref[:, rows] = jnp.transpose(piece[:, D:XW].astype(f32))[0:TOP]
    before = (iota((ROWS, ROWS), 0) < iota((ROWS, ROWS), 1)).astype(f32).astype(bf16)
    for e in range(EXP_DEV):
        own = own_ref[0] * EXP_DEV + e
        chosen = jnp.max((routes_ref[...] == own.astype(f32)).astype(f32), axis=0, keepdims=True)
        ranks = []
        for s in range(OWN):
            part = jnp.broadcast_to(chosen[:, s * ROWS : (s + 1) * ROWS], (8, ROWS)).astype(bf16)
            ranks.append(mm(part, before)[0:1] + float(CAP * (s % 2)))
        rank = jnp.concatenate(ranks, axis=1)
        slot_row = jnp.where(chosen > 0.0, rank, -1.0).astype(jnp.int32)
        slot_ref[e] = jnp.broadcast_to(slot_row, (8, GROUP))
        for b in range(PAIRS):
            pick = pick_rows(slot_row, b).astype(f32).astype(bf16)
            d_ref[e, b * PAIR : (b + 1) * PAIR, :] = mm(pick, dy_ref[b * BLK : (b + 1) * BLK, :]).astype(bf16)


def expert_kernel(own_ref, *refs):
    n_refs, refs = refs[:10], refs[10:]
    w_ref, d_ref, slot_ref, wg_ref, wu_ref, wd_ref, gg_ref, gu_ref, gd_ref, hg_ref, hu_ref, inner_ref, gate_ref = refs[:13]
    prob_ref, x_ref, n_ref = refs[13:]
    e = pl.program_id(0)
    own = own_ref[0] * EXP_DEV + e

    @pl.when(e == 0)
    def _():
        for dz, dc, load in pieces_of(n_refs):
            rows = pl.ds(pl.multiple_of(owner_of(own_ref[0], dz, dc) * ROWS, ROWS), ROWS)
            n_ref[rows, :] = load()
        for at in range(0, GROUP, BLK):
            probs = router_probs(n_ref[at : at + BLK, :], w_ref)
            prob_ref[:, at : at + BLK] = jnp.transpose(probs)

    gate_row = jnp.sum(jnp.where(iota((128, GROUP), 0) == HD + own, prob_ref[...], 0.0), axis=0, keepdims=True)
    slot_row = slot_ref[0, 0:1, :]
    for b in range(PAIRS):
        pick = pick_rows(slot_row, b)
        slots = pl.ds(b * PAIR, PAIR)
        x_ref[slots, :] = mm(pick.astype(f32).astype(bf16), n_ref[b * BLK : (b + 1) * BLK, :]).astype(bf16)
        gate_ref[0, slots, :] = jnp.sum(jnp.where(pick, gate_row[:, b * BLK : (b + 1) * BLK], 0.0), axis=1, keepdims=True)
    x = x_ref[...]
    gate_in = mm(x, wg_ref[0])
    up_in = mm(x, wu_ref[0])
    sig = jax.nn.sigmoid(gate_in)
    silu = gate_in * sig
    inner = (silu * up_in).astype(bf16)
    inner_ref[0] = inner
    gates = gate_ref[0]
    dy = d_ref[0].astype(f32)
    slot_grad = (gates * dy).astype(bf16)
    inner_grad = mm(slot_grad, wd_ref[0], NT)
    hg = (inner_grad * up_in * sig * (1.0 + gate_in * (1.0 - sig))).astype(bf16)
    hu = (inner_grad * silu).astype(bf16)
    hg_ref[0] = hg
    hu_ref[0] = hu
    gd_ref[0] = mm(inner, slot_grad, TN).astype(bf16)
    both = mm(x, jnp.concatenate([hg, hu], axis=1), TN)
    gg_ref[0] = both[:, 0:FFE].astype(bf16)
    gu_ref[0] = both[:, FFE : 2 * FFE].astype(bf16)


def widen_kernel(*refs):
    for in_ref, out_ref in zip(refs[:3], refs[3:]):
        out_ref[...] = in_ref[...].astype(f32)


def split_core(core, both):
    first, second = both[0:ROWS], both[ROWS:BLK]
    return jnp.where(core == 0, first, second), jnp.where(core == 0, second, first)


def scatter_pairs(own, slot_ref, parts):
    for dz in range(PAIRS):
        b = (own // 2 + dz) % PAIRS
        tokens = pl.ds(pl.multiple_of(b * BLK, BLK), BLK)
        slots = pl.ds(pl.multiple_of(b * PAIR, PAIR), PAIR)
        pick = jnp.concatenate(
            [(iota((PAIR, BLK), 0) == slot_ref[k, 0:1, tokens]).astype(f32).astype(bf16) for k in range(EXP_DEV)],
            axis=0,
        )
        for ref, width, at, keep_ref, send_ref in parts:
            values = jnp.concatenate([ref[k, slots, :] for k in range(EXP_DEV)], axis=0)
            keep, send = split_core(own % 2, mm(pick, values, TN))
            keep_ref[dz, :, at : at + width] = keep.astype(bf16)
            send_ref[dz, :, at : at + width] = send.astype(bf16)


def return_kernel(
    own_ref, hg_ref, hu_ref, inner_ref, gate_ref, d_ref, slot_ref, wg_ref, wu_ref, wd_ref,
    keep_ref, send_ref, gated_ref, rows_ref, p_ref,
):
    e = pl.program_id(0)
    own = own_ref[0] * EXP_DEV + e
    rows_ref[e] = (mm(hg_ref[0], wg_ref[0], NT) + mm(hu_ref[0], wu_ref[0], NT)).astype(bf16)
    out = mm(inner_ref[0], wd_ref[0]).astype(bf16).astype(f32)
    gated_ref[0] = (gate_ref[0] * out).astype(bf16)
    p = jnp.sum(d_ref[0].astype(f32) * out, axis=-1, keepdims=True)
    high = p.astype(bf16).astype(f32)
    lane = iota((SLOTS, 128), 1)
    p_ref[e] = jnp.where(lane == HD + own, high, jnp.where(lane == HD + 32 + own, p - high, 0.0)).astype(bf16)

    @pl.when(e == EXP_DEV - 1)
    def _():
        scatter_pairs(
            own_ref[0], slot_ref, ((rows_ref, D, 0, keep_ref, send_ref), (p_ref, 128, D, keep_ref, send_ref))
        )


def tokens_kernel(own_ref, gated_ref, slot_ref, dqkv_ref, w_ref, after_ref, keep_ref, send_ref):
    own = own_ref[0]
    scatter_pairs(own, slot_ref, ((gated_ref, D, D, keep_ref, send_ref),))
    for dz in range(PAIRS):
        b = (own // 2 + dz) % PAIRS
        rows = pl.ds(pl.multiple_of(b * BLK, BLK), BLK)
        keep, send = split_core(own % 2, mm(dqkv_ref[rows, :], w_ref[...], NT))
        keep_ref[dz, :, 0:D] = keep.astype(bf16)
        send_ref[dz, :, 0:D] = send.astype(bf16)


def first_sum_kernel(keep_ref, got_ref, near_ref, one_ref, three_ref, far_a_ref, far_b_ref):
    half = ROWS // 2

    def total(dz, rows):
        return (keep_ref[dz, rows, :].astype(f32) + got_ref[dz, rows, :].astype(f32)).astype(bf16)

    whole = slice(0, ROWS)
    far_a_ref[...] = total(2, slice(0, half))
    far_b_ref[...] = total(2, slice(half, ROWS))
    one_ref[...] = total(1, whole)
    three_ref[...] = total(3, whole)
    near_ref[...] = total(0, whole)


def second_sum_kernel(one_ref, three_ref, up_ref, down_ref, first_ref, last_ref):
    half = ROWS // 2
    first_ref[0:half, :] = (one_ref[0:half, :].astype(f32) + up_ref[...].astype(f32)).astype(bf16)
    first_ref[half:ROWS, :] = one_ref[half:ROWS, :]
    last_ref[0:half, :] = three_ref[0:half, :]
    last_ref[half:ROWS, :] = (three_ref[half:ROWS, :].astype(f32) + down_ref[...].astype(f32)).astype(bf16)


def hidden_kernel(
    part_a, part_b, part_c, dy_ref, hidden_ref, normed_ref, gain_ref, w_ref, wo_ref,
    grad_ref, gain_grad_ref, send_ref, cols_ref, logit_ref,
):
    hidden = hidden_ref[...]
    scale = lax.rsqrt(jnp.mean(hidden * hidden, axis=-1, keepdims=True) + EPS)
    unit = hidden * scale
    total = part_a[...].astype(f32) + part_b[...].astype(f32) + part_c[...].astype(f32)
    tail = total[:, D:XW]
    probs = router_probs(normed_ref[...], w_ref)
    p = tail + pltpu.roll(tail, 128 - 32, 1)
    logit_grad = probs * (p - jnp.sum(p * probs, axis=-1, keepdims=True))
    high = logit_grad.astype(bf16)
    low = (logit_grad - high.astype(f32)).astype(bf16)
    logit_ref[0] = high
    logit_ref[1] = low
    router = w_ref[:, BLK:WW]
    normed_grad = total[:, 0:D] + mm(high, router, NT) + mm(low, router, NT)
    gain_grad_ref[...] = jnp.sum(normed_grad * unit, axis=0, keepdims=True)
    unit_grad = normed_grad * gain_ref[...]
    grad = dy_ref[...].astype(f32) + scale * (unit_grad - unit * jnp.mean(unit_grad * unit, axis=-1, keepdims=True))
    grad_ref[...] = grad
    mix_grad = mm(grad.astype(bf16), wo_ref[...], NT)
    for j in range(OWN):
        cols = slice(j * QW, (j + 1) * QW)
        send_ref[j, :, 0:QW] = mix_grad[:, cols].astype(bf16)
        send_ref[j, :, QW:BLK] = jnp.zeros((ROWS, BLK - QW), bf16)
        cols_ref[j, :, 0:HD] = jnp.zeros((ROWS, HD), bf16)
        cols_ref[j, :, HD:BLK] = grad[:, cols].astype(bf16)


def attend_back_kernel(qkv_ref, log_ref, g_ref, cos_ref, sin_ref, start_ref, dqkv_ref, turn_ref, dk_ref, dv_ref):
    dk_ref[...] = jnp.zeros_like(dk_ref)
    dv_ref[...] = jnp.zeros_like(dv_ref)
    for at in range(0, GROUP, BLK):
        rows = pl.ds(at, BLK)
        keys = at + BLK
        seen = block_mask(start_ref, at, keys)
        k_h = qkv_ref[0:keys, QW : QW + HD]
        v_h = qkv_ref[0:keys, BLK : BLK + HD]
        for r in range(HEADS):
            q_h = qkv_ref[rows, r * HD : (r + 1) * HD] * jnp.asarray(HD**-0.5, bf16)
            g_h = g_ref[rows, r * HD : (r + 1) * HD]
            scores = jnp.where(seen, mm(q_h, k_h, NT), -1e30)
            prob = jnp.exp(scores - log_ref[rows, r : r + 1])
            dv_ref[0:keys, :] += mm(prob.astype(bf16), g_h, TN)
            prob_grad = mm(g_h, v_h, NT)
            delta = jnp.sum(prob_grad * prob, axis=-1, keepdims=True)
            score_grad = (prob * (prob_grad - delta)).astype(bf16)
            turn_ref[rows, r * HD : (r + 1) * HD] = mm(score_grad, k_h) * (HD**-0.5)
            dk_ref[0:keys, :] += mm(score_grad, q_h, TN)
    turn_ref[:, QW : QW + HD] = dk_ref[...]
    for at in range(0, GROUP, BLK):
        rows = pl.ds(at, BLK)
        turned = turn_ref[rows, :]
        turned = turned * cos_ref[rows, :] - swap_halves(turned) * sin_ref[rows, :]
        dqkv_ref[rows, 0:BLK] = turned.astype(bf16)
        dqkv_ref[rows, BLK : BLK + HD] = dv_ref[rows, :].astype(bf16)
        dqkv_ref[rows, BLK + HD : WW] = jnp.zeros((BLK, WW - BLK - HD), bf16)


def pay_kernel(normed_ref, dqkv_ref, mix_ref, got_ref, n_ref, logit_ref, moe_gain_ref, norm_ref, w_ref, pay_ref):
    left = mm(normed_ref[...], dqkv_ref[:, 0:BLK], TN)
    pay_ref[:, 0:BLK] = left.astype(bf16)
    value = mm(normed_ref[...], dqkv_ref[:, BLK:WW], TN)
    out = mm(mix_ref[...], got_ref[...], TN)
    pay_ref[:, BLK : 2 * BLK] = (jnp.concatenate([value, jnp.zeros((D, 128), f32)], axis=1) + out).astype(bf16)
    router = mm(n_ref[...], logit_ref[0], TN) + mm(n_ref[...], logit_ref[1], TN)
    attn_gain = jnp.sum(left * w_ref[:, 0:BLK].astype(f32), axis=1, keepdims=True)
    attn_gain = attn_gain + jnp.sum(value * w_ref[:, BLK:WW].astype(f32), axis=1, keepdims=True)
    gains = jnp.concatenate([1.0 / norm_ref[...], moe_gain_ref[...], jnp.zeros((126, D), f32)], axis=0)
    gains = jnp.transpose(gains)
    rows = D // DP
    lane = iota((rows, 128), 1)
    attn_gain, moe_gain = attn_gain * gains[:, 0:1], gains[:, 1:2]
    both = jnp.zeros((rows, 128), f32)
    for i in range(DP):
        part = slice(i * rows, (i + 1) * rows)
        both = jnp.where(lane == i, attn_gain[part], jnp.where(lane == DP + i, moe_gain[part], both))
    for i in range(DP):
        part = slice(i * rows, (i + 1) * rows)
        pay_ref[part, 2 * BLK : 2 * BLK + 128] = jnp.where(lane >= HD, router[part], both).astype(bf16)


def input_kernel(part_a, part_b, part_c, x_ref, gain_ref, hidden_grad_ref, hidden_ref, out_ref, layer_ref):
    x = x_ref[...].astype(f32)
    scale = lax.rsqrt(jnp.mean(x * x, axis=-1, keepdims=True) + EPS)
    unit = x * scale
    total = part_a[...].astype(f32) + part_b[...].astype(f32) + part_c[...].astype(f32)
    unit_grad = total[:, 0:D] * gain_ref[...]
    out_ref[...] = (
        hidden_grad_ref[...] + scale * (unit_grad - unit * jnp.mean(unit_grad * unit, axis=-1, keepdims=True))
    ).astype(bf16)
    layer_ref[...] = (hidden_ref[...] + total[:, D : 2 * D]).astype(bf16)


def sum_kernel(part_ref, after_ref, sum_ref):
    total = part_ref[0].astype(f32)
    for s in range(1, DP):
        total = total + part_ref[s].astype(f32)
    sum_ref[...] = jnp.broadcast_to(total.astype(bf16)[None], sum_ref.shape)


def join_kernel(part_ref, q_ref, k_ref, v_ref, o_ref, router_ref, gain_ref):
    gains = jnp.zeros((D // DP, 128), f32)
    for j in range(OWN):
        part = part_ref[j].astype(f32)
        q_ref[:, j * QW : (j + 1) * QW] = part[:, 0:QW]
        k_ref[:, j * HD : (j + 1) * HD] = part[:, QW:BLK]
        v_ref[:, j * HD : (j + 1) * HD] = part[:, BLK : BLK + HD]
        o_ref[:, j * QW : (j + 1) * QW] = part[:, BLK + HD : 2 * BLK]
        gains = gains + part[:, 2 * BLK : 2 * BLK + 128]
    router_ref[...] = gains[:, HD : HD + EXPERTS]
    gains = jnp.concatenate([gains, jnp.zeros((128 - D // DP, 128), f32)], axis=0)
    gain_ref[...] = jnp.transpose(gains)[0 : 2 * DP]


def sds(shape, dtype):
    return jax.ShapeDtypeStruct(shape, dtype)


def call(kernel, outs, scratch=(), cost=None, **grid):
    return pl.pallas_call(
        kernel,
        out_shape=outs,
        scratch_shapes=list(scratch),
        compiler_params=pltpu.CompilerParams(vmem_limit_bytes=VMEM),
        cost_estimate=cost,
        **grid,
    )


def cost(micros):
    return pl.CostEstimate(flops=int(micros * 1.15e9), bytes_accessed=1024, transcendentals=0)


VM = pl.BlockSpec(memory_space=pltpu.VMEM)
SM = pl.BlockSpec(memory_space=pltpu.SMEM)
ANY = pl.BlockSpec(memory_space=pl.ANY)


def along_z(step):
    return [(i, ((i // 2 + step) % 4) * 2 + i % 2) for i in range(OWN)]


UP, DOWN, SWAP = along_z(1), along_z(-1), [(i, i ^ 1) for i in range(OWN)]


def move(value, pairs):
    return lax.ppermute(value, "expert", pairs)


def gate(value, *after):
    return pl.pallas_call(
        gate_kernel,
        out_shape=sds(value.shape, value.dtype),
        in_specs=[ANY] * (1 + len(after)),
        out_specs=ANY,
        input_output_aliases={0: 0},
        compiler_params=pltpu.CompilerParams(vmem_limit_bytes=VMEM),
        cost_estimate=cost(0.5),
    )(value, *after)


def ring_rows(value, after=()):
    half = value.shape[0] // 2
    up, down = move(value, UP), move(value, DOWN)
    if after:
        up = gate(up, *after)
    far_a, far_b = move(up[:half], UP), move(down[half:], DOWN)
    return [value, up, down, far_a, far_b]


def swap_rows(mine):
    return mine + [move(piece, SWAP) for piece in mine]


def scatter_rows(keep, send):
    width = keep.shape[2]
    whole, half = sds((ROWS, width), bf16), sds((ROWS // 2, width), bf16)
    near, one, three, far_a, far_b = call(first_sum_kernel, [whole] * 3 + [half] * 2, cost=cost(0.1))(
        keep, move(send, SWAP)
    )
    first, last = call(second_sum_kernel, [whole] * 2, cost=cost(1))(one, three, move(far_a, UP), move(far_b, DOWN))
    return (near, move(first, UP), move(last, DOWN)), far_a


def body(
    tokens, norm_attn, query_weight, key_weight, value_weight, out_weight, norm_moe, router_weight,
    gate_weight, up_weight, down_weight, routes, seq_lengths, out_grad,
):
    own = lax.axis_index("expert").astype(jnp.int32).reshape(1)
    gain_one = norm_attn.reshape(1, D)
    gain_two = norm_moe.reshape(1, D)
    shard_rows = D // DP

    shard, rows = call(
        prep_kernel,
        [sds((DP, shard_rows, WW), bf16), sds((ROWS, XW), bf16)],
        scratch=[pltpu.VMEM((shard_rows, WW), bf16)],
        cost=cost(3),
        in_specs=[SM] + [VM] * 6,
    )(own, query_weight, key_weight, value_weight, router_weight.T, out_grad, routes.T)
    weights = lax.all_to_all(shard, "dp", 0, 0, tiled=True).reshape(D, WW)
    out_full = lax.all_gather(out_weight, "dp", axis=0, tiled=True)
    end_one = seq_lengths[0, 0]
    end_two = end_one + seq_lengths[0, 1]
    place = jnp.arange(GROUP, dtype=jnp.int32)
    start = jnp.where(place >= end_two, end_two, jnp.where(place >= end_one, end_one, 0)).astype(jnp.int32)
    steps = jnp.arange(HD // 2, dtype=f32)
    freq = jnp.exp(steps * (-2.0 * math.log(THETA) / HD))
    angles = (place - start).astype(f32)[:, None] * freq[None, :]
    cos_half, sin_half = jnp.cos(angles), jnp.sin(angles)
    cos_t = jnp.tile(cos_half, (1, 8))
    sin_t = jnp.tile(jnp.concatenate([-sin_half, sin_half], axis=1), (1, 4))
    start = start.reshape(GROUP, 1)
    x_ring = ring_rows(tokens)
    x_ring[3] = gate(x_ring[3], cos_t, sin_t, start)
    x_pieces = swap_rows(x_ring)
    dy_rows = gate(rows, x_ring[1], x_ring[2])
    dy_up, dy_down = move(dy_rows, UP), move(dy_rows, DOWN)
    dy_ring = [dy_rows, dy_up, dy_down, move(dy_up, UP)]

    part = lambda piece, width, at: pl.BlockSpec(
        (piece.shape[0], width), lambda e: (0, at), pipeline_mode=pl.Buffered(1)
    )
    normed_one, qkv, mix, logs = call(
        attend_kernel,
        [sds((GROUP, D), bf16), sds((GROUP, WW), bf16), sds((OWN, ROWS, BLK), bf16), sds((GROUP, 8), f32)],
        cost=cost(12),
        in_specs=[SM] + [VM] * 15,
    )(own, *x_pieces, weights, gain_one, cos_t, sin_t, start)

    mix_own = lax.all_to_all(gate(mix, dy_ring[2], dy_ring[3]), "expert", 0, 0, tiled=True)
    dy_pieces = swap_rows(dy_ring)
    hidden, normed_two, mix_flat = call(
        out_kernel,
        [sds((ROWS, D), f32), sds((ROWS, D), bf16), sds((ROWS, D), bf16)],
        cost=cost(4),
    )(mix_own, out_full, tokens, gain_two)
    slot_rows, d_slots = call(
        slots_kernel,
        [sds((EXP_DEV, 8, GROUP), jnp.int32), sds((EXP_DEV, SLOTS, D), bf16)],
        scratch=[pltpu.VMEM((TOP, GROUP), f32), pltpu.VMEM((GROUP, D), bf16)],
        cost=cost(6),
        in_specs=[SM] + [VM] * 8,
    )(own, *dy_pieces)
    n_pieces = swap_rows(ring_rows(normed_two, (slot_rows,)))
    mix_flat = gate(mix_flat, n_pieces[3], n_pieces[4])
    mix_all = lax.all_gather(mix_flat, "expert", axis=0, tiled=True)

    whole = lambda *shape: pl.BlockSpec(shape, lambda e: (0,) * len(shape), pipeline_mode=pl.Buffered(1))
    each = lambda *shape: pl.BlockSpec((1,) + shape, lambda e: (e, 0, 0))
    gg, gu, gd, hg, hu, inner, gates = call(
        expert_kernel,
        [
            sds((EXP_DEV, D, FFE), bf16), sds((EXP_DEV, D, FFE), bf16), sds((EXP_DEV, FFE, D), bf16),
            sds((EXP_DEV, SLOTS, FFE), bf16), sds((EXP_DEV, SLOTS, FFE), bf16), sds((EXP_DEV, SLOTS, FFE), bf16),
            sds((EXP_DEV, SLOTS, 1), f32),
        ],
        scratch=[
            pltpu.VMEM((128, GROUP), f32), pltpu.VMEM((SLOTS, D), bf16), pltpu.VMEM((GROUP, D), bf16),
        ],
        cost=cost(28),
        grid=(EXP_DEV,),
        in_specs=[
            SM, *[whole(*p.shape) for p in n_pieces], whole(D, WW), each(SLOTS, D), each(8, GROUP),
            each(D, FFE), each(D, FFE), each(FFE, D),
        ],
        out_specs=[
            each(D, FFE), each(D, FFE), each(FFE, D), each(SLOTS, FFE), each(SLOTS, FFE), each(SLOTS, FFE), each(SLOTS, 1),
        ],
    )(own, *n_pieces, weights, d_slots, slot_rows, gate_weight, up_weight, down_weight)

    gate_part, up_part, down_part = lax.psum((gate(gg, mix_all), gu, gd), "dp")

    dx_keep, dx_send, gated = call(
        return_kernel,
        [sds((PAIRS, ROWS, XW), bf16)] * 2 + [sds((EXP_DEV, SLOTS, D), bf16)],
        scratch=[pltpu.VMEM((EXP_DEV, SLOTS, D), bf16), pltpu.VMEM((EXP_DEV, SLOTS, 128), bf16)],
        cost=cost(1),
        grid=(EXP_DEV,),
        in_specs=[
            SM, each(SLOTS, FFE), each(SLOTS, FFE), each(SLOTS, FFE), each(SLOTS, 1), each(SLOTS, D),
            whole(EXP_DEV, 8, GROUP), each(D, FFE), each(D, FFE), each(FFE, D),
        ],
        out_specs=[whole(PAIRS, ROWS, XW)] * 2 + [each(SLOTS, D)],
    )(own, hg, hu, inner, gates, d_slots, slot_rows, gate_weight, up_weight, down_weight)

    dx_parts, _ = scatter_rows(dx_keep, dx_send)
    hidden_grad, moe_gain, send, cols, logit_grads = call(
        hidden_kernel,
        [sds((ROWS, D), f32), sds((1, D), f32), sds((OWN, ROWS, BLK), bf16), sds((OWN, ROWS, BLK), bf16),
            sds((2, ROWS, 128), bf16)],
        cost=cost(1),
    )(*dx_parts, out_grad, hidden, normed_two, gain_two, weights, out_full)
    mix_grad = lax.all_to_all(send, "expert", 0, 0, tiled=True).reshape(GROUP, BLK)
    got = lax.all_to_all(cols, "expert", 0, 0, tiled=True).reshape(GROUP, BLK)
    dqkv = call(
        attend_back_kernel,
        sds((GROUP, WW), bf16),
        scratch=[pltpu.VMEM((GROUP, BLK), f32), pltpu.VMEM((GROUP, HD), f32), pltpu.VMEM((GROUP, HD), f32)],
        cost=cost(12),
    )(qkv, logs, mix_grad, cos_t, sin_t, start)
    pay = call(pay_kernel, sds((D, 640), bf16), cost=cost(1))(
        normed_one, dqkv, mix_all, got, normed_two, logit_grads, moe_gain, gain_one, weights
    )
    pay_parts = lax.all_to_all(pay.reshape(DP, shard_rows, 640), "dp", 0, 0, tiled=True)
    rows_keep, rows_send = call(
        tokens_kernel, [sds((PAIRS, ROWS, 2 * D), bf16)] * 2, cost=cost(0.1), in_specs=[SM] + [VM] * 4 + [ANY]
    )(own, gated, slot_rows, dqkv, weights, pay)
    rows_parts, rows_first = scatter_rows(rows_keep, rows_send)
    pay_own = call(
        sum_kernel, sds((OWN, shard_rows, 640), bf16), cost=cost(1), in_specs=[VM, ANY]
    )(pay_parts, rows_first)
    pay_all = lax.all_to_all(pay_own, "expert", 0, 0, tiled=True)
    query_total, key_total, value_total, out_total, router_total, gains = call(
        join_kernel,
        [sds((shard_rows, w), f32) for w in (D, KVH * HD, KVH * HD, D, EXPERTS)] + [sds((2 * DP, 128), f32)],
        cost=cost(0.02),
    )(pay_all)
    gain_attn = gains[0:DP, :shard_rows].reshape(D)
    gain_moe = gains[DP:, :shard_rows].reshape(D)
    input_grad, layer_out = call(input_kernel, [sds((ROWS, D), bf16)] * 2, cost=cost(1))(
        *rows_parts, tokens, gain_one, hidden_grad, hidden
    )
    cut = lambda rows, cols: pl.BlockSpec((1, rows, cols), lambda e, h: (e, h, 0))
    widths = [cut(D // 2, FFE), cut(D // 2, FFE), cut(FFE // 2, D)]
    gate_total, up_total, down_total = call(
        widen_kernel,
        [sds((EXP_DEV, D, FFE), f32), sds((EXP_DEV, D, FFE), f32), sds((EXP_DEV, FFE, D), f32)],
        cost=cost(12),
        grid=(EXP_DEV, 2),
        in_specs=widths,
        out_specs=widths,
    )(gate_part, up_part, down_part)
    return (
        layer_out, input_grad, gain_attn, query_total, key_total, value_total, out_total, gain_moe, router_total,
        gate_total, up_total, down_total,
    )


def solution(mesh):
    both, dp, expert = P(("dp", "expert"), None), P("dp", None), P("expert", None, None)
    return jax.shard_map(
        body,
        mesh=mesh,
        in_specs=(both, P(), dp, dp, dp, dp, P(), dp, expert, expert, expert, both, dp, both),
        out_specs=(both, both, P(), dp, dp, dp, dp, P(), dp, expert, expert, expert),
        check_vma=False,
    )
```

time: 394 us -> 379 us (0.962)
  Pallas kernels: 110 us -> 144 us
  other arithmetic: 31.1 us -> 2.74 us
  waiting for transfers between devices: 136 us -> 111 us
  blocking collectives: 0 us -> 15.5 us
  starting transfers between devices: 75.4 us -> 60.7 us
    pallas_call x7 -> x12, Pallas kernels: 40.9 us -> 79.5 us  [the longest x1 17.7 us: body(): call(return_kernel, [sds((PAIRS, ROWS, XW), bf16)] * 2 + [sds((EXP_DEV, S...]
    all_gather x2 -> x1, waiting for transfers between devices: 28.1 us -> 0.64 us  [body(): out_full = lax.all_gather(out_weight, 'dp', axis=0, tiled=True)]
    convert_element_type x9 -> x0, other arithmetic: 25.7 us -> none  [the longest x6 8.01 us: add(): return (left.astype(f32) + right.astype(f32)).astype(bf16)]
    all_to_all x0 -> x1, blocking collectives: none -> 15.5 us  [body(): lax.all_to_all(send, 'expert', 0, 0, tiled=True).reshape(GROUP, BLK)]
    all_to_all x4 -> x2, starting transfers between devices: 22.7 us -> 8.95 us  [the longest x1 4.51 us: body(): lax.all_to_all(gate(mix, dy_ring[2], dy_ring[3]), 'expert', 0, 0, tiled=T...]
    all_to_all x4 -> x2, waiting for transfers between devices: 15.7 us -> 7.87 us  [the longest x1 7.87 us: body(): lax.all_to_all(gate(mix, dy_ring[2], dy_ring[3]), 'expert', 0, 0, tiled=T...]
    psum x1, waiting for transfers between devices: 31 us -> 24 us  [body(): gate_part, up_part, down_part = lax.psum((gate(gg, mix_all), gu, gd), 'dp')]
    all_to_all x1, waiting for transfers between devices: 19.8 us -> 26.6 us  [body(): lax.all_to_all(pay.reshape(DP, shard_rows, 640), 'dp', 0, 0, tiled=True)]
  transfers between devices with their start and end apart: 36 -> 43, of which waited for: 14 -> 19; matrix products, arithmetic and copies ran while one was open for 6% -> 3% of each run, Pallas kernels for 26% -> 35%
where the time goes in v3:
time: 379 us; the launch traced here: 373 us
  Pallas kernels  144 us (38%)
  waiting for transfers between devices  111 us (29%)
  starting transfers between devices  60.7 us (16%)
  local copies, waits for them, and re-layouts  23.6 us (6%)
  between operations  15.7 us (4%)
  blocking collectives  15.5 us (4%)
    ppermute x35, waiting for transfers between devices, move(): return lax.ppermute(value, 'expert', pairs)  39.3 us
    ppermute x35, starting transfers between devices, move(): return lax.ppermute(value, 'expert', pairs)  34.7 us
    all_to_all x1, waiting for transfers between devices, body(): lax.all_to_all(pay.reshape(DP, shard_rows, 640), 'dp', 0, 0, tiled=True)  26.6 us
    pallas_call x1, Pallas kernels, body(): call(expert_kernel, [sds((EXP_DEV, D, FFE), bf16), sds((EXP_DEV, D, FFE),...  24.7 us
    psum x1, waiting for transfers between devices, body(): gate_part, up_part, down_part = lax.psum((gate(gg, mix_all), gu, gd), 'dp')  24 us
    pallas_call x1, Pallas kernels, body(): call(return_kernel, [sds((PAIRS, ROWS, XW), bf16)] * 2 + [sds((EXP_DEV, S...  17.7 us
    unnamed x81, local copies, waits for them, and re-layouts  15.9 us
    all_to_all x1, blocking collectives, body(): lax.all_to_all(send, 'expert', 0, 0, tiled=True).reshape(GROUP, BLK)  15.5 us
  transfers between devices with their start and end apart: 43, of which 19 were waited for; matrix products, arithmetic and copies ran while one was open for 3% of the time, Pallas kernels for 35%

profile of v3, /device:TPU:1, one launch (start us, length us, event | category | flops | bytes accessed | tf_op | source)
XLA Modules:
  0.0 373.3 jit_solution(1150438720862749703)
XLA Ops:
  16.3 6.8 %all-to-all-start = ((bf16[16,96,384]{2,1,0:T(8,128)(2,1)}), bf16[16,96,384]{2,1,0:T(8,128)(2,1)S(1)}, u32[]{:S(2)}, u32[]{:S(2)}) async-start(bf16[16,96,384]{2,1,0:T(8,128)(2,1)} %get-tuple-element.65), calls=%async_computation | async-start | bytes 2359296 | tf_op jit(solution)/shard_map/all_to_all | solution.py:532
  48.1 12.7 %shard_map.231 = (bf16[1024,1536]{1,0:T(8,128)(2,1)}, bf16[1024,384]{1,0:T(8,128)(2,1)}, bf16[8,128,256]{2,1,0:T(8,128)(2,1)}, f32[1024,8]{1,0:T(8,128)}) custom-call(s32[1]{0:T(128)} %bitcast.own_ref, bf16[128,1536]{1,0:T(8,128)(2,1)} %x_ref.3, bf16[128,1536]{1,0:T(8,128)(2,1)} %copy-done.12, bf16[128,1536]{1,0:T(8,128)(2,1)} %copy-done.13, ...), custom_call_target="tpu_custom_call" | custom-call | flops 13799999488 | bytes 1024 | tf_op jit(solution)/shard_map/pallas_call | solution.py:555
  61.7 4.5 %all-to-all-start.1 = ((bf16[8,128,256]{2,1,0:T(8,128)(2,1)}), bf16[8,128,256]{2,1,0:T(8,128)(2,1)S(1)}, u32[]{:S(2)}, u32[]{:S(2)}) async-start(bf16[8,128,256]{2,1,0:T(8,128)(2,1)} %shard_map.233), calls=%async_computation.1 | async-start | bytes 1048576 | tf_op jit(solution)/shard_map/all_to_all | solution.py:562
  67.9 7.9 %all-to-all-done.1.mix_ref = bf16[8,128,256]{2,1,0:T(8,128)(2,1)S(1)} async-done(((bf16[8,128,256]{2,1,0:T(8,128)(2,1)}), bf16[8,128,256]{2,1,0:T(8,128)(2,1)S(1)}, u32[]{:S(2)}, u32[]{:S(2)}) %all-to-all-start.1) | async-done | bytes 524320 | tf_op jit(solution)/shard_map/all_to_all | solution.py:562
  76.6 4.5 %shard_map.234 = (f32[128,1536]{1,0:T(8,128)}, bf16[128,1536]{1,0:T(8,128)(2,1)}, bf16[128,1536]{1,0:T(8,128)(2,1)}) custom-call(bf16[8,128,256]{2,1,0:T(8,128)(2,1)} %copy-done.8, bf16[1536,1536]{1,0:T(8,128)(2,1)} %all-gather.3.cloned.1.call-done.wo_ref, bf16[128,1536]{1,0:T(8,128)(2,1)} %x_ref.3, f32[1,1536]{1,0:T(1,128)} %reshape.118.gain_ref), custom_call_target="tpu_custom_call" | custom-call | flops 4600000000 | bytes 1024 | tf_op jit(solution)/shard_map/pallas_call | solution.py:564
  85.5 6.0 %shard_map.235 = (s32[3,8,1024]{2,1,0:T(8,128)}, bf16[3,448,1536]{2,1,0:T(8,128)(2,1)}) custom-call(s32[1]{0:T(128)} %bitcast.own_ref, bf16[128,1664]{1,0:T(8,128)(2,1)} %shard_map.232.refs_0_, bf16[128,1664]{1,0:T(8,128)(2,1)} %copy-done.19, bf16[128,1664]{1,0:T(8,128)(2,1)} %copy-done.20, bf16[128,1664]{1,0:T(8,128)(2,1)} %copy-done.21, ...), custom_call_target="tpu_custom_call" | custom-call | flops 6899999744 | bytes 1024 | tf_op jit(solution)/shard_map/pallas_call | solution.py:569
  107.5 24.7 %shard_map.237 = (bf16[3,1536,512]{2,1,0:T(8,128)(2,1)}, bf16[3,1536,512]{2,1,0:T(8,128)(2,1)}, bf16[3,512,1536]{2,1,0:T(8,128)(2,1)}, bf16[3,448,512]{2,1,0:T(8...) custom-call(s32[1]{0:T(128)} %bitcast.own_ref, ...), custom_call_target="tpu_custom_call" | custom-call | flops 32199999488 | bytes 1024 | tf_op jit(solution)/shard_map/pallas_call | solution.py:582
  132.3 17.7 %shard_map.238 = (bf16[4,128,1664]{2,1,0:T(8,128)(2,1)}, bf16[4,128,1664]{2,1,0:T(8,128)(2,1)}, bf16[3,448,1536]{2,1,0:T(8,128)(2,1)}) custom-call(s32[1]{0:T(128)} %bitcast.own_ref, bf16[3,448,512]{2,1,0:T(8,128)(2,1)} %get-tuple-element.71.hg_ref, bf16[3,448,512]{2,1,0:T(8,128)(2,1)} %get-tuple-element.72.hu_ref, ...), custom_call_target="tpu_custom_call" | custom-call | flops 1150000000 | bytes 1024 | tf_op jit(solution)/shard_map/pallas_call | solution.py:605
  161.3 5.5 %collective-permute-done.26.up_ref = bf16[64,1664]{1,0:T(8,128)(2,1)S(1)} collective-permute-done((bf16[64,1664]{1,0:T(8,128)(2,1)}, bf16[64,1664]{1,0:T(8,128)(2,1)S(1)}, u32[]{:S(2)}, u32[]{:S(2)}) %collective-permute-start.26) | collective-permute-done | bytes 213024 | tf_op jit(solution)/shard_map/ppermute | solution.py:478
  172.7 9.1 %collective-permute-done.28.part_b = bf16[128,1664]{1,0:T(8,128)(2,1)S(1)} collective-permute-done((bf16[128,1664]{1,0:T(8,128)(2,1)}, bf16[128,1664]{1,0:T(8,128)(2,1)S(1)}, u32[]{:S(2)}, u32[]{:S(2)}) %collective-permute-start.28) | collective-permute-done | bytes 426016 | tf_op jit(solution)/shard_map/ppermute | solution.py:478
  182.8 7.4 %shard_map.241 = (f32[128,1536]{1,0:T(8,128)}, f32[1,1536]{1,0:T(1,128)}, bf16[8,128,256]{2,1,0:T(8,128)(2,1)}, bf16[8,128,256]{2,1,0:T(8,128)(2,1)}, bf16[2,128,128]{2,1,0:T(8,128)(2,1)}) custom-call(bf16[128,1664]{1,0:T(8,128)(2,1)} %get-tuple-element.80.part_a, bf16[128,1664]{1,0:T(8,128)(2,1)} %copy-done.9, bf16[128,1664]{1,0:T(8,128)(2,1)} %copy-done.10, ...), custom_call_target="tpu_custom_call" | custom-call | flops 1150000000 | bytes 1024 | tf_op jit(solution)/shard_map/pallas_call | solution.py:619
  190.1 15.5 %all_to_all.30 = bf16[8,128,256]{2,1,0:T(8,128)(2,1)} all-to-all(bf16[8,128,256]{2,1,0:T(8,128)(2,1)} %get-tuple-element.88), channel_id=1, replica_groups=mesh['dp'=16,'expert'=8] {'expert'}, dimensions={0} | all-to-all | bytes 1048576 | tf_op jit(solution)/shard_map/all_to_all | solution.py:625
  205.6 4.4 %all-to-all-start.3 = ((bf16[8,128,256]{2,1,0:T(8,128)(2,1)}), bf16[8,128,256]{2,1,0:T(8,128)(2,1)S(1)}, u32[]{:S(2)}, u32[]{:S(2)}) async-start(bf16[8,128,256]{2,1,0:T(8,128)(2,1)} %get-tuple-element.91), calls=%async_computation.3 | async-start | bytes 1048576 | tf_op jit(solution)/shard_map/all_to_all | solution.py:626
  210.0 12.5 %shard_map.242.dqkv_ref = bf16[1024,384]{1,0:T(8,128)(2,1)} custom-call(bf16[1024,384]{1,0:T(8,128)(2,1)} %get-tuple-element.76.qkv_ref, f32[1024,8]{1,0:T(8,128)} %get-tuple-element.77.log_ref, bf16[1024,256]{1,0:T(8,128)(2,1)} %bitcast.19, f32[1024,256]{1,0:T(8,128)} %copy.33.refs_0_.refs_12_.cos_ref, f32[1024,256]{1,0:T(8,128)} %copy.34.refs_1_.refs_13_.sin_ref, ...), custom_call_target="tpu_custom_call" | custom-call | flops 13799999488 | bytes 1024 | tf_op jit(solution)/shard_map/pallas_call | solution.py:627
  223.3 8.9 %shard_map.244.after_ref = bf16[1536,640]{1,0:T(8,128)(2,1)} custom-call(bf16[1024,1536]{1,0:T(8,128)(2,1)} %get-tuple-element.89.normed_ref, bf16[1024,384]{1,0:T(8,128)(2,1)} %shard_map.242.dqkv_ref, bf16[1024,1536]{1,0:T(8,128)(2,1)} %all-gather.5.cloned.1.call-done.mix_ref.refs_0_, bf16[1024,256]{1,0:T(8,128)(2,1)} %bitcast.18, ...), custom_call_target="tpu_custom_call" | custom-call | flops 1150000000 | bytes 1024 | tf_op jit(solution)/shard_map/pallas_call | solution.py:633
  232.2 9.1 %shard_map.245 = (bf16[4,128,3072]{2,1,0:T(8,128)(2,1)}, bf16[4,128,3072]{2,1,0:T(8,128)(2,1)}) custom-call(s32[1]{0:T(128)} %bitcast.own_ref, bf16[3,448,1536]{2,1,0:T(8,128)(2,1)} %get-tuple-element.75.gated_ref, s32[3,8,1024]{2,1,0:T(8,128)} %get-tuple-element.69.refs_0_.refs_12_.slot_ref, bf16[1024,384]{1,0:T(8,128)(2,1)} %shard_map.242.dqkv_ref, ...), custom_call_target="tpu_custom_call" | custom-call | flops 115000000 | bytes 1024 | tf_op jit(solution)/shard_map/pallas_call | solution.py:637
  241.5 4.6 %all-to-all-start.4 = ((bf16[16,96,640]{2,1,0:T(8,128)(2,1)}), bf16[16,96,640]{2,1,0:T(8,128)(2,1)}, u32[]{:S(2)}, u32[]{:S(2)}) async-start(bf16[16,96,640]{2,1,0:T(8,128)(2,1)} %bitcast.10), calls=%async_computation.4 | async-start | bytes 3932160 | tf_op jit(solution)/shard_map/all_to_all | solution.py:636
  248.9 4.7 %shard_map.246 = (bf16[128,3072]{1,0:T(8,128)(2,1)}, bf16[128,3072]{1,0:T(8,128)(2,1)}, bf16[128,3072]{1,0:T(8,128)(2,1)}, bf16[64,3072]{1,0:T(8,128)(2,1)}, bf16[64,3072]{1,0:T(8,128)(2,1)}) custom-call(bf16[4,128,3072]{2,1,0:T(8,128)(2,1)} %get-tuple-element.94.keep_ref, bf16[4,128,3072]{2,1,0:T(8,128)(2,1)} %copy-done.2), custom_call_target="tpu_custom_call" | custom-call | flops 115000000 | bytes 1024 | tf_op jit(solution)/shard_map/pallas_call | solution.py:509
  256.3 26.6 %all-to-all-done.4.part_ref = bf16[16,96,640]{2,1,0:T(8,128)(2,1)} async-done(((bf16[16,96,640]{2,1,0:T(8,128)(2,1)}), bf16[16,96,640]{2,1,0:T(8,128)(2,1)}, u32[]{:S(2)}, u32[]{:S(2)}) %all-to-all-start.4) | async-done | bytes 1966112 | tf_op jit(solution)/shard_map/all_to_all | solution.py:636
  285.7 5.5 %all-to-all-start.5 = ((bf16[8,96,640]{2,1,0:T(8,128)(2,1)}), bf16[8,96,640]{2,1,0:T(8,128)(2,1)S(1)}, u32[]{:S(2)}, u32[]{:S(2)}) async-start(bf16[8,96,640]{2,1,0:T(8,128)(2,1)} %shard_map.249), calls=%async_computation.5 | async-start | bytes 1966080 | tf_op jit(solution)/shard_map/all_to_all | solution.py:644
  298.0 7.7 %all-to-all-done.5.part_ref = bf16[8,96,640]{2,1,0:T(8,128)(2,1)S(1)} async-done(((bf16[8,96,640]{2,1,0:T(8,128)(2,1)}), bf16[8,96,640]{2,1,0:T(8,128)(2,1)S(1)}, u32[]{:S(2)}, u32[]{:S(2)}) %all-to-all-start.5) | async-done | bytes 983072 | tf_op jit(solution)/shard_map/all_to_all | solution.py:644
  312.7 9.7 %collective-permute-done.33.part_b = bf16[128,3072]{1,0:T(8,128)(2,1)S(1)} collective-permute-done((bf16[128,3072]{1,0:T(8,128)(2,1)}, bf16[128,3072]{1,0:T(8,128)(2,1)S(1)}, u32[]{:S(2)}, u32[]{:S(2)}) %collective-permute-start.33) | collective-permute-done | bytes 786464 | tf_op jit(solution)/shard_map/ppermute | solution.py:478
  327.7 24.0 %all-reduce.3.cloned.1.call-done = (bf16[3,1536,512]{2,1,0:T(8,128)(2,1)}, bf16[3,1536,512]{2,1,0:T(8,128)(2,1)}, bf16[3,512,1536]{2,1,0:T(8,128)(2,1)}) async-done(((bf16[3,1536,512]{2,1,0:T(8,128)(2,1)}, bf16[3,1536,512]{2,1,0:T(8,128)(2,1)}, bf16[3,512,1536]{2,1,0:T(8,128)(2,1)}), (bf16[3,1536,512]{2,1,0:T(8,128)(2,1)}, bf16[3,1536,512]{2,1,0:T(8,128)(2,1)}, ...) | async-done | bytes 14155792 | tf_op jit(solution)/shard_map/psum | solution.py:603
  351.7 14.9 %shard_map.252 = (f32[3,1536,512]{2,1,0:T(8,128)}, f32[3,1536,512]{2,1,0:T(8,128)}, f32[3,512,1536]{2,1,0:T(8,128)}) custom-call(bf16[3,1536,512]{2,1,0:T(8,128)(2,1)} %get-tuple-element.142.refs_0_, bf16[3,1536,512]{2,1,0:T(8,128)(2,1)} %get-tuple-element.143.refs_1_, bf16[3,512,1536]{2,1,0:T(8,128)(2,1)} %get-tuple-element.144.refs_2_), custom_call_target="tpu_custom_call" | custom-call | flops 13799999488 | bytes 1024 | tf_op jit(solution)/shard_map/pallas_call | solution.py:657
  (190 shorter events, 102.8 us)
Async XLA Ops:
  7.2 69.2 %all-gather.3.cloned.1.call-start = ((), (), s32[]{:S(2)}) async-start(), calls=%async_computation.6 | async-start | bytes 5013504 | tf_op jit(solution)/shard_map/all_gather | solution.py:533
  7.9 17.7 %collective-permute-start = (bf16[128,1536]{1,0:T(8,128)(2,1)}, bf16[128,1536]{1,0:T(8,128)(2,1)S(1)}, u32[]{:S(2)}, u32[]{:S(2)}) collective-permute-start(bf16[128,1536]{1,0:T(8,128)(2,1)} %x_ref.3), channel_id=1, source_target_pairs={{0,2},{1,3},{2,4},{3,5},{4,6},{5,7},{6,0},{7,1},{8,10},{9,11},{10,... | collective-permute-start | bytes 1179656 | tf_op jit(solution)/shard_map/ppermute | solution.py:478
  10.4 15.9 %collective-permute-start.1 = (bf16[128,1536]{1,0:T(8,128)(2,1)}, bf16[128,1536]{1,0:T(8,128)(2,1)S(1)}, u32[]{:S(2)}, u32[]{:S(2)}) collective-permute-start(bf16[128,1536]{1,0:T(8,128)(2,1)} %x_ref.3), channel_id=1, source_target_pairs={{0,6},{1,7},{2,0},{3,1},{4,2},{5,3},{6,4},{7,5},{8,14},{9,15},{10,... | collective-permute-start | bytes 1179656 | tf_op jit(solution)/shard_map/ppermute | solution.py:478
  12.7 26.7 %collective-permute-start.4 = (bf16[128,1536]{1,0:T(8,128)(2,1)}, bf16[128,1536]{1,0:T(8,128)(2,1)}, u32[]{:S(2)}, u32[]{:S(2)}) collective-permute-start(bf16[128,1536]{1,0:T(8,128)(2,1)} %x_ref.3), channel_id=1, source_target_pairs={{0,1},{1,0},{2,3},{3,2},{4,5},{5,4},{6,7},{7,6},{8,9},{9,8},{10,11... | collective-permute-start | bytes 1179656 | tf_op jit(solution)/shard_map/ppermute | solution.py:478
  16.3 30.8 %all-to-all-start = ((bf16[16,96,384]{2,1,0:T(8,128)(2,1)}), bf16[16,96,384]{2,1,0:T(8,128)(2,1)S(1)}, u32[]{:S(2)}, u32[]{:S(2)}) async-start(bf16[16,96,384]{2,1,0:T(8,128)(2,1)} %get-tuple-element.65), calls=%async_computation | async-start | bytes 2359296 | tf_op jit(solution)/shard_map/all_to_all | solution.py:532
  26.4 13.0 %collective-permute-start.3 = (bf16[64,1536]{1,0:T(8,128)(2,1)S(1)}, bf16[64,1536]{1,0:T(8,128)(2,1)S(1)}, u32[]{:S(2)}, u32[]{:S(2)}) collective-permute-start(bf16[64,1536]{1,0:T(8,128)(2,1)S(1)} %slice.33), channel_id=1, source_target_pairs={{0,6},{1,7},{2,0},{3,1},{4,2},{5,3},{6,4},{7,5},{8,14},{9,15},{10,... | collective-permute-start | bytes 589832 | tf_op jit(solution)/shard_map/ppermute | solution.py:478
  29.1 13.4 %collective-permute-start.10 = (bf16[128,1664]{1,0:T(8,128)(2,1)}, bf16[128,1664]{1,0:T(8,128)(2,1)S(1)}, u32[]{:S(2)}, u32[]{:S(2)}) collective-permute-start(bf16[128,1664]{1,0:T(8,128)(2,1)} %shard_map.232.refs_0_), channel_id=1, source_target_pairs={{0,2},{1,3},{2,4},{3,5},{4,6},{5,7},{6,0},{7,1},{8,10},{9,11},{10,... | collective-permute-start | bytes 1277960 | tf_op jit(solution)/shard_map/ppermute | solution.py:478
  40.5 20.4 %collective-permute-start.9 = (bf16[128,1664]{1,0:T(8,128)(2,1)}, bf16[128,1664]{1,0:T(8,128)(2,1)S(1)}, u32[]{:S(2)}, u32[]{:S(2)}) collective-permute-start(bf16[128,1664]{1,0:T(8,128)(2,1)} %shard_map.232.refs_0_), channel_id=1, source_target_pairs={{0,6},{1,7},{2,0},{3,1},{4,2},{5,3},{6,4},{7,5},{8,14},{9,15},{10,... | collective-permute-start | bytes 1277960 | tf_op jit(solution)/shard_map/ppermute | solution.py:478
  42.5 18.4 %collective-permute-start.11 = (bf16[128,1664]{1,0:T(8,128)(2,1)S(1)}, bf16[128,1664]{1,0:T(8,128)(2,1)S(1)}, u32[]{:S(2)}, u32[]{:S(2)}) collective-permute-start(bf16[128,1664]{1,0:T(8,128)(2,1)S(1)} %collective-permute-done.10.refs_1_), channel_id=1, source_target_pairs={{0,2},{1,3},{2,4},{3,5},{4,6},{5,7},{6,0},{7,1},{8,10},{9,11},{10,... | collective-permute-start | bytes 1277960 | tf_op jit(solution)/shard_map/ppermute | solution.py:478
  61.7 14.0 %all-to-all-start.1 = ((bf16[8,128,256]{2,1,0:T(8,128)(2,1)}), bf16[8,128,256]{2,1,0:T(8,128)(2,1)S(1)}, u32[]{:S(2)}, u32[]{:S(2)}) async-start(bf16[8,128,256]{2,1,0:T(8,128)(2,1)} %shard_map.233), calls=%async_computation.1 | async-start | bytes 1048576 | tf_op jit(solution)/shard_map/all_to_all | solution.py:562
  66.3 66.0 %all-gather.5.cloned.1.call-start = ((), (), s32[]{:S(2)}) async-start(), calls=%async_computation.7 | async-start | bytes 3538944 | tf_op jit(solution)/shard_map/all_gather | solution.py:578
  66.9 15.4 %collective-permute-start.13 = (bf16[128,1664]{1,0:T(8,128)(2,1)}, bf16[128,1664]{1,0:T(8,128)(2,1)S(1)}, u32[]{:S(2)}, u32[]{:S(2)}) collective-permute-start(bf16[128,1664]{1,0:T(8,128)(2,1)} %shard_map.232.refs_0_), channel_id=1, source_target_pairs={{0,1},{1,0},{2,3},{3,2},{4,5},{5,4},{6,7},{7,6},{8,9},{9,8},{10,11... | collective-permute-start | bytes 1277960 | tf_op jit(solution)/shard_map/ppermute | solution.py:478
  67.0 16.8 %collective-permute-start.14 = (bf16[128,1664]{1,0:T(8,128)(2,1)S(1)}, bf16[128,1664]{1,0:T(8,128)(2,1)S(1)}, u32[]{:S(2)}, u32[]{:S(2)}) collective-permute-start(bf16[128,1664]{1,0:T(8,128)(2,1)S(1)} %collective-permute-done.10.refs_1_), channel_id=1, source_target_pairs={{0,1},{1,0},{2,3},{3,2},{4,5},{5,4},{6,7},{7,6},{8,9},{9,8},{10,11... | collective-permute-start | bytes 1277960 | tf_op jit(solution)/shard_map/ppermute | solution.py:478
  67.4 16.4 %collective-permute-start.15 = (bf16[128,1664]{1,0:T(8,128)(2,1)}, bf16[128,1664]{1,0:T(8,128)(2,1)S(1)}, u32[]{:S(2)}, u32[]{:S(2)}) collective-permute-start(bf16[128,1664]{1,0:T(8,128)(2,1)} %copy-done.20), channel_id=1, source_target_pairs={{0,1},{1,0},{2,3},{3,2},{4,5},{5,4},{6,7},{7,6},{8,9},{9,8},{10,11... | collective-permute-start | bytes 1277960 | tf_op jit(solution)/shard_map/ppermute | solution.py:478
  67.5 16.3 %collective-permute-start.16 = (bf16[128,1664]{1,0:T(8,128)(2,1)}, bf16[128,1664]{1,0:T(8,128)(2,1)S(1)}, u32[]{:S(2)}, u32[]{:S(2)}) collective-permute-start(bf16[128,1664]{1,0:T(8,128)(2,1)} %copy-done.21), channel_id=1, source_target_pairs={{0,1},{1,0},{2,3},{3,2},{4,5},{5,4},{6,7},{7,6},{8,9},{9,8},{10,11... | collective-permute-start | bytes 1277960 | tf_op jit(solution)/shard_map/ppermute | solution.py:478
  100.5 251.2 %all-reduce.3.cloned.1.call-start = ((), (), s32[]{:S(2)}) async-start(), calls=%async_computation.8 | async-start | bytes 28311552 | tf_op jit(solution)/shard_map/psum | solution.py:603
  169.9 12.0 %collective-permute-start.28 = (bf16[128,1664]{1,0:T(8,128)(2,1)}, bf16[128,1664]{1,0:T(8,128)(2,1)S(1)}, u32[]{:S(2)}, u32[]{:S(2)}) collective-permute-start(bf16[128,1664]{1,0:T(8,128)(2,1)} %get-tuple-element.85), channel_id=1, source_target_pairs={{0,2},{1,3},{2,4},{3,5},{4,6},{5,7},{6,0},{7,1},{8,10},{9,11},{10,... | collective-permute-start | bytes 1277960 | tf_op jit(solution)/shard_map/ppermute | solution.py:478
  205.6 16.9 %all-to-all-start.3 = ((bf16[8,128,256]{2,1,0:T(8,128)(2,1)}), bf16[8,128,256]{2,1,0:T(8,128)(2,1)S(1)}, u32[]{:S(2)}, u32[]{:S(2)}) async-start(bf16[8,128,256]{2,1,0:T(8,128)(2,1)} %get-tuple-element.91), calls=%async_computation.3 | async-start | bytes 1048576 | tf_op jit(solution)/shard_map/all_to_all | solution.py:626
  241.5 41.4 %all-to-all-start.4 = ((bf16[16,96,640]{2,1,0:T(8,128)(2,1)}), bf16[16,96,640]{2,1,0:T(8,128)(2,1)}, u32[]{:S(2)}, u32[]{:S(2)}) async-start(bf16[16,96,640]{2,1,0:T(8,128)(2,1)} %bitcast.10), calls=%async_computation.4 | async-start | bytes 3932160 | tf_op jit(solution)/shard_map/all_to_all | solution.py:636
  253.6 37.6 %collective-permute-start.31 = (bf16[64,3072]{1,0:T(8,128)(2,1)}, bf16[64,3072]{1,0:T(8,128)(2,1)S(1)}, u32[]{:S(2)}, u32[]{:S(2)}) collective-permute-start(bf16[64,3072]{1,0:T(8,128)(2,1)} %get-tuple-element.99.after_ref), channel_id=1, source_target_pairs={{0,2},{1,3},{2,4},{3,5},{4,6},{5,7},{6,0},{7,1},{8,10},{9,11},{10,... | collective-permute-start | bytes 1179656 | tf_op jit(solution)/shard_map/ppermute | solution.py:478
  255.1 36.2 %collective-permute-start.32 = (bf16[64,3072]{1,0:T(8,128)(2,1)}, bf16[64,3072]{1,0:T(8,128)(2,1)S(1)}, u32[]{:S(2)}, u32[]{:S(2)}) collective-permute-start(bf16[64,3072]{1,0:T(8,128)(2,1)} %get-tuple-element.100), channel_id=1, source_target_pairs={{0,6},{1,7},{2,0},{3,1},{4,2},{5,3},{6,4},{7,5},{8,14},{9,15},{10,... | collective-permute-start | bytes 1179656 | tf_op jit(solution)/shard_map/ppermute | solution.py:478
  285.7 20.0 %all-to-all-start.5 = ((bf16[8,96,640]{2,1,0:T(8,128)(2,1)}), bf16[8,96,640]{2,1,0:T(8,128)(2,1)S(1)}, u32[]{:S(2)}, u32[]{:S(2)}) async-start(bf16[8,96,640]{2,1,0:T(8,128)(2,1)} %shard_map.249), calls=%async_computation.5 | async-start | bytes 1966080 | tf_op jit(solution)/shard_map/all_to_all | solution.py:644
  295.3 27.2 %collective-permute-start.33 = (bf16[128,3072]{1,0:T(8,128)(2,1)}, bf16[128,3072]{1,0:T(8,128)(2,1)S(1)}, u32[]{:S(2)}, u32[]{:S(2)}) collective-permute-start(bf16[128,3072]{1,0:T(8,128)(2,1)} %get-tuple-element.101), channel_id=1, source_target_pairs={{0,2},{1,3},{2,4},{3,5},{4,6},{5,7},{6,0},{7,1},{8,10},{9,11},{10,... | collective-permute-start | bytes 2359304 | tf_op jit(solution)/shard_map/ppermute | solution.py:478
  296.7 25.8 %collective-permute-start.34 = (bf16[128,3072]{1,0:T(8,128)(2,1)}, bf16[128,3072]{1,0:T(8,128)(2,1)S(1)}, u32[]{:S(2)}, u32[]{:S(2)}) collective-permute-start(bf16[128,3072]{1,0:T(8,128)(2,1)} %get-tuple-element.102), channel_id=1, source_target_pairs={{0,6},{1,7},{2,0},{3,1},{4,2},{5,3},{6,4},{7,5},{8,14},{9,15},{10,... | collective-permute-start | bytes 2359304 | tf_op jit(solution)/shard_map/ppermute | solution.py:478
  (59 other events, 255.9 us)
Sparse Core Ops, SparseCore 0:
  10.2 66.1 all-gather.2
  100.7 30.3 all-gather.4
  135.8 215.8 all-reduce.2

commit v4 on v3

--- a/solution.py
+++ b/solution.py
@@ -35,7 +35,7 @@
 HALF = D // 2
 EPS = 1e-06
 THETA = 10000.0
-VMEM = 60 * 1024 * 1024
+VMEM = 64 * 1024 * 1024 - 65536
 f32 = jnp.float32
 bf16 = jnp.bfloat16
 
@@ -50,6 +50,10 @@
 
 def iota(shape, dim):
     return lax.broadcasted_iota(jnp.int32, shape, dim)
+
+
+def twice(v):
+    return jnp.concatenate([v, v], axis=1)
 
 
 def swap_halves(v):
@@ -126,12 +130,11 @@
         rows = pl.ds(pl.multiple_of(owner_of(own, dz, dc) * ROWS, ROWS), ROWS)
         x = load().astype(f32)
         scale = lax.rsqrt(jnp.mean(x * x, axis=-1, keepdims=True) + EPS)
-        normed_ref[rows, :] = (x * scale * gain_ref[...]).astype(bf16)
-    for at in range(0, GROUP, 2 * BLK):
-        rows = pl.ds(at, 2 * BLK)
-        raw = mm(normed_ref[rows, :], w_ref[...])
+        normed = (x * scale * gain_ref[...]).astype(bf16)
+        normed_ref[rows, :] = normed
+        raw = mm(normed, w_ref[...])
         turned = raw[:, :BLK]
-        turned = turned * cos_ref[rows, :] + swap_halves(turned) * sin_ref[rows, :]
+        turned = turned * twice(cos_ref[rows, :]) + swap_halves(turned) * twice(sin_ref[rows, :])
         qkv_ref[rows, 0:BLK] = turned.astype(bf16)
         qkv_ref[rows, BLK:WW] = raw[:, BLK:WW].astype(bf16)
     for at in range(0, GROUP, BLK):
@@ -204,8 +207,8 @@
 
 def expert_kernel(own_ref, *refs):
     n_refs, refs = refs[:10], refs[10:]
-    w_ref, d_ref, slot_ref, wg_ref, wu_ref, wd_ref, gg_ref, gu_ref, gd_ref, hg_ref, hu_ref, inner_ref, gate_ref = refs[:13]
-    prob_ref, x_ref, n_ref = refs[13:]
+    w_ref, d_ref, slot_ref, wg_ref, wu_ref, wd_ref, grad_ref, hg_ref, hu_ref, inner_ref, gate_ref = refs[:11]
+    prob_ref, x_ref, n_ref = refs[11:]
     e = pl.program_id(0)
     own = own_ref[0] * EXP_DEV + e
 
@@ -240,15 +243,19 @@
     hu = (inner_grad * silu).astype(bf16)
     hg_ref[0] = hg
     hu_ref[0] = hu
-    gd_ref[0] = mm(inner, slot_grad, TN).astype(bf16)
+    down = mm(inner, slot_grad, TN).astype(bf16)
+    for c in range(3):
+        grad_ref[0, 2, c * FFE : (c + 1) * FFE, :] = down[:, c * FFE : (c + 1) * FFE]
     both = mm(x, jnp.concatenate([hg, hu], axis=1), TN)
-    gg_ref[0] = both[:, 0:FFE].astype(bf16)
-    gu_ref[0] = both[:, FFE : 2 * FFE].astype(bf16)
-
-
-def widen_kernel(*refs):
-    for in_ref, out_ref in zip(refs[:3], refs[3:]):
-        out_ref[...] = in_ref[...].astype(f32)
+    grad_ref[0, 0] = both[:, 0:FFE].astype(bf16)
+    grad_ref[0, 1] = both[:, FFE : 2 * FFE].astype(bf16)
+
+
+def widen_kernel(both_ref, down_part_ref, gate_ref, up_ref, down_ref):
+    gate_ref[0] = both_ref[0, 0].astype(f32)
+    up_ref[0] = both_ref[0, 1].astype(f32)
+    for c in range(3):
+        down_ref[0, :, c * FFE : (c + 1) * FFE] = down_part_ref[0, 0, c].astype(f32)
 
 
 def split_core(core, both):
@@ -381,7 +388,7 @@
     for at in range(0, GROUP, BLK):
         rows = pl.ds(at, BLK)
         turned = turn_ref[rows, :]
-        turned = turned * cos_ref[rows, :] - swap_halves(turned) * sin_ref[rows, :]
+        turned = turned * twice(cos_ref[rows, :]) - swap_halves(turned) * twice(sin_ref[rows, :])
         dqkv_ref[rows, 0:BLK] = turned.astype(bf16)
         dqkv_ref[rows, BLK : BLK + HD] = dv_ref[rows, :].astype(bf16)
         dqkv_ref[rows, BLK + HD : WW] = jnp.zeros((BLK, WW - BLK - HD), bf16)
@@ -424,7 +431,7 @@
 
 def sum_kernel(part_ref, after_ref, sum_ref):
     total = part_ref[0].astype(f32)
-    for s in range(1, DP):
+    for s in range(1, part_ref.shape[0]):
         total = total + part_ref[s].astype(f32)
     sum_ref[...] = jnp.broadcast_to(total.astype(bf16)[None], sum_ref.shape)
 
@@ -471,6 +478,8 @@
     return [(i, ((i // 2 + step) % 4) * 2 + i % 2) for i in range(OWN)]
 
 
+X_GROUPS = [[y, 4 + y, 8 + y, 12 + y] for y in range(4)]
+Y_GROUPS = [[4 * x + y for y in range(4)] for x in range(4)]
 UP, DOWN, SWAP = along_z(1), along_z(-1), [(i, i ^ 1) for i in range(OWN)]
 
 
@@ -539,13 +548,13 @@
     freq = jnp.exp(steps * (-2.0 * math.log(THETA) / HD))
     angles = (place - start).astype(f32)[:, None] * freq[None, :]
     cos_half, sin_half = jnp.cos(angles), jnp.sin(angles)
-    cos_t = jnp.tile(cos_half, (1, 8))
-    sin_t = jnp.tile(jnp.concatenate([-sin_half, sin_half], axis=1), (1, 4))
+    cos_t = jnp.tile(cos_half, (1, 4))
+    sin_t = jnp.tile(jnp.concatenate([-sin_half, sin_half], axis=1), (1, 2))
     start = start.reshape(GROUP, 1)
     x_ring = ring_rows(tokens)
-    x_ring[3] = gate(x_ring[3], cos_t, sin_t, start)
+    x_ring[1] = gate(x_ring[1], cos_t, sin_t, start, gain_one, gain_two)
     x_pieces = swap_rows(x_ring)
-    dy_rows = gate(rows, x_ring[1], x_ring[2])
+    dy_rows = rows
     dy_up, dy_down = move(dy_rows, UP), move(dy_rows, DOWN)
     dy_ring = [dy_rows, dy_up, dy_down, move(dy_up, UP)]
 
@@ -574,16 +583,15 @@
         in_specs=[SM] + [VM] * 8,
     )(own, *dy_pieces)
     n_pieces = swap_rows(ring_rows(normed_two, (slot_rows,)))
-    mix_flat = gate(mix_flat, n_pieces[3], n_pieces[4])
+    mix_flat = gate(mix_flat, n_pieces[1], n_pieces[2])
     mix_all = lax.all_gather(mix_flat, "expert", axis=0, tiled=True)
 
     whole = lambda *shape: pl.BlockSpec(shape, lambda e: (0,) * len(shape), pipeline_mode=pl.Buffered(1))
     each = lambda *shape: pl.BlockSpec((1,) + shape, lambda e: (e, 0, 0))
-    gg, gu, gd, hg, hu, inner, gates = call(
+    grads, hg, hu, inner, gates = call(
         expert_kernel,
         [
-            sds((EXP_DEV, D, FFE), bf16), sds((EXP_DEV, D, FFE), bf16), sds((EXP_DEV, FFE, D), bf16),
-            sds((EXP_DEV, SLOTS, FFE), bf16), sds((EXP_DEV, SLOTS, FFE), bf16), sds((EXP_DEV, SLOTS, FFE), bf16),
+            sds((EXP_DEV, 3, D, FFE), bf16), sds((EXP_DEV, SLOTS, FFE), bf16), sds((EXP_DEV, SLOTS, FFE), bf16), sds((EXP_DEV, SLOTS, FFE), bf16),
             sds((EXP_DEV, SLOTS, 1), f32),
         ],
         scratch=[
@@ -596,11 +604,12 @@
             each(D, FFE), each(D, FFE), each(FFE, D),
         ],
         out_specs=[
-            each(D, FFE), each(D, FFE), each(FFE, D), each(SLOTS, FFE), each(SLOTS, FFE), each(SLOTS, FFE), each(SLOTS, 1),
+            pl.BlockSpec((1, 3, D, FFE), lambda e: (e, 0, 0, 0)),
+            each(SLOTS, FFE), each(SLOTS, FFE), each(SLOTS, FFE), each(SLOTS, 1),
         ],
     )(own, *n_pieces, weights, d_slots, slot_rows, gate_weight, up_weight, down_weight)
 
-    gate_part, up_part, down_part = lax.psum((gate(gg, mix_all), gu, gd), "dp")
+    grad_sums = lax.psum(gate(grads, mix_all).reshape(EXP_DEV * 3 * D, FFE), "dp")
 
     dx_keep, dx_send, gated = call(
         return_kernel,
@@ -633,14 +642,20 @@
     pay = call(pay_kernel, sds((D, 640), bf16), cost=cost(1))(
         normed_one, dqkv, mix_all, got, normed_two, logit_grads, moe_gain, gain_one, weights
     )
-    pay_parts = lax.all_to_all(pay.reshape(DP, shard_rows, 640), "dp", 0, 0, tiled=True)
+    pay_parts = lax.all_to_all(pay.reshape(4, D // 4, 640), "dp", 0, 0, tiled=True, axis_index_groups=X_GROUPS)
     rows_keep, rows_send = call(
         tokens_kernel, [sds((PAIRS, ROWS, 2 * D), bf16)] * 2, cost=cost(0.1), in_specs=[SM] + [VM] * 4 + [ANY]
     )(own, gated, slot_rows, dqkv, weights, pay)
     rows_parts, rows_first = scatter_rows(rows_keep, rows_send)
+    pay_line = call(
+        sum_kernel, sds((1, D // 4, 640), bf16), cost=cost(0.1), in_specs=[VM, ANY]
+    )(pay_parts, rows_first)
+    pay_parts = lax.all_to_all(
+        pay_line.reshape(4, shard_rows, 640), "dp", 0, 0, tiled=True, axis_index_groups=Y_GROUPS
+    )
     pay_own = call(
-        sum_kernel, sds((OWN, shard_rows, 640), bf16), cost=cost(1), in_specs=[VM, ANY]
-    )(pay_parts, rows_first)
+        sum_kernel, sds((OWN, shard_rows, 640), bf16), cost=cost(0.1), in_specs=[VM, ANY]
+    )(pay_parts, pay_line)
     pay_all = lax.all_to_all(pay_own, "expert", 0, 0, tiled=True)
     query_total, key_total, value_total, out_total, router_total, gains = call(
         join_kernel,
@@ -659,9 +674,12 @@
         [sds((EXP_DEV, D, FFE), f32), sds((EXP_DEV, D, FFE), f32), sds((EXP_DEV, FFE, D), f32)],
         cost=cost(12),
         grid=(EXP_DEV, 2),
-        in_specs=widths,
+        in_specs=[
+            pl.BlockSpec((1, 2, D // 2, FFE), lambda e, h: (e, 0, h, 0)),
+            pl.BlockSpec((1, 1, 3, FFE // 2, FFE), lambda e, h: (e, 2, 0, h, 0)),
+        ],
         out_specs=widths,
-    )(gate_part, up_part, down_part)
+    )(grad_sums.reshape(EXP_DEV, 3, D, FFE), grad_sums.reshape(EXP_DEV, 3, 3, FFE, FFE))
     return (
         layer_out, input_grad, gain_attn, query_total, key_total, value_total, out_total, gain_moe, router_total,
         gate_total, up_total, down_total,

time: 379 us -> 366 us (0.966)
  waiting for transfers between devices: 111 us -> 96.2 us
  starting transfers between devices: 60.7 us -> 70.4 us
  local copies, waits for them, and re-layouts: 23.6 us -> 13.9 us
    psum x1, waiting for transfers between devices: 24 us -> 9.67 us  [body(): lax.psum(gate(grads, mix_all).reshape(EXP_DEV * 3 * D, FFE), 'dp')]
    unnamed x81 -> x15, local copies, waits for them, and re-layouts: 15.9 us -> 2.84 us
    ppermute x35, waiting for transfers between devices: 39.3 us -> 32.2 us  [move(): return lax.ppermute(value, 'expert', pairs)]
    all_to_all x1 -> x2, waiting for transfers between devices: 26.6 us -> 32.6 us  [the longest x1 24.2 us: body(): lax.all_to_all(pay.reshape(4, D // 4, 640), 'dp', 0, 0, tiled=True, axis_...]
    all_to_all x1, waiting for transfers between devices: 4.36 us -> 0.35 us  [body(): weights = lax.all_to_all(shard, 'dp', 0, 0, tiled=True).reshape(D, WW)]
    all_to_all x1 -> x2, starting transfers between devices: 4.63 us -> 8.62 us  [the longest x1 4.49 us: body(): lax.all_to_all(pay.reshape(4, D // 4, 640), 'dp', 0, 0, tiled=True, axis_...]
    pallas_call x2 -> x3, Pallas kernels: 27.5 us -> 30 us  [the longest x1 25.3 us: body(): call(expert_kernel, [sds((EXP_DEV, 3, D, FFE), bf16), sds((EXP_DEV, SLOTS...]
  transfers between devices with their start and end apart: 43 -> 44, of which waited for: 19 -> 20; matrix products, arithmetic and copies ran while one was open for 3% -> 4% of each run, Pallas kernels for 35% -> 36%
where the time goes in v4:
time: 366 us; the launch traced here: 361 us
  Pallas kernels  146 us (40%)
  waiting for transfers between devices  96.2 us (26%)
  starting transfers between devices  70.4 us (19%)
  between operations  15.5 us (4%)
  blocking collectives  15.3 us (4%)
  local copies, waits for them, and re-layouts  13.9 us (4%)
    ppermute x35, starting transfers between devices, move(): return lax.ppermute(value, 'expert', pairs)  37.9 us
    ppermute x35, waiting for transfers between devices, move(): return lax.ppermute(value, 'expert', pairs)  32.2 us
    pallas_call x1, Pallas kernels, body(): call(expert_kernel, [sds((EXP_DEV, 3, D, FFE), bf16), sds((EXP_DEV, SLOTS...  25.3 us
    all_to_all x1, waiting for transfers between devices, body(): lax.all_to_all(pay.reshape(4, D // 4, 640), 'dp', 0, 0, tiled=True, axis_...  24.2 us
    pallas_call x1, Pallas kernels, body(): call(return_kernel, [sds((PAIRS, ROWS, XW), bf16)] * 2 + [sds((EXP_DEV, S...  18.5 us
    all_to_all x1, blocking collectives, body(): lax.all_to_all(send, 'expert', 0, 0, tiled=True).reshape(GROUP, BLK)  15.3 us
    pallas_call x1, Pallas kernels, body(): call(widen_kernel, [sds((EXP_DEV, D, FFE), f32), sds((EXP_DEV, D, FFE), f...  15 us
    pallas_call x1, Pallas kernels, body(): call(attend_back_kernel, sds((GROUP, WW), bf16), scratch=[pltpu.VMEM((GRO...  12.3 us
  transfers between devices with their start and end apart: 44, of which 20 were waited for; matrix products, arithmetic and copies ran while one was open for 4% of the time, Pallas kernels for 36%

profile of v4, /device:TPU:1, one launch (start us, length us, event | category | flops | bytes accessed | tf_op | source)
XLA Modules:
  0.0 360.5 jit_solution(13125274803667320998)
XLA Ops:
  16.3 6.9 %all-to-all-start = ((bf16[16,96,384]{2,1,0:T(8,128)(2,1)}), bf16[16,96,384]{2,1,0:T(8,128)(2,1)}, u32[]{:S(2)}, u32[]{:S(2)}) async-start(bf16[16,96,384]{2,1,0:T(8,128)(2,1)} %get-tuple-element.63), calls=%async_computation | async-start | bytes 2359296 | tf_op jit(solution)/shard_map/all_to_all | solution.py:541
  47.7 11.8 %shard_map.231 = (bf16[1024,1536]{1,0:T(8,128)(2,1)}, bf16[1024,384]{1,0:T(8,128)(2,1)}, bf16[8,128,256]{2,1,0:T(8,128)(2,1)}, f32[1024,8]{1,0:T(8,128)}) custom-call(s32[1]{0:T(128)} %bitcast.own_ref, bf16[128,1536]{1,0:T(8,128)(2,1)} %x_ref.3, bf16[128,1536]{1,0:T(8,128)(2,1)} %shard_map.229.refs_1_, bf16[128,1536]{1,0:T(8,128)(2,1)} %collective-permute-done.1.refs_2_, ...), custom_call_target="tpu_custom_call" | custom-call | flops 13799999488 | bytes 1024 | tf_op jit(solution)/shard_map/pallas_call | solution.py:564
  60.0 5.1 %all-to-all-start.1 = ((bf16[8,128,256]{2,1,0:T(8,128)(2,1)}), bf16[8,128,256]{2,1,0:T(8,128)(2,1)}, u32[]{:S(2)}, u32[]{:S(2)}) async-start(bf16[8,128,256]{2,1,0:T(8,128)(2,1)} %shard_map.232), calls=%async_computation.1 | async-start | bytes 1048576 | tf_op jit(solution)/shard_map/all_to_all | solution.py:571
  66.1 8.6 %all-to-all-done.1.mix_ref = bf16[8,128,256]{2,1,0:T(8,128)(2,1)} async-done(((bf16[8,128,256]{2,1,0:T(8,128)(2,1)}), bf16[8,128,256]{2,1,0:T(8,128)(2,1)}, u32[]{:S(2)}, u32[]{:S(2)}) %all-to-all-start.1) | async-done | bytes 524320 | tf_op jit(solution)/shard_map/all_to_all | solution.py:571
  76.5 4.5 %shard_map.233 = (f32[128,1536]{1,0:T(8,128)}, bf16[128,1536]{1,0:T(8,128)(2,1)}, bf16[128,1536]{1,0:T(8,128)(2,1)}) custom-call(bf16[8,128,256]{2,1,0:T(8,128)(2,1)} %all-to-all-done.1.mix_ref, bf16[1536,1536]{1,0:T(8,128)(2,1)} %all-gather.3.cloned.1.call-done.wo_ref, bf16[128,1536]{1,0:T(8,128)(2,1)} %x_ref.3, f32[1,1536]{1,0:T(1,128)} %reshape.129.refs_4_.gain_ref), custom_call_target="tpu_custom_call" | custom-call | flops 4600000000 | bytes 1024 | tf_op jit(solution)/shard_map/pallas_call | solution.py:573
  83.8 6.0 %shard_map.234 = (s32[3,8,1024]{2,1,0:T(8,128)}, bf16[3,448,1536]{2,1,0:T(8,128)(2,1)}) custom-call(s32[1]{0:T(128)} %bitcast.own_ref, bf16[128,1664]{1,0:T(8,128)(2,1)} %get-tuple-element.65.refs_0_, bf16[128,1664]{1,0:T(8,128)(2,1)} %collective-permute-done.10.refs_1_, bf16[128,1664]{1,0:T(8,128)(2,1)} %collective-permute-done.9.refs_0_.refs_2_, ...), custom_call_target="tpu_custom_call" | custom-call | flops 6899999744 | bytes 1024 | tf_op jit(solution)/shard_map/pallas_call | solution.py:578
  108.1 25.3 %shard_map.236 = (bf16[3,3,1536,512]{3,2,1,0:T(8,128)(2,1)}, bf16[3,448,512]{2,1,0:T(8,128)(2,1)}, bf16[3,448,512]{2,1,0:T(8,128)(2,1)}, bf16[3,448,512]{2,1,0:T(8,128)(2,1)}, f32[3,448,1]{2,1,0:T(8,128)}) custom-call(s32[1]{0:T(128)} %bitcast.own_ref, bf16[128,1536]{1,0:T(8,128)(2,1)} %get-tuple-element.66.refs_0_.normed_ref.n_ref, ...), custom_call_target="tpu_custom_call" | custom-call | flops 32199999488 | bytes 1024 | tf_op jit(solution)/shard_map/pallas_call | solution.py:591
  133.6 18.5 %shard_map.237 = (bf16[4,128,1664]{2,1,0:T(8,128)(2,1)}, bf16[4,128,1664]{2,1,0:T(8,128)(2,1)}, bf16[3,448,1536]{2,1,0:T(8,128)(2,1)}) custom-call(s32[1]{0:T(128)} %bitcast.own_ref, bf16[3,448,512]{2,1,0:T(8,128)(2,1)} %get-tuple-element.69.hg_ref, bf16[3,448,512]{2,1,0:T(8,128)(2,1)} %get-tuple-element.70.hu_ref, ...), custom_call_target="tpu_custom_call" | custom-call | flops 1150000000 | bytes 1024 | tf_op jit(solution)/shard_map/pallas_call | solution.py:614
  162.5 5.8 %collective-permute-done.26.up_ref = bf16[64,1664]{1,0:T(8,128)(2,1)} collective-permute-done((bf16[64,1664]{1,0:T(8,128)(2,1)}, bf16[64,1664]{1,0:T(8,128)(2,1)}, u32[]{:S(2)}, u32[]{:S(2)}) %collective-permute-start.26) | collective-permute-done | bytes 213024 | tf_op jit(solution)/shard_map/ppermute | solution.py:487
  173.6 9.3 %collective-permute-done.28.part_b = bf16[128,1664]{1,0:T(8,128)(2,1)} collective-permute-done((bf16[128,1664]{1,0:T(8,128)(2,1)}, bf16[128,1664]{1,0:T(8,128)(2,1)}, u32[]{:S(2)}, u32[]{:S(2)}) %collective-permute-start.28) | collective-permute-done | bytes 426016 | tf_op jit(solution)/shard_map/ppermute | solution.py:487
  183.0 7.4 %shard_map.240 = (f32[128,1536]{1,0:T(8,128)}, f32[1,1536]{1,0:T(1,128)}, bf16[8,128,256]{2,1,0:T(8,128)(2,1)}, bf16[8,128,256]{2,1,0:T(8,128)(2,1)}, bf16[2,128,128]{2,1,0:T(8,128)(2,1)}) custom-call(bf16[128,1664]{1,0:T(8,128)(2,1)} %get-tuple-element.78.part_a, bf16[128,1664]{1,0:T(8,128)(2,1)} %collective-permute-done.28.part_b, ...), custom_call_target="tpu_custom_call" | custom-call | flops 1150000000 | bytes 1024 | tf_op jit(solution)/shard_map/pallas_call | solution.py:628
  190.4 15.3 %all_to_all.35 = bf16[8,128,256]{2,1,0:T(8,128)(2,1)} all-to-all(bf16[8,128,256]{2,1,0:T(8,128)(2,1)} %get-tuple-element.86), channel_id=1, replica_groups=mesh['dp'=16,'expert'=8] {'expert'}, dimensions={0} | all-to-all | bytes 1048576 | tf_op jit(solution)/shard_map/all_to_all | solution.py:634
  205.7 5.1 %all-to-all-start.3 = ((bf16[8,128,256]{2,1,0:T(8,128)(2,1)}), bf16[8,128,256]{2,1,0:T(8,128)(2,1)}, u32[]{:S(2)}, u32[]{:S(2)}) async-start(bf16[8,128,256]{2,1,0:T(8,128)(2,1)} %get-tuple-element.89), calls=%async_computation.3 | async-start | bytes 1048576 | tf_op jit(solution)/shard_map/all_to_all | solution.py:635
  210.8 12.3 %shard_map.241.dqkv_ref = bf16[1024,384]{1,0:T(8,128)(2,1)} custom-call(bf16[1024,384]{1,0:T(8,128)(2,1)} %get-tuple-element.74.qkv_ref, f32[1024,8]{1,0:T(8,128)} %get-tuple-element.75.log_ref, bf16[1024,256]{1,0:T(8,128)(2,1)} %bitcast.20, f32[1024,128]{1,0:T(8,128)} %copy.32.refs_0_.refs_12_.cos_ref, f32[1024,128]{1,0:T(8,128)} %copy.33.refs_1_.refs_13_.sin_ref, ...), custom_call_target="tpu_custom_call" | custom-call | flops 13799999488 | bytes 1024 | tf_op jit(solution)/shard_map/pallas_call | solution.py:636
  223.1 8.9 %shard_map.243.after_ref = bf16[1536,640]{1,0:T(8,128)(2,1)} custom-call(bf16[1024,1536]{1,0:T(8,128)(2,1)} %get-tuple-element.87.normed_ref, bf16[1024,384]{1,0:T(8,128)(2,1)} %shard_map.241.dqkv_ref, bf16[1024,1536]{1,0:T(8,128)(2,1)} %all-gather.5.cloned.1.call-done.mix_ref.refs_0_, bf16[1024,256]{1,0:T(8,128)(2,1)} %bitcast.9.got_ref, ...), custom_call_target="tpu_custom_call" | custom-call | flops 1150000000 | bytes 1024 | tf_op jit(solution)/shard_map/pallas_call | solution.py:642
  232.0 9.0 %shard_map.244 = (bf16[4,128,3072]{2,1,0:T(8,128)(2,1)}, bf16[4,128,3072]{2,1,0:T(8,128)(2,1)}) custom-call(s32[1]{0:T(128)} %bitcast.own_ref, bf16[3,448,1536]{2,1,0:T(8,128)(2,1)} %get-tuple-element.73.gated_ref, s32[3,8,1024]{2,1,0:T(8,128)} %get-tuple-element.67.refs_0_.refs_12_.slot_ref, bf16[1024,384]{1,0:T(8,128)(2,1)} %shard_map.241.dqkv_ref, ...), custom_call_target="tpu_custom_call" | custom-call | flops 115000000 | bytes 1024 | tf_op jit(solution)/shard_map/pallas_call | solution.py:646
  241.2 4.5 %all-to-all-start.4 = ((bf16[4,384,640]{2,1,0:T(8,128)(2,1)}), bf16[4,384,640]{2,1,0:T(8,128)(2,1)}, u32[]{:S(2)}, u32[]{:S(2)}) async-start(bf16[4,384,640]{2,1,0:T(8,128)(2,1)} %bitcast.16), calls=%async_computation.4 | async-start | bytes 3932160 | tf_op jit(solution)/shard_map/all_to_all | solution.py:645
  247.0 4.7 %shard_map.245 = (bf16[128,3072]{1,0:T(8,128)(2,1)}, bf16[128,3072]{1,0:T(8,128)(2,1)}, bf16[128,3072]{1,0:T(8,128)(2,1)}, bf16[64,3072]{1,0:T(8,128)(2,1)}, bf16[64,3072]{1,0:T(8,128)(2,1)}) custom-call(bf16[4,128,3072]{2,1,0:T(8,128)(2,1)} %get-tuple-element.92.keep_ref, bf16[4,128,3072]{2,1,0:T(8,128)(2,1)} %collective-permute-done.30.got_ref), custom_call_target="tpu_custom_call" | custom-call | flops 115000000 | bytes 1024 | tf_op jit(solution)/shard_map/pallas_call | solution.py:518
  254.5 24.2 %all-to-all-done.4.part_ref = bf16[4,384,640]{2,1,0:T(8,128)(2,1)} async-done(((bf16[4,384,640]{2,1,0:T(8,128)(2,1)}), bf16[4,384,640]{2,1,0:T(8,128)(2,1)}, u32[]{:S(2)}, u32[]{:S(2)}) %all-to-all-start.4) | async-done | bytes 1966112 | tf_op jit(solution)/shard_map/all_to_all | solution.py:645
  291.5 8.3 %all-to-all-done.5.part_ref = bf16[4,96,640]{2,1,0:T(8,128)(2,1)} async-done(((bf16[4,96,640]{2,1,0:T(8,128)(2,1)}), bf16[4,96,640]{2,1,0:T(8,128)(2,1)}, u32[]{:S(2)}, u32[]{:S(2)}) %all-to-all-start.5) | async-done | bytes 491552 | tf_op jit(solution)/shard_map/all_to_all | solution.py:653
  301.9 6.6 %all-to-all-start.6 = ((bf16[8,96,640]{2,1,0:T(8,128)(2,1)}), bf16[8,96,640]{2,1,0:T(8,128)(2,1)}, u32[]{:S(2)}, u32[]{:S(2)}) async-start(bf16[8,96,640]{2,1,0:T(8,128)(2,1)} %shard_map.249), calls=%async_computation.6 | async-start | bytes 1966080 | tf_op jit(solution)/shard_map/all_to_all | solution.py:659
  312.7 10.2 %all-to-all-done.6.part_ref = bf16[8,96,640]{2,1,0:T(8,128)(2,1)} async-done(((bf16[8,96,640]{2,1,0:T(8,128)(2,1)}), bf16[8,96,640]{2,1,0:T(8,128)(2,1)}, u32[]{:S(2)}, u32[]{:S(2)}) %all-to-all-start.6) | async-done | bytes 983072 | tf_op jit(solution)/shard_map/all_to_all | solution.py:659
  329.1 9.7 %all-reduce.2.cloned.1.call-done = bf16[13824,512]{1,0:T(8,128)(2,1)} async-done(((bf16[13824,512]{1,0:T(8,128)(2,1)}), bf16[13824,512]{1,0:T(8,128)(2,1)}) %all-reduce.2.cloned.1.call-update) | async-done | bytes 14155792 | tf_op jit(solution)/shard_map/psum | solution.py:612
  338.8 15.0 %shard_map.252 = (f32[3,1536,512]{2,1,0:T(8,128)}, f32[3,1536,512]{2,1,0:T(8,128)}, f32[3,512,1536]{2,1,0:T(8,128)}) custom-call(bf16[3,3,1536,512]{3,2,1,0:T(8,128)(2,1)} %bitcast.21, bf16[3,3,3,512,512]{4,3,2,1,0:T(8,128)(2,1)} %bitcast.22), custom_call_target="tpu_custom_call" | custom-call | flops 13799999488 | bytes 1024 | tf_op jit(solution)/shard_map/pallas_call | solution.py:672
  (126 shorter events, 101.6 us)
Async XLA Ops:
  7.2 69.4 %all-gather.3.cloned.1.call-start = ((), (), s32[]{:S(2)}) async-start(), calls=%async_computation.7 | async-start | bytes 5013504 | tf_op jit(solution)/shard_map/all_gather | solution.py:542
  7.9 24.1 %collective-permute-start = (bf16[128,1536]{1,0:T(8,128)(2,1)}, bf16[128,1536]{1,0:T(8,128)(2,1)}, u32[]{:S(2)}, u32[]{:S(2)}) collective-permute-start(bf16[128,1536]{1,0:T(8,128)(2,1)} %x_ref.3), channel_id=1, source_target_pairs={{0,2},{1,3},{2,4},{3,5},{4,6},{5,7},{6,0},{7,1},{8,10},{9,11},{10,... | collective-permute-start | bytes 1179656 | tf_op jit(solution)/shard_map/ppermute | solution.py:487
  10.4 25.2 %collective-permute-start.1 = (bf16[128,1536]{1,0:T(8,128)(2,1)}, bf16[128,1536]{1,0:T(8,128)(2,1)}, u32[]{:S(2)}, u32[]{:S(2)}) collective-permute-start(bf16[128,1536]{1,0:T(8,128)(2,1)} %x_ref.3), channel_id=1, source_target_pairs={{0,6},{1,7},{2,0},{3,1},{4,2},{5,3},{6,4},{7,5},{8,14},{9,15},{10,... | collective-permute-start | bytes 1179656 | tf_op jit(solution)/shard_map/ppermute | solution.py:487
  12.7 24.0 %collective-permute-start.4 = (bf16[128,1536]{1,0:T(8,128)(2,1)}, bf16[128,1536]{1,0:T(8,128)(2,1)}, u32[]{:S(2)}, u32[]{:S(2)}) collective-permute-start(bf16[128,1536]{1,0:T(8,128)(2,1)} %x_ref.3), channel_id=1, source_target_pairs={{0,1},{1,0},{2,3},{3,2},{4,5},{5,4},{6,7},{7,6},{8,9},{9,8},{10,11... | collective-permute-start | bytes 1179656 | tf_op jit(solution)/shard_map/ppermute | solution.py:487
  16.3 31.4 %all-to-all-start = ((bf16[16,96,384]{2,1,0:T(8,128)(2,1)}), bf16[16,96,384]{2,1,0:T(8,128)(2,1)}, u32[]{:S(2)}, u32[]{:S(2)}) async-start(bf16[16,96,384]{2,1,0:T(8,128)(2,1)} %get-tuple-element.63), calls=%async_computation | async-start | bytes 2359296 | tf_op jit(solution)/shard_map/all_to_all | solution.py:541
  23.3 21.5 %collective-permute-start.10 = (bf16[128,1664]{1,0:T(8,128)(2,1)}, bf16[128,1664]{1,0:T(8,128)(2,1)}, u32[]{:S(2)}, u32[]{:S(2)}) collective-permute-start(bf16[128,1664]{1,0:T(8,128)(2,1)} %get-tuple-element.65.refs_0_), channel_id=1, source_target_pairs={{0,2},{1,3},{2,4},{3,5},{4,6},{5,7},{6,0},{7,1},{8,10},{9,11},{10,... | collective-permute-start | bytes 1277960 | tf_op jit(solution)/shard_map/ppermute | solution.py:487
  44.7 14.8 %collective-permute-start.9 = (bf16[128,1664]{1,0:T(8,128)(2,1)}, bf16[128,1664]{1,0:T(8,128)(2,1)}, u32[]{:S(2)}, u32[]{:S(2)}) collective-permute-start(bf16[128,1664]{1,0:T(8,128)(2,1)} %get-tuple-element.65.refs_0_), channel_id=1, source_target_pairs={{0,6},{1,7},{2,0},{3,1},{4,2},{5,3},{6,4},{7,5},{8,14},{9,15},{10,... | collective-permute-start | bytes 1277960 | tf_op jit(solution)/shard_map/ppermute | solution.py:487
  47.2 12.8 %collective-permute-start.11 = (bf16[128,1664]{1,0:T(8,128)(2,1)}, bf16[128,1664]{1,0:T(8,128)(2,1)}, u32[]{:S(2)}, u32[]{:S(2)}) collective-permute-start(bf16[128,1664]{1,0:T(8,128)(2,1)} %collective-permute-done.10.refs_1_), channel_id=1, source_target_pairs={{0,2},{1,3},{2,4},{3,5},{4,6},{5,7},{6,0},{7,1},{8,10},{9,11},{10,... | collective-permute-start | bytes 1277960 | tf_op jit(solution)/shard_map/ppermute | solution.py:487
  60.0 14.7 %all-to-all-start.1 = ((bf16[8,128,256]{2,1,0:T(8,128)(2,1)}), bf16[8,128,256]{2,1,0:T(8,128)(2,1)}, u32[]{:S(2)}, u32[]{:S(2)}) async-start(bf16[8,128,256]{2,1,0:T(8,128)(2,1)} %shard_map.232), calls=%async_computation.1 | async-start | bytes 1048576 | tf_op jit(solution)/shard_map/all_to_all | solution.py:571
  65.1 68.4 %all-gather.5.cloned.1.call-start = ((), (), s32[]{:S(2)}) async-start(), calls=%async_computation.8 | async-start | bytes 3538944 | tf_op jit(solution)/shard_map/all_gather | solution.py:587
  65.1 17.2 %collective-permute-start.13 = (bf16[128,1664]{1,0:T(8,128)(2,1)}, bf16[128,1664]{1,0:T(8,128)(2,1)}, u32[]{:S(2)}, u32[]{:S(2)}) collective-permute-start(bf16[128,1664]{1,0:T(8,128)(2,1)} %get-tuple-element.65.refs_0_), channel_id=1, source_target_pairs={{0,1},{1,0},{2,3},{3,2},{4,5},{5,4},{6,7},{7,6},{8,9},{9,8},{10,11... | collective-permute-start | bytes 1277960 | tf_op jit(solution)/shard_map/ppermute | solution.py:487
  65.4 18.5 %collective-permute-start.14 = (bf16[128,1664]{1,0:T(8,128)(2,1)}, bf16[128,1664]{1,0:T(8,128)(2,1)}, u32[]{:S(2)}, u32[]{:S(2)}) collective-permute-start(bf16[128,1664]{1,0:T(8,128)(2,1)} %collective-permute-done.10.refs_1_), channel_id=1, source_target_pairs={{0,1},{1,0},{2,3},{3,2},{4,5},{5,4},{6,7},{7,6},{8,9},{9,8},{10,11... | collective-permute-start | bytes 1277960 | tf_op jit(solution)/shard_map/ppermute | solution.py:487
  65.6 18.2 %collective-permute-start.15 = (bf16[128,1664]{1,0:T(8,128)(2,1)}, bf16[128,1664]{1,0:T(8,128)(2,1)}, u32[]{:S(2)}, u32[]{:S(2)}) collective-permute-start(bf16[128,1664]{1,0:T(8,128)(2,1)} %collective-permute-done.9.refs_0_.refs_2_), channel_id=1, source_target_pairs={{0,1},{1,0},{2,3},{3,2},{4,5},{5,4},{6,7},{7,6},{8,9},{9,8},{10,11... | collective-permute-start | bytes 1277960 | tf_op jit(solution)/shard_map/ppermute | solution.py:487
  65.9 18.0 %collective-permute-start.16 = (bf16[128,1664]{1,0:T(8,128)(2,1)}, bf16[128,1664]{1,0:T(8,128)(2,1)}, u32[]{:S(2)}, u32[]{:S(2)}) collective-permute-start(bf16[128,1664]{1,0:T(8,128)(2,1)} %collective-permute-done.11.refs_1_.refs_3_), channel_id=1, source_target_pairs={{0,1},{1,0},{2,3},{3,2},{4,5},{5,4},{6,7},{7,6},{8,9},{9,8},{10,11... | collective-permute-start | bytes 1277960 | tf_op jit(solution)/shard_map/ppermute | solution.py:487
  92.6 246.1 %all-reduce.2.cloned.1.call-start = ((), (), s32[]{:S(2)}) async-start(), calls=%async_computation.9 | async-start | bytes 28311552 | tf_op jit(solution)/shard_map/psum | solution.py:612
  92.7 13.7 %collective-permute-start.20 = (bf16[128,1536]{1,0:T(8,128)(2,1)}, bf16[128,1536]{1,0:T(8,128)(2,1)}, u32[]{:S(2)}, u32[]{:S(2)}) collective-permute-start(bf16[128,1536]{1,0:T(8,128)(2,1)} %get-tuple-element.66.refs_0_.normed_ref.n_ref), channel_id=1, source_target_pairs={{0,1},{1,0},{2,3},{3,2},{4,5},{5,4},{6,7},{7,6},{8,9},{9,8},{10,11... | collective-permute-start | bytes 1179656 | tf_op jit(solution)/shard_map/ppermute | solution.py:487
  205.7 17.3 %all-to-all-start.3 = ((bf16[8,128,256]{2,1,0:T(8,128)(2,1)}), bf16[8,128,256]{2,1,0:T(8,128)(2,1)}, u32[]{:S(2)}, u32[]{:S(2)}) async-start(bf16[8,128,256]{2,1,0:T(8,128)(2,1)} %get-tuple-element.89), calls=%async_computation.3 | async-start | bytes 1048576 | tf_op jit(solution)/shard_map/all_to_all | solution.py:635
  241.2 37.5 %all-to-all-start.4 = ((bf16[4,384,640]{2,1,0:T(8,128)(2,1)}), bf16[4,384,640]{2,1,0:T(8,128)(2,1)}, u32[]{:S(2)}, u32[]{:S(2)}) async-start(bf16[4,384,640]{2,1,0:T(8,128)(2,1)} %bitcast.16), calls=%async_computation.4 | async-start | bytes 3932160 | tf_op jit(solution)/shard_map/all_to_all | solution.py:645
  251.8 33.6 %collective-permute-start.31 = (bf16[64,3072]{1,0:T(8,128)(2,1)}, bf16[64,3072]{1,0:T(8,128)(2,1)}, u32[]{:S(2)}, u32[]{:S(2)}) collective-permute-start(bf16[64,3072]{1,0:T(8,128)(2,1)} %get-tuple-element.97.after_ref), channel_id=1, source_target_pairs={{0,2},{1,3},{2,4},{3,5},{4,6},{5,7},{6,0},{7,1},{8,10},{9,11},{10,... | collective-permute-start | bytes 1179656 | tf_op jit(solution)/shard_map/ppermute | solution.py:487
  253.2 32.3 %collective-permute-start.32 = (bf16[64,3072]{1,0:T(8,128)(2,1)}, bf16[64,3072]{1,0:T(8,128)(2,1)}, u32[]{:S(2)}, u32[]{:S(2)}) collective-permute-start(bf16[64,3072]{1,0:T(8,128)(2,1)} %get-tuple-element.98), channel_id=1, source_target_pairs={{0,6},{1,7},{2,0},{3,1},{4,2},{5,3},{6,4},{7,5},{8,14},{9,15},{10,... | collective-permute-start | bytes 1179656 | tf_op jit(solution)/shard_map/ppermute | solution.py:487
  281.3 18.5 %all-to-all-start.5 = ((bf16[4,96,640]{2,1,0:T(8,128)(2,1)}), bf16[4,96,640]{2,1,0:T(8,128)(2,1)}, u32[]{:S(2)}, u32[]{:S(2)}) async-start(bf16[4,96,640]{2,1,0:T(8,128)(2,1)} %bitcast.17), calls=%async_computation.5 | async-start | bytes 983040 | tf_op jit(solution)/shard_map/all_to_all | solution.py:653
  288.4 20.2 %collective-permute-start.33 = (bf16[128,3072]{1,0:T(8,128)(2,1)}, bf16[128,3072]{1,0:T(8,128)(2,1)}, u32[]{:S(2)}, u32[]{:S(2)}) collective-permute-start(bf16[128,3072]{1,0:T(8,128)(2,1)} %get-tuple-element.99), channel_id=1, source_target_pairs={{0,2},{1,3},{2,4},{3,5},{4,6},{5,7},{6,0},{7,1},{8,10},{9,11},{10,... | collective-permute-start | bytes 2359304 | tf_op jit(solution)/shard_map/ppermute | solution.py:487
  290.1 18.5 %collective-permute-start.34 = (bf16[128,3072]{1,0:T(8,128)(2,1)}, bf16[128,3072]{1,0:T(8,128)(2,1)}, u32[]{:S(2)}, u32[]{:S(2)}) collective-permute-start(bf16[128,3072]{1,0:T(8,128)(2,1)} %get-tuple-element.100), channel_id=1, source_target_pairs={{0,6},{1,7},{2,0},{3,1},{4,2},{5,3},{6,4},{7,5},{8,14},{9,15},{10,... | collective-permute-start | bytes 2359304 | tf_op jit(solution)/shard_map/ppermute | solution.py:487
  301.9 21.1 %all-to-all-start.6 = ((bf16[8,96,640]{2,1,0:T(8,128)(2,1)}), bf16[8,96,640]{2,1,0:T(8,128)(2,1)}, u32[]{:S(2)}, u32[]{:S(2)}) async-start(bf16[8,96,640]{2,1,0:T(8,128)(2,1)} %shard_map.249), calls=%async_computation.6 | async-start | bytes 1966080 | tf_op jit(solution)/shard_map/all_to_all | solution.py:659
  (27 other events, 193.1 us)
Sparse Core Ops, SparseCore 0:
  10.2 66.2 all-gather.2
  92.7 28.8 all-gather.4
  133.7 205.0 all-reduce.1

commit v5 on v4

--- a/solution.py
+++ b/solution.py
@@ -168,7 +168,7 @@
 
 
 def router_probs(normed, w_ref):
-    logits = mm(normed, w_ref[:, BLK:WW])
+    logits = mm(normed, w_ref[:, -128:])
     lane = iota(logits.shape, 1)
     real = (lane >= HD) & (lane < HD + EXPERTS)
     logits = jnp.where(real, logits, -1e30)
@@ -251,11 +251,52 @@
     grad_ref[0, 1] = both[:, FFE : 2 * FFE].astype(bf16)
 
 
-def widen_kernel(both_ref, down_part_ref, gate_ref, up_ref, down_ref):
-    gate_ref[0] = both_ref[0, 0].astype(f32)
-    up_ref[0] = both_ref[0, 1].astype(f32)
-    for c in range(3):
-        down_ref[0, :, c * FFE : (c + 1) * FFE] = down_part_ref[0, 0, c].astype(f32)
+def widen_kernel(part_ref, gate_ref, up_ref, down_ref, in_buf, out_buf, in_sems, out_sems):
+    slots, long = in_buf.shape[0], D // 2
+
+    def moves(n):
+        e, m, h = n // 6, n // 2 % 3, n % 2
+        s = n % slots
+        if m < 2:
+            rows = pl.ds(h * long, long)
+            out_ref = (gate_ref, up_ref)[m]
+            return (
+                [pltpu.make_async_copy(part_ref.at[e, m, rows, :], in_buf.at[s], in_sems.at[s, 0])],
+                [pltpu.make_async_copy(out_buf.at[s], out_ref.at[e, rows, :], out_sems.at[s, 0])],
+            )
+        size = FFE // 2
+        ins, outs = [], []
+        for c in range(3):
+            here, rows = pl.ds(c * size, size), pl.ds(c * FFE + h * size, size)
+            ins.append(pltpu.make_async_copy(part_ref.at[e, m, rows, :], in_buf.at[s, here, :], in_sems.at[s, c]))
+            outs.append(
+                pltpu.make_async_copy(
+                    out_buf.at[s, here, :],
+                    down_ref.at[e, pl.ds(h * size, size), pl.ds(c * FFE, FFE)],
+                    out_sems.at[s, c],
+                )
+            )
+        return ins, outs
+
+    steps = [moves(n) for n in range(6 * EXP_DEV)]
+    for ins, _ in steps[: slots - 1]:
+        for copy in ins:
+            copy.start()
+    for n, (ins, outs) in enumerate(steps):
+        if n + slots - 1 < len(steps):
+            for copy in steps[n + slots - 1][0]:
+                copy.start()
+        for copy in ins:
+            copy.wait()
+        if n >= slots:
+            for copy in steps[n - slots][1]:
+                copy.wait()
+        out_buf[n % slots] = in_buf[n % slots].astype(f32)
+        for copy in outs:
+            copy.start()
+    for _, outs in steps[-slots:]:
+        for copy in outs:
+            copy.wait()
 
 
 def split_core(core, both):
@@ -396,10 +437,9 @@
 
 def pay_kernel(normed_ref, dqkv_ref, mix_ref, got_ref, n_ref, logit_ref, moe_gain_ref, norm_ref, w_ref, pay_ref):
     left = mm(normed_ref[...], dqkv_ref[:, 0:BLK], TN)
-    pay_ref[:, 0:BLK] = left.astype(bf16)
     value = mm(normed_ref[...], dqkv_ref[:, BLK:WW], TN)
     out = mm(mix_ref[...], got_ref[...], TN)
-    pay_ref[:, BLK : 2 * BLK] = (jnp.concatenate([value, jnp.zeros((D, 128), f32)], axis=1) + out).astype(bf16)
+    middle = jnp.concatenate([value, jnp.zeros((D, 128), f32)], axis=1) + out
     router = mm(n_ref[...], logit_ref[0], TN) + mm(n_ref[...], logit_ref[1], TN)
     attn_gain = jnp.sum(left * w_ref[:, 0:BLK].astype(f32), axis=1, keepdims=True)
     attn_gain = attn_gain + jnp.sum(value * w_ref[:, BLK:WW].astype(f32), axis=1, keepdims=True)
@@ -413,8 +453,10 @@
         part = slice(i * rows, (i + 1) * rows)
         both = jnp.where(lane == i, attn_gain[part], jnp.where(lane == DP + i, moe_gain[part], both))
     for i in range(DP):
-        part = slice(i * rows, (i + 1) * rows)
-        pay_ref[part, 2 * BLK : 2 * BLK + 128] = jnp.where(lane >= HD, router[part], both).astype(bf16)
+        part, at = slice(i * rows, (i + 1) * rows), ((i % 4) * 4 + i // 4) * rows
+        pay_ref[at : at + rows, 0:BLK] = left[part].astype(bf16)
+        pay_ref[at : at + rows, BLK : 2 * BLK] = middle[part].astype(bf16)
+        pay_ref[at : at + rows, 2 * BLK : 2 * BLK + 128] = jnp.where(lane >= HD, router[part], both).astype(bf16)
 
 
 def input_kernel(part_a, part_b, part_c, x_ref, gain_ref, hidden_grad_ref, hidden_ref, out_ref, layer_ref):
@@ -587,6 +629,7 @@
     mix_all = lax.all_gather(mix_flat, "expert", axis=0, tiled=True)
 
     whole = lambda *shape: pl.BlockSpec(shape, lambda e: (0,) * len(shape), pipeline_mode=pl.Buffered(1))
+    tile = pl.BlockSpec((D, 128), lambda e: (0, 2), pipeline_mode=pl.Buffered(1))
     each = lambda *shape: pl.BlockSpec((1,) + shape, lambda e: (e, 0, 0))
     grads, hg, hu, inner, gates = call(
         expert_kernel,
@@ -600,7 +643,7 @@
         cost=cost(28),
         grid=(EXP_DEV,),
         in_specs=[
-            SM, *[whole(*p.shape) for p in n_pieces], whole(D, WW), each(SLOTS, D), each(8, GROUP),
+            SM, *[whole(*p.shape) for p in n_pieces], tile, each(SLOTS, D), each(8, GROUP),
             each(D, FFE), each(D, FFE), each(FFE, D),
         ],
         out_specs=[
@@ -642,7 +685,7 @@
     pay = call(pay_kernel, sds((D, 640), bf16), cost=cost(1))(
         normed_one, dqkv, mix_all, got, normed_two, logit_grads, moe_gain, gain_one, weights
     )
-    pay_parts = lax.all_to_all(pay.reshape(4, D // 4, 640), "dp", 0, 0, tiled=True, axis_index_groups=X_GROUPS)
+    pay_parts = lax.all_to_all(pay.reshape(4, D // 4, 640), "dp", 0, 0, tiled=True, axis_index_groups=Y_GROUPS)
     rows_keep, rows_send = call(
         tokens_kernel, [sds((PAIRS, ROWS, 2 * D), bf16)] * 2, cost=cost(0.1), in_specs=[SM] + [VM] * 4 + [ANY]
     )(own, gated, slot_rows, dqkv, weights, pay)
@@ -651,7 +694,7 @@
         sum_kernel, sds((1, D // 4, 640), bf16), cost=cost(0.1), in_specs=[VM, ANY]
     )(pay_parts, rows_first)
     pay_parts = lax.all_to_all(
-        pay_line.reshape(4, shard_rows, 640), "dp", 0, 0, tiled=True, axis_index_groups=Y_GROUPS
+        pay_line.reshape(4, shard_rows, 640), "dp", 0, 0, tiled=True, axis_index_groups=X_GROUPS
     )
     pay_own = call(
         sum_kernel, sds((OWN, shard_rows, 640), bf16), cost=cost(0.1), in_specs=[VM, ANY]
@@ -667,19 +710,17 @@
     input_grad, layer_out = call(input_kernel, [sds((ROWS, D), bf16)] * 2, cost=cost(1))(
         *rows_parts, tokens, gain_one, hidden_grad, hidden
     )
-    cut = lambda rows, cols: pl.BlockSpec((1, rows, cols), lambda e, h: (e, h, 0))
-    widths = [cut(D // 2, FFE), cut(D // 2, FFE), cut(FFE // 2, D)]
     gate_total, up_total, down_total = call(
         widen_kernel,
         [sds((EXP_DEV, D, FFE), f32), sds((EXP_DEV, D, FFE), f32), sds((EXP_DEV, FFE, D), f32)],
+        scratch=[
+            pltpu.VMEM((6, D // 2, FFE), bf16), pltpu.VMEM((6, D // 2, FFE), f32),
+            pltpu.SemaphoreType.DMA((6, 3)), pltpu.SemaphoreType.DMA((6, 3)),
+        ],
         cost=cost(12),
-        grid=(EXP_DEV, 2),
-        in_specs=[
-            pl.BlockSpec((1, 2, D // 2, FFE), lambda e, h: (e, 0, h, 0)),
-            pl.BlockSpec((1, 1, 3, FFE // 2, FFE), lambda e, h: (e, 2, 0, h, 0)),
-        ],
-        out_specs=widths,
-    )(grad_sums.reshape(EXP_DEV, 3, D, FFE), grad_sums.reshape(EXP_DEV, 3, 3, FFE, FFE))
+        in_specs=[ANY],
+        out_specs=[ANY] * 3,
+    )(grad_sums.reshape(EXP_DEV, 3, D, FFE))
     return (
         layer_out, input_grad, gain_attn, query_total, key_total, value_total, out_total, gain_moe, router_total,
         gate_total, up_total, down_total,

time: 366 us -> 365 us (level)
  transfers between devices with their start and end apart: 44 -> 44, of which waited for: 20 -> 18; matrix products, arithmetic and copies ran while one was open for 4% -> 4% of each run, Pallas kernels for 36% -> 36%
where the time goes in v5:
time: 365 us; the launch traced here: 359 us
  Pallas kernels  145 us (40%)
  waiting for transfers between devices  96.8 us (27%)
  starting transfers between devices  69.9 us (19%)
  between operations  15.5 us (4%)
  blocking collectives  15.3 us (4%)
  local copies, waits for them, and re-layouts  13.9 us (4%)
    ppermute x35, starting transfers between devices, move(): return lax.ppermute(value, 'expert', pairs)  37.6 us
    ppermute x35, waiting for transfers between devices, move(): return lax.ppermute(value, 'expert', pairs)  32.1 us
    pallas_call x1, Pallas kernels, body(): call(expert_kernel, [sds((EXP_DEV, 3, D, FFE), bf16), sds((EXP_DEV, SLOTS...  25 us
    all_to_all x1, waiting for transfers between devices, body(): lax.all_to_all(pay.reshape(4, D // 4, 640), 'dp', 0, 0, tiled=True, axis_...  22.9 us
    pallas_call x1, Pallas kernels, body(): call(return_kernel, [sds((PAIRS, ROWS, XW), bf16)] * 2 + [sds((EXP_DEV, S...  18.5 us
    all_to_all x1, blocking collectives, body(): lax.all_to_all(send, 'expert', 0, 0, tiled=True).reshape(GROUP, BLK)  15.3 us
    pallas_call x1, Pallas kernels, body(): call(widen_kernel, [sds((EXP_DEV, D, FFE), f32), sds((EXP_DEV, D, FFE), f...  13.9 us
    pallas_call x1, Pallas kernels, body(): call(attend_back_kernel, sds((GROUP, WW), bf16), scratch=[pltpu.VMEM((GRO...  12.3 us
  transfers between devices with their start and end apart: 44, of which 18 were waited for; matrix products, arithmetic and copies ran while one was open for 4% of the time, Pallas kernels for 36%

profile of v5, /device:TPU:1, one launch (start us, length us, event | category | flops | bytes accessed | tf_op | source)
XLA Modules:
  0.0 359.1 jit_solution(9634863540529081020)
XLA Ops:
  16.3 6.9 %all-to-all-start = ((bf16[16,96,384]{2,1,0:T(8,128)(2,1)}), bf16[16,96,384]{2,1,0:T(8,128)(2,1)}, u32[]{:S(2)}, u32[]{:S(2)}) async-start(bf16[16,96,384]{2,1,0:T(8,128)(2,1)} %get-tuple-element.63), calls=%async_computation | async-start | bytes 2359296 | tf_op jit(solution)/shard_map/all_to_all | solution.py:583
  47.7 11.8 %shard_map.231 = (bf16[1024,1536]{1,0:T(8,128)(2,1)}, bf16[1024,384]{1,0:T(8,128)(2,1)}, bf16[8,128,256]{2,1,0:T(8,128)(2,1)}, f32[1024,8]{1,0:T(8,128)}) custom-call(s32[1]{0:T(128)} %bitcast.own_ref, bf16[128,1536]{1,0:T(8,128)(2,1)} %x_ref.3, bf16[128,1536]{1,0:T(8,128)(2,1)} %shard_map.229.refs_1_, bf16[128,1536]{1,0:T(8,128)(2,1)} %collective-permute-done.1.refs_2_, ...), custom_call_target="tpu_custom_call" | custom-call | flops 13799999488 | bytes 1024 | tf_op jit(solution)/shard_map/pallas_call | solution.py:606
  60.0 5.1 %all-to-all-start.1 = ((bf16[8,128,256]{2,1,0:T(8,128)(2,1)}), bf16[8,128,256]{2,1,0:T(8,128)(2,1)}, u32[]{:S(2)}, u32[]{:S(2)}) async-start(bf16[8,128,256]{2,1,0:T(8,128)(2,1)} %shard_map.232), calls=%async_computation.1 | async-start | bytes 1048576 | tf_op jit(solution)/shard_map/all_to_all | solution.py:613
  66.1 8.6 %all-to-all-done.1.mix_ref = bf16[8,128,256]{2,1,0:T(8,128)(2,1)} async-done(((bf16[8,128,256]{2,1,0:T(8,128)(2,1)}), bf16[8,128,256]{2,1,0:T(8,128)(2,1)}, u32[]{:S(2)}, u32[]{:S(2)}) %all-to-all-start.1) | async-done | bytes 524320 | tf_op jit(solution)/shard_map/all_to_all | solution.py:613
  76.5 4.5 %shard_map.233 = (f32[128,1536]{1,0:T(8,128)}, bf16[128,1536]{1,0:T(8,128)(2,1)}, bf16[128,1536]{1,0:T(8,128)(2,1)}) custom-call(bf16[8,128,256]{2,1,0:T(8,128)(2,1)} %all-to-all-done.1.mix_ref, bf16[1536,1536]{1,0:T(8,128)(2,1)} %all-gather.3.cloned.1.call-done.wo_ref, bf16[128,1536]{1,0:T(8,128)(2,1)} %x_ref.3, f32[1,1536]{1,0:T(1,128)} %reshape.126.refs_4_.gain_ref), custom_call_target="tpu_custom_call" | custom-call | flops 4600000000 | bytes 1024 | tf_op jit(solution)/shard_map/pallas_call | solution.py:615
  83.8 6.0 %shard_map.234 = (s32[3,8,1024]{2,1,0:T(8,128)}, bf16[3,448,1536]{2,1,0:T(8,128)(2,1)}) custom-call(s32[1]{0:T(128)} %bitcast.own_ref, bf16[128,1664]{1,0:T(8,128)(2,1)} %get-tuple-element.65.refs_0_, bf16[128,1664]{1,0:T(8,128)(2,1)} %collective-permute-done.10.refs_1_, bf16[128,1664]{1,0:T(8,128)(2,1)} %collective-permute-done.9.refs_0_.refs_2_, ...), custom_call_target="tpu_custom_call" | custom-call | flops 6899999744 | bytes 1024 | tf_op jit(solution)/shard_map/pallas_call | solution.py:620
  108.1 25.0 %shard_map.236 = (bf16[3,3,1536,512]{3,2,1,0:T(8,128)(2,1)}, bf16[3,448,512]{2,1,0:T(8,128)(2,1)}, bf16[3,448,512]{2,1,0:T(8,128)(2,1)}, bf16[3,448,512]{2,1,0:T(8,128)(2,1)}, f32[3,448,1]{2,1,0:T(8,128)}) custom-call(s32[1]{0:T(128)} %bitcast.own_ref, bf16[128,1536]{1,0:T(8,128)(2,1)} %get-tuple-element.66.refs_0_.normed_ref.n_ref, ...), custom_call_target="tpu_custom_call" | custom-call | flops 32199999488 | bytes 1024 | tf_op jit(solution)/shard_map/pallas_call | solution.py:634
  133.3 18.5 %shard_map.237 = (bf16[4,128,1664]{2,1,0:T(8,128)(2,1)}, bf16[4,128,1664]{2,1,0:T(8,128)(2,1)}, bf16[3,448,1536]{2,1,0:T(8,128)(2,1)}) custom-call(s32[1]{0:T(128)} %bitcast.own_ref, bf16[3,448,512]{2,1,0:T(8,128)(2,1)} %get-tuple-element.69.hg_ref, bf16[3,448,512]{2,1,0:T(8,128)(2,1)} %get-tuple-element.70.hu_ref, ...), custom_call_target="tpu_custom_call" | custom-call | flops 1150000000 | bytes 1024 | tf_op jit(solution)/shard_map/pallas_call | solution.py:657
  162.2 5.8 %collective-permute-done.26.up_ref = bf16[64,1664]{1,0:T(8,128)(2,1)} collective-permute-done((bf16[64,1664]{1,0:T(8,128)(2,1)}, bf16[64,1664]{1,0:T(8,128)(2,1)}, u32[]{:S(2)}, u32[]{:S(2)}) %collective-permute-start.26) | collective-permute-done | bytes 213024 | tf_op jit(solution)/shard_map/ppermute | solution.py:529
  173.3 9.4 %collective-permute-done.28.part_b = bf16[128,1664]{1,0:T(8,128)(2,1)} collective-permute-done((bf16[128,1664]{1,0:T(8,128)(2,1)}, bf16[128,1664]{1,0:T(8,128)(2,1)}, u32[]{:S(2)}, u32[]{:S(2)}) %collective-permute-start.28) | collective-permute-done | bytes 426016 | tf_op jit(solution)/shard_map/ppermute | solution.py:529
  182.7 7.4 %shard_map.240 = (f32[128,1536]{1,0:T(8,128)}, f32[1,1536]{1,0:T(1,128)}, bf16[8,128,256]{2,1,0:T(8,128)(2,1)}, bf16[8,128,256]{2,1,0:T(8,128)(2,1)}, bf16[2,128,128]{2,1,0:T(8,128)(2,1)}) custom-call(bf16[128,1664]{1,0:T(8,128)(2,1)} %get-tuple-element.78.part_a, bf16[128,1664]{1,0:T(8,128)(2,1)} %collective-permute-done.28.part_b, ...), custom_call_target="tpu_custom_call" | custom-call | flops 1150000000 | bytes 1024 | tf_op jit(solution)/shard_map/pallas_call | solution.py:671
  190.1 15.3 %all_to_all.35 = bf16[8,128,256]{2,1,0:T(8,128)(2,1)} all-to-all(bf16[8,128,256]{2,1,0:T(8,128)(2,1)} %get-tuple-element.86), channel_id=1, replica_groups=mesh['dp'=16,'expert'=8] {'expert'}, dimensions={0} | all-to-all | bytes 1048576 | tf_op jit(solution)/shard_map/all_to_all | solution.py:677
  205.5 5.1 %all-to-all-start.3 = ((bf16[8,128,256]{2,1,0:T(8,128)(2,1)}), bf16[8,128,256]{2,1,0:T(8,128)(2,1)}, u32[]{:S(2)}, u32[]{:S(2)}) async-start(bf16[8,128,256]{2,1,0:T(8,128)(2,1)} %get-tuple-element.89), calls=%async_computation.3 | async-start | bytes 1048576 | tf_op jit(solution)/shard_map/all_to_all | solution.py:678
  210.5 12.3 %shard_map.241.dqkv_ref = bf16[1024,384]{1,0:T(8,128)(2,1)} custom-call(bf16[1024,384]{1,0:T(8,128)(2,1)} %get-tuple-element.74.qkv_ref, f32[1024,8]{1,0:T(8,128)} %get-tuple-element.75.log_ref, bf16[1024,256]{1,0:T(8,128)(2,1)} %bitcast.16, f32[1024,128]{1,0:T(8,128)} %copy.32.refs_0_.refs_12_.cos_ref, f32[1024,128]{1,0:T(8,128)} %copy.33.refs_1_.refs_13_.sin_ref, ...), custom_call_target="tpu_custom_call" | custom-call | flops 13799999488 | bytes 1024 | tf_op jit(solution)/shard_map/pallas_call | solution.py:679
  222.8 8.6 %shard_map.243.after_ref = bf16[1536,640]{1,0:T(8,128)(2,1)} custom-call(bf16[1024,1536]{1,0:T(8,128)(2,1)} %get-tuple-element.87.normed_ref, bf16[1024,384]{1,0:T(8,128)(2,1)} %shard_map.241.dqkv_ref, bf16[1024,1536]{1,0:T(8,128)(2,1)} %all-gather.5.cloned.1.call-done.mix_ref.refs_0_, bf16[1024,256]{1,0:T(8,128)(2,1)} %bitcast.9.got_ref, ...), custom_call_target="tpu_custom_call" | custom-call | flops 1150000000 | bytes 1024 | tf_op jit(solution)/shard_map/pallas_call | solution.py:685
  231.4 9.0 %shard_map.244 = (bf16[4,128,3072]{2,1,0:T(8,128)(2,1)}, bf16[4,128,3072]{2,1,0:T(8,128)(2,1)}) custom-call(s32[1]{0:T(128)} %bitcast.own_ref, bf16[3,448,1536]{2,1,0:T(8,128)(2,1)} %get-tuple-element.73.gated_ref, s32[3,8,1024]{2,1,0:T(8,128)} %get-tuple-element.67.refs_0_.refs_12_.slot_ref, bf16[1024,384]{1,0:T(8,128)(2,1)} %shard_map.241.dqkv_ref, ...), custom_call_target="tpu_custom_call" | custom-call | flops 115000000 | bytes 1024 | tf_op jit(solution)/shard_map/pallas_call | solution.py:689
  240.6 4.5 %all-to-all-start.4 = ((bf16[4,384,640]{2,1,0:T(8,128)(2,1)}), bf16[4,384,640]{2,1,0:T(8,128)(2,1)}, u32[]{:S(2)}, u32[]{:S(2)}) async-start(bf16[4,384,640]{2,1,0:T(8,128)(2,1)} %bitcast.12), calls=%async_computation.4 | async-start | bytes 3932160 | tf_op jit(solution)/shard_map/all_to_all | solution.py:688
  246.4 4.8 %shard_map.245 = (bf16[128,3072]{1,0:T(8,128)(2,1)}, bf16[128,3072]{1,0:T(8,128)(2,1)}, bf16[128,3072]{1,0:T(8,128)(2,1)}, bf16[64,3072]{1,0:T(8,128)(2,1)}, bf16[64,3072]{1,0:T(8,128)(2,1)}) custom-call(bf16[4,128,3072]{2,1,0:T(8,128)(2,1)} %get-tuple-element.92.keep_ref, bf16[4,128,3072]{2,1,0:T(8,128)(2,1)} %collective-permute-done.30.got_ref), custom_call_target="tpu_custom_call" | custom-call | flops 115000000 | bytes 1024 | tf_op jit(solution)/shard_map/pallas_call | solution.py:560
  253.9 22.9 %all-to-all-done.4.part_ref = bf16[4,384,640]{2,1,0:T(8,128)(2,1)} async-done(((bf16[4,384,640]{2,1,0:T(8,128)(2,1)}), bf16[4,384,640]{2,1,0:T(8,128)(2,1)}, u32[]{:S(2)}, u32[]{:S(2)}) %all-to-all-start.4) | async-done | bytes 1966112 | tf_op jit(solution)/shard_map/all_to_all | solution.py:688
  289.1 8.7 %all-to-all-done.5.part_ref = bf16[4,96,640]{2,1,0:T(8,128)(2,1)} async-done(((bf16[4,96,640]{2,1,0:T(8,128)(2,1)}), bf16[4,96,640]{2,1,0:T(8,128)(2,1)}, u32[]{:S(2)}, u32[]{:S(2)}) %all-to-all-start.5) | async-done | bytes 491552 | tf_op jit(solution)/shard_map/all_to_all | solution.py:696
  299.9 6.5 %all-to-all-start.6 = ((bf16[8,96,640]{2,1,0:T(8,128)(2,1)}), bf16[8,96,640]{2,1,0:T(8,128)(2,1)}, u32[]{:S(2)}, u32[]{:S(2)}) async-start(bf16[8,96,640]{2,1,0:T(8,128)(2,1)} %shard_map.249), calls=%async_computation.6 | async-start | bytes 1966080 | tf_op jit(solution)/shard_map/all_to_all | solution.py:702
  310.7 10.2 %all-to-all-done.6.part_ref = bf16[8,96,640]{2,1,0:T(8,128)(2,1)} async-done(((bf16[8,96,640]{2,1,0:T(8,128)(2,1)}), bf16[8,96,640]{2,1,0:T(8,128)(2,1)}, u32[]{:S(2)}, u32[]{:S(2)}) %all-to-all-start.6) | async-done | bytes 983072 | tf_op jit(solution)/shard_map/all_to_all | solution.py:702
  327.0 11.4 %all-reduce.2.cloned.1.call-done.part_ref = bf16[3,3,1536,512]{3,2,1,0:T(8,128)(2,1)} async-done(((bf16[3,3,1536,512]{3,2,1,0:T(8,128)(2,1)}), bf16[3,3,1536,512]{3,2,1,0:T(8,128)(2,1)}) %all-reduce.2.cloned.1.call-update) | async-done | bytes 14155792 | tf_op jit(solution)/shard_map/psum | solution.py:655
  338.4 13.9 %shard_map.252 = (f32[3,1536,512]{2,1,0:T(8,128)}, f32[3,1536,512]{2,1,0:T(8,128)}, f32[3,512,1536]{2,1,0:T(8,128)}) custom-call(bf16[3,3,1536,512]{3,2,1,0:T(8,128)(2,1)} %all-reduce.2.cloned.1.call-done.part_ref), custom_call_target="tpu_custom_call" | custom-call | flops 13799999488 | bytes 1024 | tf_op jit(solution)/shard_map/pallas_call | solution.py:713
  (126 shorter events, 101.3 us)
Async XLA Ops:
  7.2 69.4 %all-gather.3.cloned.1.call-start = ((), (), s32[]{:S(2)}) async-start(), calls=%async_computation.7 | async-start | bytes 5013504 | tf_op jit(solution)/shard_map/all_gather | solution.py:584
  7.9 24.1 %collective-permute-start = (bf16[128,1536]{1,0:T(8,128)(2,1)}, bf16[128,1536]{1,0:T(8,128)(2,1)}, u32[]{:S(2)}, u32[]{:S(2)}) collective-permute-start(bf16[128,1536]{1,0:T(8,128)(2,1)} %x_ref.3), channel_id=1, source_target_pairs={{0,2},{1,3},{2,4},{3,5},{4,6},{5,7},{6,0},{7,1},{8,10},{9,11},{10,... | collective-permute-start | bytes 1179656 | tf_op jit(solution)/shard_map/ppermute | solution.py:529
  10.4 25.2 %collective-permute-start.1 = (bf16[128,1536]{1,0:T(8,128)(2,1)}, bf16[128,1536]{1,0:T(8,128)(2,1)}, u32[]{:S(2)}, u32[]{:S(2)}) collective-permute-start(bf16[128,1536]{1,0:T(8,128)(2,1)} %x_ref.3), channel_id=1, source_target_pairs={{0,6},{1,7},{2,0},{3,1},{4,2},{5,3},{6,4},{7,5},{8,14},{9,15},{10,... | collective-permute-start | bytes 1179656 | tf_op jit(solution)/shard_map/ppermute | solution.py:529
  12.7 24.0 %collective-permute-start.4 = (bf16[128,1536]{1,0:T(8,128)(2,1)}, bf16[128,1536]{1,0:T(8,128)(2,1)}, u32[]{:S(2)}, u32[]{:S(2)}) collective-permute-start(bf16[128,1536]{1,0:T(8,128)(2,1)} %x_ref.3), channel_id=1, source_target_pairs={{0,1},{1,0},{2,3},{3,2},{4,5},{5,4},{6,7},{7,6},{8,9},{9,8},{10,11... | collective-permute-start | bytes 1179656 | tf_op jit(solution)/shard_map/ppermute | solution.py:529
  16.3 31.4 %all-to-all-start = ((bf16[16,96,384]{2,1,0:T(8,128)(2,1)}), bf16[16,96,384]{2,1,0:T(8,128)(2,1)}, u32[]{:S(2)}, u32[]{:S(2)}) async-start(bf16[16,96,384]{2,1,0:T(8,128)(2,1)} %get-tuple-element.63), calls=%async_computation | async-start | bytes 2359296 | tf_op jit(solution)/shard_map/all_to_all | solution.py:583
  23.3 21.5 %collective-permute-start.10 = (bf16[128,1664]{1,0:T(8,128)(2,1)}, bf16[128,1664]{1,0:T(8,128)(2,1)}, u32[]{:S(2)}, u32[]{:S(2)}) collective-permute-start(bf16[128,1664]{1,0:T(8,128)(2,1)} %get-tuple-element.65.refs_0_), channel_id=1, source_target_pairs={{0,2},{1,3},{2,4},{3,5},{4,6},{5,7},{6,0},{7,1},{8,10},{9,11},{10,... | collective-permute-start | bytes 1277960 | tf_op jit(solution)/shard_map/ppermute | solution.py:529
  44.7 14.8 %collective-permute-start.9 = (bf16[128,1664]{1,0:T(8,128)(2,1)}, bf16[128,1664]{1,0:T(8,128)(2,1)}, u32[]{:S(2)}, u32[]{:S(2)}) collective-permute-start(bf16[128,1664]{1,0:T(8,128)(2,1)} %get-tuple-element.65.refs_0_), channel_id=1, source_target_pairs={{0,6},{1,7},{2,0},{3,1},{4,2},{5,3},{6,4},{7,5},{8,14},{9,15},{10,... | collective-permute-start | bytes 1277960 | tf_op jit(solution)/shard_map/ppermute | solution.py:529
  47.2 12.8 %collective-permute-start.11 = (bf16[128,1664]{1,0:T(8,128)(2,1)}, bf16[128,1664]{1,0:T(8,128)(2,1)}, u32[]{:S(2)}, u32[]{:S(2)}) collective-permute-start(bf16[128,1664]{1,0:T(8,128)(2,1)} %collective-permute-done.10.refs_1_), channel_id=1, source_target_pairs={{0,2},{1,3},{2,4},{3,5},{4,6},{5,7},{6,0},{7,1},{8,10},{9,11},{10,... | collective-permute-start | bytes 1277960 | tf_op jit(solution)/shard_map/ppermute | solution.py:529
  60.0 14.7 %all-to-all-start.1 = ((bf16[8,128,256]{2,1,0:T(8,128)(2,1)}), bf16[8,128,256]{2,1,0:T(8,128)(2,1)}, u32[]{:S(2)}, u32[]{:S(2)}) async-start(bf16[8,128,256]{2,1,0:T(8,128)(2,1)} %shard_map.232), calls=%async_computation.1 | async-start | bytes 1048576 | tf_op jit(solution)/shard_map/all_to_all | solution.py:613
  65.1 68.1 %all-gather.5.cloned.1.call-start = ((), (), s32[]{:S(2)}) async-start(), calls=%async_computation.8 | async-start | bytes 3538944 | tf_op jit(solution)/shard_map/all_gather | solution.py:629
  65.1 17.2 %collective-permute-start.13 = (bf16[128,1664]{1,0:T(8,128)(2,1)}, bf16[128,1664]{1,0:T(8,128)(2,1)}, u32[]{:S(2)}, u32[]{:S(2)}) collective-permute-start(bf16[128,1664]{1,0:T(8,128)(2,1)} %get-tuple-element.65.refs_0_), channel_id=1, source_target_pairs={{0,1},{1,0},{2,3},{3,2},{4,5},{5,4},{6,7},{7,6},{8,9},{9,8},{10,11... | collective-permute-start | bytes 1277960 | tf_op jit(solution)/shard_map/ppermute | solution.py:529
  65.4 18.5 %collective-permute-start.14 = (bf16[128,1664]{1,0:T(8,128)(2,1)}, bf16[128,1664]{1,0:T(8,128)(2,1)}, u32[]{:S(2)}, u32[]{:S(2)}) collective-permute-start(bf16[128,1664]{1,0:T(8,128)(2,1)} %collective-permute-done.10.refs_1_), channel_id=1, source_target_pairs={{0,1},{1,0},{2,3},{3,2},{4,5},{5,4},{6,7},{7,6},{8,9},{9,8},{10,11... | collective-permute-start | bytes 1277960 | tf_op jit(solution)/shard_map/ppermute | solution.py:529
  65.6 18.2 %collective-permute-start.15 = (bf16[128,1664]{1,0:T(8,128)(2,1)}, bf16[128,1664]{1,0:T(8,128)(2,1)}, u32[]{:S(2)}, u32[]{:S(2)}) collective-permute-start(bf16[128,1664]{1,0:T(8,128)(2,1)} %collective-permute-done.9.refs_0_.refs_2_), channel_id=1, source_target_pairs={{0,1},{1,0},{2,3},{3,2},{4,5},{5,4},{6,7},{7,6},{8,9},{9,8},{10,11... | collective-permute-start | bytes 1277960 | tf_op jit(solution)/shard_map/ppermute | solution.py:529
  65.9 18.0 %collective-permute-start.16 = (bf16[128,1664]{1,0:T(8,128)(2,1)}, bf16[128,1664]{1,0:T(8,128)(2,1)}, u32[]{:S(2)}, u32[]{:S(2)}) collective-permute-start(bf16[128,1664]{1,0:T(8,128)(2,1)} %collective-permute-done.11.refs_1_.refs_3_), channel_id=1, source_target_pairs={{0,1},{1,0},{2,3},{3,2},{4,5},{5,4},{6,7},{7,6},{8,9},{9,8},{10,11... | collective-permute-start | bytes 1277960 | tf_op jit(solution)/shard_map/ppermute | solution.py:529
  92.6 245.8 %all-reduce.2.cloned.1.call-start = ((), (), s32[]{:S(2)}) async-start(), calls=%async_computation.9 | async-start | bytes 28311552 | tf_op jit(solution)/shard_map/psum | solution.py:655
  92.7 13.7 %collective-permute-start.20 = (bf16[128,1536]{1,0:T(8,128)(2,1)}, bf16[128,1536]{1,0:T(8,128)(2,1)}, u32[]{:S(2)}, u32[]{:S(2)}) collective-permute-start(bf16[128,1536]{1,0:T(8,128)(2,1)} %get-tuple-element.66.refs_0_.normed_ref.n_ref), channel_id=1, source_target_pairs={{0,1},{1,0},{2,3},{3,2},{4,5},{5,4},{6,7},{7,6},{8,9},{9,8},{10,11... | collective-permute-start | bytes 1179656 | tf_op jit(solution)/shard_map/ppermute | solution.py:529
  205.5 17.3 %all-to-all-start.3 = ((bf16[8,128,256]{2,1,0:T(8,128)(2,1)}), bf16[8,128,256]{2,1,0:T(8,128)(2,1)}, u32[]{:S(2)}, u32[]{:S(2)}) async-start(bf16[8,128,256]{2,1,0:T(8,128)(2,1)} %get-tuple-element.89), calls=%async_computation.3 | async-start | bytes 1048576 | tf_op jit(solution)/shard_map/all_to_all | solution.py:678
  240.6 36.1 %all-to-all-start.4 = ((bf16[4,384,640]{2,1,0:T(8,128)(2,1)}), bf16[4,384,640]{2,1,0:T(8,128)(2,1)}, u32[]{:S(2)}, u32[]{:S(2)}) async-start(bf16[4,384,640]{2,1,0:T(8,128)(2,1)} %bitcast.12), calls=%async_computation.4 | async-start | bytes 3932160 | tf_op jit(solution)/shard_map/all_to_all | solution.py:688
  251.2 32.3 %collective-permute-start.31 = (bf16[64,3072]{1,0:T(8,128)(2,1)}, bf16[64,3072]{1,0:T(8,128)(2,1)}, u32[]{:S(2)}, u32[]{:S(2)}) collective-permute-start(bf16[64,3072]{1,0:T(8,128)(2,1)} %get-tuple-element.97.after_ref), channel_id=1, source_target_pairs={{0,2},{1,3},{2,4},{3,5},{4,6},{5,7},{6,0},{7,1},{8,10},{9,11},{10,... | collective-permute-start | bytes 1179656 | tf_op jit(solution)/shard_map/ppermute | solution.py:529
  252.6 30.9 %collective-permute-start.32 = (bf16[64,3072]{1,0:T(8,128)(2,1)}, bf16[64,3072]{1,0:T(8,128)(2,1)}, u32[]{:S(2)}, u32[]{:S(2)}) collective-permute-start(bf16[64,3072]{1,0:T(8,128)(2,1)} %get-tuple-element.98), channel_id=1, source_target_pairs={{0,6},{1,7},{2,0},{3,1},{4,2},{5,3},{6,4},{7,5},{8,14},{9,15},{10,... | collective-permute-start | bytes 1179656 | tf_op jit(solution)/shard_map/ppermute | solution.py:529
  279.3 18.6 %all-to-all-start.5 = ((bf16[4,96,640]{2,1,0:T(8,128)(2,1)}), bf16[4,96,640]{2,1,0:T(8,128)(2,1)}, u32[]{:S(2)}, u32[]{:S(2)}) async-start(bf16[4,96,640]{2,1,0:T(8,128)(2,1)} %bitcast.13), calls=%async_computation.5 | async-start | bytes 983040 | tf_op jit(solution)/shard_map/all_to_all | solution.py:696
  286.4 20.0 %collective-permute-start.33 = (bf16[128,3072]{1,0:T(8,128)(2,1)}, bf16[128,3072]{1,0:T(8,128)(2,1)}, u32[]{:S(2)}, u32[]{:S(2)}) collective-permute-start(bf16[128,3072]{1,0:T(8,128)(2,1)} %get-tuple-element.99), channel_id=1, source_target_pairs={{0,2},{1,3},{2,4},{3,5},{4,6},{5,7},{6,0},{7,1},{8,10},{9,11},{10,... | collective-permute-start | bytes 2359304 | tf_op jit(solution)/shard_map/ppermute | solution.py:529
  287.7 18.7 %collective-permute-start.34 = (bf16[128,3072]{1,0:T(8,128)(2,1)}, bf16[128,3072]{1,0:T(8,128)(2,1)}, u32[]{:S(2)}, u32[]{:S(2)}) collective-permute-start(bf16[128,3072]{1,0:T(8,128)(2,1)} %get-tuple-element.100), channel_id=1, source_target_pairs={{0,6},{1,7},{2,0},{3,1},{4,2},{5,3},{6,4},{7,5},{8,14},{9,15},{10,... | collective-permute-start | bytes 2359304 | tf_op jit(solution)/shard_map/ppermute | solution.py:529
  299.9 21.0 %all-to-all-start.6 = ((bf16[8,96,640]{2,1,0:T(8,128)(2,1)}), bf16[8,96,640]{2,1,0:T(8,128)(2,1)}, u32[]{:S(2)}, u32[]{:S(2)}) async-start(bf16[8,96,640]{2,1,0:T(8,128)(2,1)} %shard_map.249), calls=%async_computation.6 | async-start | bytes 1966080 | tf_op jit(solution)/shard_map/all_to_all | solution.py:702
  (27 other events, 193.2 us)
Sparse Core Ops, SparseCore 0:
  10.2 66.2 all-gather.2
  92.7 28.8 all-gather.4
  133.4 204.9 all-reduce.1
